TPU v7x, 128 devices: a whole 4x4x4 slice. The times are simulated.
128 devices in a mesh: grp: 4 (over x_lo, core), brick: 32 (over x_hi, y, z).
Axes of the slice: x: 4 (x_hi: 2, x_lo: 2; x = x_hi * 2 + x_lo), y: 4, z: 4, core: 2. Of those that a mesh axis runs over, the one named last changes fastest.
Arguments:
- positions: float32 [3, 1048576], P(None, ('grp', 'brick')), may hold values from -6 to 6
- features: float32 [128, 1048576], P(None, ('grp', 'brick')), may hold values from -6 to 6
- teacher_nbr: int32 [1048576, 12], P(('grp', 'brick')), may hold values from 0 to 10239, as said below
- nbr_count: int32 [1048576], P(('grp', 'brick')), may hold values from 3 to 12
- w_rad: float32 [8, 128], replicated, may hold values from -2 to 2
- w_mix: float32 [128, 128], replicated, may hold values from -0.5 to 0.5
- w_out: float32 [128], replicated, may hold values from -0.5 to 0.5
- block_owner: int32 [32768], P(('grp', 'brick')), may hold values from 0 to 127, as said below
- block_start: int32 [32768], P(('grp', 'brick')), may hold values from 0 to 480
- atom_bead: int32 [1048576], P(('grp', 'brick')), may hold values from -1 to 31
- bead_pos: float32 [3, 65536], P(None, ('grp', 'brick')), may hold values from -6 to 6
- bead_nbr: int32 [65536, 16], P(('grp', 'brick')), may hold values from 0 to 575, as said below
- bead_weight: float32 [65536], P(('grp', 'brick')), may hold values from 0.5 to 18
- w_first: float32 [8, 128], replicated, may hold values from -2 to 2
- w_second: float32 [128], replicated, may hold values from -0.5 to 0.5
Outputs:
- atom_force: float32 [3, 1048576], P(None, ('grp', 'brick'))
- bead_force: float32 [3, 65536], P(None, ('grp', 'brick'))
- student_force: float32 [3, 65536], P(None, ('grp', 'brick'))
- grad_first: float32 [8, 128], replicated
- grad_second: float32 [128], replicated
- loss: float32 [], replicated
Inputs may be any that keep to these rules, and one draw needn't show every extreme that they name: `teacher_nbr`: each slot of an atom names an atom within 1024 places of it along the chain of bricks, never itself and never past the chain's ends: a column of 1024 left ghosts, the brick's 8192 atoms and 1024 right ghosts. `block_owner`: every owner is named by exactly 2 of each brick's blocks. `bead_nbr`: each edge of a bead names a bead within 32 places of it in sequence order, never itself and never past the chain's ends: a column of 32 left ghosts, the owner's 512 beads and 32 right ghosts.
All inputs are finite; a program needn't handle non-finite values.
Results may differ from a plain program's by a relative error of at most 0.0003.
Values sent between devices are 32-bit elements; how exact they have to be, the bound alone decides.
A program may use at most 320 MiB of HBM per device.

v0:
```python
import math

import jax
import jax.numpy as jnp
from jax import lax
from jax.sharding import PartitionSpec as P

G = 1024
BPB = 32
BW = 32


HIGHEST_PRECISION = lax.Precision.HIGHEST


def with_halo(cells, sides, width):
    for axis, dim in sides:
        count = lax.axis_size(axis)
        ends = count - 1
        head = lax.slice_in_dim(cells, 0, width, axis=dim)
        tail = lax.slice_in_dim(cells, cells.shape[dim] - width, cells.shape[dim], axis=dim)
        cells = jnp.concatenate(
            [
                lax.ppermute(tail, axis, [(i, (i + 1) % count) for i in range(ends)]),
                cells,
                lax.ppermute(head, axis, [((i + 1) % count, i) for i in range(ends)]),
            ],
            axis=dim,
        )
    return cells


def shifted(array, axis, by):
    peers = lax.axis_size(axis)
    pairs = [(i, i + by) for i in range(peers) if 0 <= i + by < peers]
    return lax.ppermute(array, axis, pairs)


def decay_rates(rate_count):
    return 0.05 * 1.6 ** jnp.arange(rate_count, dtype=jnp.float32)


def block_energy(own_pos, near_pos, own_feat, near_feat, slot_mask, w_rad, w_mix, w_out):
    offsets = near_pos - own_pos[:, None, :]
    dist_sq = jnp.sum(offsets * offsets, axis=0)
    radial_basis = (
        jnp.exp(-decay_rates(w_rad.shape[0])[:, None, None] * dist_sq[None]) * slot_mask[None]
    )
    radial = jnp.einsum("bkn,bc->ckn", radial_basis, w_rad, precision=HIGHEST_PRECISION)
    message = jnp.sum(radial * near_feat, axis=1) / math.sqrt(near_feat.shape[1])
    mixed_feat = jnp.einsum("cn,cd->dn", message, w_mix, precision=HIGHEST_PRECISION) + own_feat
    return jnp.sum(w_out[:, None] * jax.nn.silu(mixed_feat))


def block_grads(own_pos, near_pos, own_feat, near_feat, slot_mask, w_rad, w_mix, w_out):

    def energy(first_arg, second_arg):
        return block_energy(
            first_arg, second_arg, own_feat, near_feat, slot_mask, w_rad, w_mix, w_out
        )

    energy_value, pullback = jax.vjp(energy, own_pos, near_pos)
    return pullback(jnp.ones_like(energy_value))


def student_eval(own_pos, near_pos, w_first, w_second):
    offsets = near_pos - own_pos[:, None, :]
    dist_sq = jnp.sum(offsets * offsets, axis=0)
    radial_basis = jnp.exp(-decay_rates(w_first.shape[0])[:, None, None] * dist_sq[None])
    hidden = jax.nn.silu(
        jnp.einsum("bkn,bh->hkn", radial_basis, w_first, precision=HIGHEST_PRECISION)
    )
    strength = jnp.einsum("hkn,h->kn", hidden, w_second, precision=HIGHEST_PRECISION)
    return jnp.sum(strength[None] * offsets, axis=1)


def local(
    positions,
    features,
    teacher_nbr,
    nbr_count,
    w_rad,
    w_mix,
    w_out,
    block_owner,
    block_start,
    atom_bead,
    bead_pos,
    bead_nbr,
    bead_weight,
    w_first,
    w_second,
):
    atom_total = positions.shape[1]
    ghost_width = G
    devices = lax.axis_size(("grp", "brick"))
    slot_mask = (
        jnp.arange(teacher_nbr.shape[1], dtype=jnp.int32)[None, :] < nbr_count[:, None]
    ).astype(jnp.float32)
    block_starts = list(range(0, atom_total, ghost_width))
    ghost_grad = jnp.zeros((3, atom_total + 2 * ghost_width), jnp.float32)
    boundary = tuple(block_starts)
    stacked = jnp.concatenate([positions, features], axis=0)
    extended = with_halo(stacked, ((("grp", "brick"), 1),), ghost_width)
    ext_pos = extended[:3]
    ext_feat = extended[3:]
    for first_atom in boundary:
        neighbours = (teacher_nbr[first_atom : first_atom + ghost_width] - 0).T
        own_pos = positions[:, first_atom : first_atom + ghost_width]
        own_feat = features[:, first_atom : first_atom + ghost_width]
        near_pos = ext_pos[:, neighbours]
        near_feat = ext_feat[:, neighbours]
        block_mask = slot_mask[first_atom : first_atom + ghost_width].T
        grad_own, grad_near = block_grads(
            own_pos, near_pos, own_feat, near_feat, block_mask, w_rad, w_mix, w_out
        )
        neighbours, grad_own, grad_near = (neighbours, grad_own, grad_near)
        ghost_grad = ghost_grad.at[:, ghost_width + first_atom : 2 * ghost_width + first_atom].add(
            grad_own
        )
        ghost_grad = ghost_grad.at[:, neighbours].add(grad_near)
    from_above = shifted(ghost_grad[:, :ghost_width], ("grp", "brick"), -1)
    from_below = shifted(ghost_grad[:, atom_total + ghost_width :], ("grp", "brick"), 1)
    total_grad = ghost_grad[:, ghost_width : ghost_width + atom_total]
    total_grad = total_grad.at[:, :ghost_width].add(from_below)
    total_grad = total_grad.at[:, atom_total - ghost_width :].add(from_above)
    atom_force = -total_grad
    bead_dev = bead_pos.shape[1]
    block_count = block_owner.shape[0]
    block_size = atom_total // block_count
    capacity = block_count // devices
    bead_span = jnp.arange(BPB, dtype=jnp.int32)
    block_force = atom_force.reshape(3, block_count, block_size)
    bead_hot = (
        atom_bead.reshape(block_count, block_size)[:, :, None] == bead_span[None, None, :]
    ).astype(jnp.float32)
    partial_value = jnp.einsum("cna,naq->ncq", block_force, bead_hot, precision=HIGHEST_PRECISION)
    block_rows = jnp.arange(block_count, dtype=jnp.int32)
    same_owner = block_owner[:, None] == block_owner[None, :]
    earlier = block_rows[None, :] < block_rows[:, None]
    slot_rank = jnp.sum(same_owner & earlier, axis=1)
    outgoing = jnp.zeros((devices, 3, capacity, BPB), jnp.float32)
    outgoing = outgoing.at[
        block_owner[:, None, None],
        jnp.arange(3, dtype=jnp.int32)[None, :, None],
        slot_rank[:, None, None],
        bead_span[None, None, :],
    ].set(partial_value)
    starts_out = (
        jnp.zeros((devices, capacity), jnp.float32)
        .at[block_owner, slot_rank]
        .set(block_start.astype(jnp.float32))
    )
    received, starts_in = (
        lax.all_to_all(
            outgoing.reshape(devices, 3, capacity * BPB),
            ("grp", "brick"),
            split_axis=0,
            concat_axis=0,
            tiled=True,
        ),
        lax.all_to_all(starts_out, ("grp", "brick"), split_axis=0, concat_axis=0, tiled=True),
    )
    columns_in = starts_in.astype(jnp.int32)[:, :, None] + bead_span[None, None, :]
    bead_force = jnp.zeros((3, bead_dev), jnp.float32)
    bead_force = bead_force.at[
        jnp.arange(3, dtype=jnp.int32)[None, :, None, None], columns_in[:, None, :, :]
    ].add(received.reshape(devices, 3, capacity, BPB))
    bead_ext = with_halo(bead_pos, ((("grp", "brick"), 1),), BW)
    near_beads = bead_ext[:, bead_nbr.T]
    bead_total = bead_dev * devices

    def local_loss(first_w, second_w):
        predicted = student_eval(bead_pos, near_beads, first_w, second_w)
        residual = predicted - bead_force
        return (
            jnp.sum(bead_weight * jnp.sum(residual * residual, axis=0)) / (3.0 * bead_total),
            predicted,
        )

    loss_part, pullback, predicted = jax.vjp(local_loss, w_first, w_second, has_aux=True)
    grad_one, grad_two = pullback(jnp.ones_like(loss_part))
    grad_one, grad_two, loss_sum = lax.psum((grad_one, grad_two, loss_part), ("grp", "brick"))
    return (atom_force, bead_force, predicted, grad_one, grad_two, loss_sum)


def solution(mesh):
    placed = (
        P(None, ("grp", "brick")),
        P(None, ("grp", "brick")),
        P(("grp", "brick"), None),
        P(("grp", "brick")),
        P(),
        P(),
        P(),
        P(("grp", "brick")),
        P(("grp", "brick")),
        P(("grp", "brick")),
        P(None, ("grp", "brick")),
        P(("grp", "brick"), None),
        P(("grp", "brick")),
        P(),
        P(),
    )
    return jax.shard_map(
        local,
        mesh=mesh,
        in_specs=placed,
        out_specs=(
            P(None, ("grp", "brick")),
            P(None, ("grp", "brick")),
            P(None, ("grp", "brick")),
            P(),
            P(),
            P(),
        ),
        check_vma=False,
    )
```

profile of v0, /device:TPU:0, one launch (start us, length us, event | category | flops | bytes accessed | tf_op | source)
XLA Modules:
  0.0 1974.6 jit_solution(9411478524763454156)
XLA Ops:
  181.0 43.5 %gather_fusion.2 = f32[12288,3]{1,0:T(8,128)} fusion(f32[3,10240]{0,1:T(8,128)} %slice.397, s32[12288]{0:T(1024)S(1)} %broadcast_clamp_fusion.6), kind=kCustom, calls=%fused_computation.2 | custom fusion | bytes 344064 | tf_op jit(solution)/shard_map/gather | solution.py:111
  268.0 43.5 %gather_fusion = f32[12288,3]{1,0:T(8,128)} fusion(f32[3,10240]{0,1:T(8,128)} %slice.397, s32[12288]{0:T(1024)S(1)} %broadcast_clamp_fusion.7), kind=kCustom, calls=%fused_computation | custom fusion | bytes 344064 | tf_op jit(solution)/shard_map/gather | solution.py:111
  311.5 43.5 %gather_fusion.7 = f32[12288,128]{1,0:T(8,128)} fusion(f32[128,10240]{0,1:T(8,128)} %slice.399, s32[12288]{0:T(1024)S(1)} %broadcast_clamp_fusion.4), kind=kCustom, calls=%fused_computation.7 | custom fusion | bytes 12632064 | tf_op jit(solution)/shard_map/gather | solution.py:112
  355.1 43.5 %gather_fusion.6 = f32[12288,3]{1,0:T(8,128)} fusion(f32[3,10240]{0,1:T(8,128)} %slice.397, s32[12288]{0:T(1024)S(1)} %broadcast_clamp_fusion.4), kind=kCustom, calls=%fused_computation.6 | custom fusion | bytes 344064 | tf_op jit(solution)/shard_map/gather | solution.py:111
  398.6 43.5 %gather_fusion.5 = f32[12288,128]{1,0:T(8,128)} fusion(f32[128,10240]{0,1:T(8,128)} %slice.399, s32[12288]{0:T(1024)S(1)} %broadcast_clamp_fusion.5), kind=kCustom, calls=%fused_computation.5 | custom fusion | bytes 12632064 | tf_op jit(solution)/shard_map/gather | solution.py:112
  442.1 43.5 %gather_fusion.4 = f32[12288,3]{1,0:T(8,128)} fusion(f32[3,10240]{0,1:T(8,128)} %slice.397, s32[12288]{0:T(1024)S(1)} %broadcast_clamp_fusion.5), kind=kCustom, calls=%fused_computation.4 | custom fusion | bytes 344064 | tf_op jit(solution)/shard_map/gather | solution.py:111
  485.6 43.5 %gather_fusion.11 = f32[12288,128]{1,0:T(8,128)} fusion(f32[128,10240]{0,1:T(8,128)} %slice.399, s32[12288]{0:T(1024)S(1)} %broadcast_clamp_fusion.2), kind=kCustom, calls=%fused_computation.11 | custom fusion | bytes 12632064 | tf_op jit(solution)/shard_map/gather | solution.py:112
  529.2 43.5 %gather_fusion.10 = f32[12288,3]{1,0:T(8,128)} fusion(f32[3,10240]{0,1:T(8,128)} %slice.397, s32[12288]{0:T(1024)S(1)} %broadcast_clamp_fusion.2), kind=kCustom, calls=%fused_computation.10 | custom fusion | bytes 344064 | tf_op jit(solution)/shard_map/gather | solution.py:111
  572.7 43.5 %gather_fusion.9 = f32[12288,128]{1,0:T(8,128)} fusion(f32[128,10240]{0,1:T(8,128)} %slice.399, s32[12288]{0:T(1024)S(1)} %broadcast_clamp_fusion.3), kind=kCustom, calls=%fused_computation.9 | custom fusion | bytes 12632064 | tf_op jit(solution)/shard_map/gather | solution.py:112
  616.2 43.6 %gather_fusion.8 = f32[12288,3]{1,0:T(8,128)} fusion(f32[3,10240]{0,1:T(8,128)} %slice.397, s32[12288]{0:T(1024)S(1)} %broadcast_clamp_fusion.3), kind=kCustom, calls=%fused_computation.8 | custom fusion | bytes 344064 | tf_op jit(solution)/shard_map/gather | solution.py:111
  659.8 43.6 %gather_fusion.15 = f32[12288,128]{1,0:T(8,128)} fusion(f32[128,10240]{0,1:T(8,128)} %slice.399, s32[12288]{0:T(1024)S(1)} %copy-done.21), kind=kCustom, calls=%fused_computation.15 | custom fusion | bytes 12632064 | tf_op jit(solution)/shard_map/gather | solution.py:112
  746.8 43.6 %gather_fusion.13 = f32[12288,128]{1,0:T(8,128)} fusion(f32[128,10240]{0,1:T(8,128)} %slice.399, s32[12288]{0:T(1024)S(1)} %copy-done.22), kind=kCustom, calls=%fused_computation.13 | custom fusion | bytes 12632064 | tf_op jit(solution)/shard_map/gather | solution.py:112
  790.4 43.5 %gather_fusion.12 = f32[12288,3]{1,0:T(8,128)} fusion(f32[3,10240]{0,1:T(8,128)} %slice.397, s32[12288]{0:T(1024)S(1)} %copy-done.22), kind=kCustom, calls=%fused_computation.12 | custom fusion | bytes 344064 | tf_op jit(solution)/shard_map/gather | solution.py:111
  1014.1 64.3 %scatter_fusion = f32[3,10240]{0,1:T(8,128)} fusion(f32[3,10240]{0,1:T(8,128)} %scatter-add.94, s32[12288]{0:T(1024)S(1)} %copy-done.50, f32[12288,3]{1,0:T(8,128)} %bitcast.439), kind=kCustom, calls=%fused_computation.17 | custom fusion | flops 36864 | bytes 491520 | tf_op jit(solution)/shard_map/scatter-add | solution.py:121
  1081.1 64.1 %scatter_fusion.1 = f32[3,10240]{0,1:T(8,128)} fusion(f32[3,10240]{0,1:T(8,128)} %fusion.193, s32[12288]{0:T(1024)S(1)} %copy-done.46, f32[12288,3]{1,0:T(8,128)} %bitcast.438), kind=kCustom, calls=%fused_computation.18 | custom fusion | flops 36864 | bytes 491520 | tf_op jit(solution)/shard_map/scatter-add | solution.py:121
  1159.1 64.1 %scatter_fusion.2 = f32[3,10240]{0,1:T(8,128)} fusion(f32[3,10240]{0,1:T(8,128)} %fusion.197, s32[12288]{0:T(1024)S(1)} %copy-done.48, f32[12288,3]{1,0:T(8,128)} %bitcast.443), kind=kCustom, calls=%fused_computation.19 | custom fusion | flops 36864 | bytes 491520 | tf_op jit(solution)/shard_map/scatter-add | solution.py:121
  1225.9 64.1 %scatter_fusion.3 = f32[3,10240]{0,1:T(8,128)} fusion(f32[3,10240]{0,1:T(8,128)} %fusion.201, s32[12288]{0:T(1024)S(1)} %copy-done.44, f32[12288,3]{1,0:T(8,128)} %bitcast.440), kind=kCustom, calls=%fused_computation.20 | custom fusion | flops 36864 | bytes 491520 | tf_op jit(solution)/shard_map/scatter-add | solution.py:121
  1302.9 64.1 %scatter_fusion.4 = f32[3,10240]{0,1:T(8,128)} fusion(f32[3,10240]{0,1:T(8,128)} %fusion.205, s32[12288]{0:T(1024)S(1)} %copy-done.42, f32[12288,3]{1,0:T(8,128)} %bitcast.444), kind=kCustom, calls=%fused_computation.21 | custom fusion | flops 36864 | bytes 491520 | tf_op jit(solution)/shard_map/scatter-add | solution.py:121
  1369.5 64.3 %scatter_fusion.5 = f32[3,10240]{0,1:T(8,128)} fusion(f32[3,10240]{0,1:T(8,128)} %fusion.209, s32[12288]{0:T(1024)S(1)} %copy-done.40, f32[12288,3]{1,0:T(8,128)} %bitcast.441), kind=kCustom, calls=%fused_computation.22 | custom fusion | flops 36864 | bytes 491520 | tf_op jit(solution)/shard_map/scatter-add | solution.py:121
  1446.8 64.1 %scatter_fusion.6 = f32[3,10240]{0,1:T(8,128)} fusion(f32[3,10240]{0,1:T(8,128)} %fusion.213, s32[12288]{0:T(1024)S(1)} %copy-done.38, f32[12288,3]{1,0:T(8,128)} %bitcast.445), kind=kCustom, calls=%fused_computation.23 | custom fusion | flops 36864 | bytes 491520 | tf_op jit(solution)/shard_map/scatter-add | solution.py:121
  1513.4 64.1 %scatter_fusion.7 = f32[3,10240]{0,1:T(8,128)} fusion(f32[3,10240]{0,1:T(8,128)} %fusion.217, s32[12288]{0:T(1024)S(1)} %copy-done.36, f32[12288,3]{1,0:T(8,128)} %bitcast.442), kind=kCustom, calls=%fused_computation.24 | custom fusion | flops 36864 | bytes 491520 | tf_op jit(solution)/shard_map/scatter-add | solution.py:121
  1604.7 90.5 %scatter_custom_fusion.9 = f32[24576]{0:T(1024)S(1)} fusion(s32[24576]{0:T(1024)} %reshape.613, f32[24576]{0:T(1024)S(1)} %reshape.615, f32[]{:T(128)} %constant.316.clone.1), kind=kCustom, calls=%fused_computation.386 | custom fusion | bytes 98816
  1728.5 169.0 %scatter_custom_fusion.10 = f32[1536]{0:T(1024)S(1)} fusion(s32[24576]{0:T(1024)S(1)} %reshape.619, f32[24576]{0:T(1024)S(1)} %reshape.621, f32[]{:T(128)} %constant.316.clone.1), kind=kCustom, calls=%fused_computation.423 | custom fusion | flops 24576 | bytes 6148
  1911.0 63.2 %all-reduce.1 = (f32[8,128]{1,0:T(8,128)}, f32[128]{0:T(128)}, f32[]{:T(128)}) all-reduce(f32[8,128]{1,0:T(8,128)S(1)} %fusion.183, f32[128]{0:T(128)S(1)} %convolution_bitcast_fusion.8, f32[]{:T(128)S(6)} %div.129), channel_id=1, replica_groups=mesh['grp'=4,'brick'=32] {'grp','brick'}, use_global_device_ids=true, to_apply=%region_56.57 | all-reduce | flops 1153 | bytes 9224 | tf_op jit(solution)/shard_map/psum | solution.py:183
  (421 shorter events, 569.1 us)
Async XLA Ops:
  0.6 850.7 %copy-start = (f32[128,128]{1,0:T(8,128)S(1)}, f32[128,128]{1,0:T(8,128)}, u32[]{:S(2)}) copy-start(f32[128,128]{1,0:T(8,128)} %param.40) | copy-start | bytes 196612
  11.4 111.2 %collective-permute-start.1 = (f32[131,1024]{1,0:T(8,128)S(1)}, f32[131,1024]{1,0:T(8,128)S(1)}, u32[]{:S(2)}, u32[]{:S(2)}) collective-permute-start(f32[131,1024]{1,0:T(8,128)S(1)} %copy.294), channel_id=1, source_target_pairs={{1,0},{2,1},{3,2},{4,3},{5,4},{6,5},{7,6},{8,7},{9,8},{10,9},{11,1... | collective-permute-start | bytes 1609736 | tf_op jit(solution)/shard_map/ppermute | solution.py:26
  13.8 109.1 %collective-permute-start = (f32[131,1024]{1,0:T(8,128)}, f32[131,1024]{1,0:T(8,128)}, u32[]{:S(2)}, u32[]{:S(2)}) collective-permute-start(f32[131,1024]{1,0:T(8,128)} %copy.293), channel_id=1, source_target_pairs={{0,1},{1,2},{2,3},{3,4},{4,5},{5,6},{6,7},{7,8},{8,9},{9,10},{10,1... | collective-permute-start | bytes 1609736 | tf_op jit(solution)/shard_map/ppermute | solution.py:24
  31.4 90.3 %all-to-all-start = ((f32[128,1,2]{2,1,0:T(1,128)}), f32[128,1,2]{2,1,0:T(1,128)S(1)}, u32[]{:S(2)}, u32[]{:S(2)}) async-start(f32[128,1,2]{2,1,0:T(1,128)} %copy.321), calls=%async_computation | async-start | bytes 131072 | tf_op jit(solution)/shard_map/all_to_all | solution.py:162
  47.1 28.6 %collective-permute-start.5 = (f32[3,32]{1,0:T(4,128)S(1)}, f32[3,32]{1,0:T(4,128)}, u32[]{:S(2)}, u32[]{:S(2)}) collective-permute-start(f32[3,32]{1,0:T(4,128)S(1)} %get-tuple-element.224), channel_id=1, source_target_pairs={{1,0},{2,1},{3,2},{4,3},{5,4},{6,5},{7,6},{8,7},{9,8},{10,9},{11,1... | collective-permute-start | bytes 1160 | tf_op jit(solution)/shard_map/ppermute | solution.py:26
  48.4 27.3 %collective-permute-start.4 = (f32[3,32]{1,0:T(4,128)S(1)}, f32[3,32]{1,0:T(4,128)}, u32[]{:S(2)}, u32[]{:S(2)}) collective-permute-start(f32[3,32]{1,0:T(4,128)S(1)} %get-tuple-element.223), channel_id=1, source_target_pairs={{0,1},{1,2},{2,3},{3,4},{4,5},{5,6},{6,7},{7,8},{8,9},{9,10},{10,1... | collective-permute-start | bytes 1160 | tf_op jit(solution)/shard_map/ppermute | solution.py:24
  572.7 87.1 %copy-start.21 = (s32[12288]{0:T(1024)S(1)}, s32[12288]{0:T(1024)}, u32[]{:S(2)}) copy-start(s32[12288]{0:T(1024)} %broadcast_clamp_fusion) | copy-start | bytes 147460
  746.8 87.1 %copy-start.10 = (f32[3,1024]{0,1:T(8,128)S(1)}, f32[3,1024]{0,1:T(8,128)}, u32[]{:S(2)}) copy-start(f32[3,1024]{0,1:T(8,128)} %copy.300) | copy-start | bytes 36868
  1156.5 133.5 %copy-start.55 = (f32[12,1024]{1,0:T(8,128)S(1)}, f32[12,1024]{1,0:T(8,128)}, u32[]{:S(2)}) copy-start(f32[12,1024]{1,0:T(8,128)} %fusion.165) | copy-start | bytes 147460
  1156.5 133.5 %copy-start.57 = (f32[12,1024]{1,0:T(8,128)S(1)}, f32[12,1024]{1,0:T(8,128)}, u32[]{:S(2)}) copy-start(f32[12,1024]{1,0:T(8,128)} %fusion.168) | copy-start | bytes 147460
  1300.4 133.4 %copy-start.54 = (f32[12,1024]{1,0:T(8,128)S(1)}, f32[12,1024]{1,0:T(8,128)}, u32[]{:S(2)}) copy-start(f32[12,1024]{1,0:T(8,128)} %fusion.159) | copy-start | bytes 147460
  1300.4 133.4 %copy-start.56 = (f32[12,1024]{1,0:T(8,128)S(1)}, f32[12,1024]{1,0:T(8,128)}, u32[]{:S(2)}) copy-start(f32[12,1024]{1,0:T(8,128)} %fusion.162) | copy-start | bytes 147460
  1444.2 137.1 %copy-start.18 = (s32[128,3,2,32,1]{0,3,4,2,1:T(8,128)S(1)}, s32[128,3,2,32,1]{0,3,4,2,1:T(8,128)}, u32[]{:S(2)}) copy-start(s32[128,3,2,32,1]{0,3,4,2,1:T(8,128)} %copy-done.17) | copy-start | bytes 294916
  1444.2 137.1 %copy-start.20 = (s32[128,3,2,32,1]{0,3,4,2,1:T(8,128)S(1)}, s32[128,3,2,32,1]{0,3,4,2,1:T(8,128)}, u32[]{:S(2)}) copy-start(s32[128,3,2,32,1]{0,3,4,2,1:T(8,128)} %copy-done.19) | copy-start | bytes 294916
  1444.2 137.1 %copy-start.72 = (s32[2]{0:T(128)S(1)}, s32[2]{0:T(128)}, u32[]{:S(2)}) copy-start(s32[2]{0:T(128)} %constant.338) | copy-start | bytes 28
  1578.8 10.7 collective-permute-start.2
  1583.9 13.1 collective-permute-start.3
  1597.1 120.1 %copy-start.62 = (pred[128,3,2,32]{0,3,2,1:T(8,128)(4,1)S(1)}, pred[128,3,2,32]{0,3,2,1:T(8,128)(4,1)}, u32[]{:S(2)}) copy-start(pred[128,3,2,32]{0,3,2,1:T(8,128)(4,1)} %fusion.340) | copy-start | bytes 73732
  1599.4 298.1 %copy-start.64 = (f32[3,512]{1,0:T(4,128)S(1)}, f32[3,512]{1,0:T(4,128)}, u32[]{:S(2)}) copy-start(f32[3,512]{1,0:T(4,128)} %copy.333) | copy-start | bytes 18436
  1599.4 298.1 %copy-start.67 = (f32[512]{0:T(512)S(1)}, f32[512]{0:T(512)}, u32[]{:S(2)}) copy-start(f32[512]{0:T(512)} %broadcast_multiply_fusion) | copy-start | bytes 6148
  1599.4 298.3 %copy-start.13 = (f32[3,512]{0,1:T(8,128)S(1)}, f32[3,512]{0,1:T(8,128)}, u32[]{:S(2)}) copy-start(f32[3,512]{0,1:T(8,128)} %copy-done.12) | copy-start | bytes 18436
  1695.2 205.8 %copy-start.61 = (f32[16,512]{1,0:T(8,128)S(1)}, f32[16,512]{1,0:T(8,128)}, u32[]{:S(2)}) copy-start(f32[16,512]{1,0:T(8,128)} %copy-done.60) | copy-start | bytes 98308
  1695.2 205.8 %copy-start.78 = (f32[128]{0:T(128)S(1)}, f32[128]{0:T(128)}, u32[]{:S(2)}) copy-start(f32[128]{0:T(128)} %param.49) | copy-start | bytes 1540
  1696.3 30.4 %all-to-all-start.1 = ((f32[128,1,192]{2,1,0:T(1,128)}), f32[128,1,192]{2,1,0:T(1,128)S(1)}, u32[]{:S(2)}, u32[]{:S(2)}) async-start(f32[128,1,192]{2,1,0:T(1,128)} %reshape.687), calls=%async_computation.1 | async-start | bytes 262144 | tf_op jit(solution)/shard_map/all_to_all | solution.py:155
  (95 other events, 1841.4 us)
where the time goes:
time: 1980 us; the launch traced here: 1970 us
  local copies, waits for them, and re-layouts  873 us (44%)
  other arithmetic  791 us (40%)
  matrix products  176 us (9%)
  blocking collectives  63.2 us (3%)
  starting transfers between devices  53.6 us (3%)
    scatter-add x8, other arithmetic, local(): ghost_grad = ghost_grad.at[:, neighbours].add(grad_near)  513 us
    gather x8, local copies, waits for them, and re-layouts, local(): near_pos = ext_pos[:, neighbours]  348 us
    gather x8, local copies, waits for them, and re-layouts, local(): near_feat = ext_feat[:, neighbours]  348 us
    unnamed x24, other arithmetic  171 us
    dot_general x16, matrix products, block_energy(): jnp.einsum('bkn,bc->ckn', radial_basis, w_rad, precision=HIGHEST_PRECISION)  141 us
    unnamed x235, local copies, waits for them, and re-layouts  109 us
    psum x1, blocking collectives, local(): lax.psum((grad_one, grad_two, loss_part), ('grp', 'brick'))  63.2 us
  transfers between devices with their start and end apart: 8, of which 3 were waited for; matrix products, arithmetic and copies ran while one was open for 5% of the time, Pallas kernels for 0%

commit v1 on v0

v1 whole, which is shorter than its diff:
```python
import functools
import math

import jax
import jax.numpy as jnp
from jax import lax
from jax.experimental import pallas as pl
from jax.experimental.pallas import tpu as pltpu
from jax.sharding import PartitionSpec as P

G = 1024
BPB = 32
BW = 32
K = 12
L = 128
WIN = 24
AXES = ("grp", "brick")
F32 = jnp.float32
BF16 = jnp.bfloat16
RATES = tuple(0.05 * 1.6**b for b in range(8))


def iota(shape, dim):
    return lax.broadcasted_iota(jnp.int32, shape, dim)


def split(x):
    hi = x.astype(BF16).astype(F32)
    return hi, x - hi


def nn(a, b):
    return lax.dot_general(a, b, (((1,), (0,)), ((), ())), preferred_element_type=F32)


def nt(a, b):
    return lax.dot_general(a, b, (((1,), (1,)), ((), ())), preferred_element_type=F32)


def tn(a, b):
    return lax.dot_general(a, b, (((0,), (0,)), ((), ())), preferred_element_type=F32)


def dot3(dot, a, b):
    a_hi, a_lo = (t.astype(BF16) for t in split(a))
    b_hi, b_lo = (t.astype(BF16) for t in split(b))
    return dot(a_hi, b_hi) + dot(a_lo, b_hi) + dot(a_hi, b_lo)


def sigmoid(v):
    return 1.0 / (1.0 + jnp.exp(-v))


def rate_column():
    rows = iota((8, L), 0)
    out = jnp.zeros((8, L), F32)
    for b, rate in enumerate(RATES):
        out = jnp.where(rows == b, rate, out)
    return out


def stack_basis(basis):
    hi, lo = split(basis)
    return jnp.concatenate([hi, lo, hi, jnp.zeros_like(hi)], axis=0)


def stack_weight(weight):
    hi, lo = split(weight)
    return jnp.concatenate([hi, hi, lo, jnp.zeros_like(hi)], axis=0)


def teacher_kernel(
    idx_s, idx_v, count_v, feat, left, right, pos, w_rad, w_mix, w_out, acc, table, rows
):
    step = pl.program_id(0)

    @pl.when(step == 0)
    def _():
        acc[...] = jnp.zeros_like(acc)

        def flip(source, base):
            def one(j, carry):
                src = pl.ds(pl.multiple_of(j * L, L), L)
                dst = pl.ds(pl.multiple_of(base + j * L, L), L)
                table[dst, :] = source[:, src].T
                return carry

            lax.fori_loop(0, source.shape[1] // L, one, 0)

        flip(left, 0)
        flip(feat, G)
        flip(right, G + feat.shape[1])

    for s in range(K):
        def fetch(g, carry):
            base = pl.multiple_of(g * 64, 64)
            for j in range(64):
                r = idx_s[s, base + j]
                rows[pl.ds(s * L + base + j, 1), :] = table[pl.ds(r, 1), :]
            return carry

        lax.fori_loop(0, L // 64, fetch, 0)

    rel = idx_v[...] - step * L
    hi = rel >> 7
    lo = rel & 127
    sub = iota((L, L), 0)
    subw = iota((WIN, L), 0)
    hot = jnp.concatenate(
        [jnp.where(sub == lo[s : s + 1, :], 1.0, 0.0) for s in range(K)], axis=1
    ).astype(BF16)
    masks = [subw == hi[s : s + 1, :] for s in range(K)]
    source = jnp.concatenate([pos[j, pl.ds(step, WIN), :] for j in range(6)], axis=0)
    found = nn(source.astype(BF16), hot)
    own = [pos[c, pl.ds(step + 8, 1), :] + pos[3 + c, pl.ds(step + 8, 1), :] for c in range(3)]
    rates = rate_column()
    live = iota((K, L), 0) < count_v[0]
    offsets = []
    bases = []
    for s in range(K):
        lanes = slice(s * L, (s + 1) * L)
        d = []
        for c in range(3):
            both = found[c * WIN : (c + 1) * WIN, lanes] + found[(3 + c) * WIN : (4 + c) * WIN, lanes]
            d.append(jnp.sum(jnp.where(masks[s], both, 0.0), axis=0, keepdims=True) - own[c])
        q = d[0] * d[0] + d[1] * d[1] + d[2] * d[2]
        basis = jnp.exp(-rates * q) * jnp.where(live[s : s + 1, :], 1.0, 0.0)
        offsets.append(d)
        bases.append(stack_basis(basis))
    weight = w_rad[...]
    rate_w = rate_column() * weight
    weights = jnp.concatenate([stack_weight(weight), stack_weight(-rate_w)], axis=1)
    radial = tn(jnp.concatenate(bases, axis=1).astype(BF16), weights.astype(BF16))
    message = jnp.zeros((L, L), F32)
    for s in range(K):
        message += radial[s * L : (s + 1) * L, :L] * rows[s * L : (s + 1) * L, :]
    scale = 1.0 / math.sqrt(K)
    own_rows = table[pl.ds(pl.multiple_of(G + step * L, L), L), :]
    pre = dot3(nn, message * scale, w_mix[...]) + own_rows
    sig = sigmoid(pre)
    up = w_out[...] * (sig * (1.0 + pre * (1.0 - sig)))
    back = dot3(nt, up * scale, w_mix[...])
    ones = jnp.ones((2 * L, L), BF16)
    diag = sub == iota((L, L), 1)
    own_grad = [jnp.zeros((1, L), F32) for _ in range(3)]
    parts = [[] for _ in range(6)]
    for s in range(K):
        prod = back * rows[s * L : (s + 1) * L, :] * radial[s * L : (s + 1) * L, L:]
        prod_hi, prod_lo = split(prod)
        total = nn(jnp.concatenate([prod_hi, prod_lo], axis=1).astype(BF16), ones)
        slope = 2.0 * jnp.sum(jnp.where(diag, total, 0.0), axis=0, keepdims=True)
        for c in range(3):
            value = slope * offsets[s][c]
            own_grad[c] -= value
            v_hi, v_lo = split(value)
            parts[c].append(jnp.where(masks[s], v_hi, 0.0))
            parts[3 + c].append(jnp.where(masks[s], v_lo, 0.0))
    spread = jnp.concatenate([jnp.concatenate(p, axis=1) for p in parts], axis=0).astype(BF16)
    out = nt(spread, hot)
    for c in range(3):
        both = out[c * WIN : (c + 1) * WIN] + out[(3 + c) * WIN : (4 + c) * WIN]
        both += jnp.where(subw == 8, own_grad[c], 0.0)
        acc[c, pl.ds(step, WIN), :] += both


def teacher(idx, count, feat, left, right, ext_pos, w_rad, w_mix, w_out):
    atoms = feat.shape[1]
    steps = atoms // L
    ext_rows = (atoms + 2 * G) // L
    tall = ext_rows + 24
    pos = jnp.pad(ext_pos.reshape(3, ext_rows, L), ((0, 0), (0, 24), (0, 0)))
    hi = lax.reduce_precision(pos, 8, 7)
    pos = jnp.concatenate([hi, pos - hi], axis=0)
    whole = lambda shape: pl.BlockSpec(shape, lambda i: (0,) * len(shape))
    return pl.pallas_call(
        teacher_kernel,
        grid=(steps,),
        in_specs=[
            pl.BlockSpec((K, L), lambda i: (0, i), memory_space=pltpu.SMEM),
            pl.BlockSpec((K, L), lambda i: (0, i)),
            pl.BlockSpec((1, 1, L), lambda i: (i, 0, 0)),
            whole(feat.shape),
            whole(left.shape),
            whole(right.shape),
            whole(pos.shape),
            whole((8, L)),
            whole((L, L)),
            whole((1, L)),
        ],
        out_specs=whole((3, tall, L)),
        out_shape=jax.ShapeDtypeStruct((3, tall, L), F32),
        scratch_shapes=[
            pltpu.VMEM((atoms + 2 * G, L), F32),
            pltpu.VMEM((K * L, L), F32),
        ],
        compiler_params=pltpu.CompilerParams(vmem_limit_bytes=52 * 2**20),
        cost_estimate=pl.CostEstimate(
            flops=2 * 10**10, bytes_accessed=8 * 2**20, transcendentals=10**6
        ),
        name="teacher",
    )(
        idx,
        idx,
        count.reshape(steps, 1, L),
        feat,
        left,
        right,
        pos,
        w_rad,
        w_mix,
        w_out.reshape(1, L),
    )


KB = 16


def student_kernel(nbr, pos, w_first, w_second, force, off_out, basis_out, hid_out, slope_out):
    step = pl.program_id(0)
    rel = nbr[...] - step * L
    hi = rel >> 7
    lo = rel & 127
    lane = iota((1, L), 1)
    near = []
    own = []
    for c in range(3):
        first = pos[c, pl.ds(step, 1), :]
        second = pos[c, pl.ds(step + 1, 1), :]
        take = lambda row: jnp.take_along_axis(
            jnp.broadcast_to(row, (KB, L)), lo, axis=1, mode="promise_in_bounds"
        )
        near.append(jnp.where(hi == 0, take(first), take(second)))
        own.append(
            jnp.where(lane < L - BW, pltpu.roll(first, L - BW, 1), pltpu.roll(second, L - BW, 1))
        )
    offs = [near[c] - own[c] for c in range(3)]
    q = offs[0] * offs[0] + offs[1] * offs[1] + offs[2] * offs[2]
    rates = rate_column()
    basis = [jnp.exp(-rates * q[s : s + 1, :]) for s in range(KB)]
    stacked = jnp.concatenate([stack_basis(b) for b in basis], axis=1).astype(BF16)
    z = tn(stack_weight(w_first[...]).astype(BF16), stacked)
    w2 = w_second[...]
    out = [jnp.zeros((1, L), F32) for _ in range(3)]
    for s in range(KB):
        lanes = slice(s * L, (s + 1) * L)
        zs = z[:, lanes]
        sig = sigmoid(zs)
        hid = zs * sig
        hid_out[:, lanes] = hid
        slope_out[:, lanes] = w2 * (sig * (1.0 + zs * (1.0 - sig)))
        strength = jnp.sum(w2 * hid, axis=0, keepdims=True)
        basis_out[:, lanes] = basis[s]
        for c in range(3):
            out[c] += strength * offs[c][s : s + 1, :]
    for c in range(3):
        off_out[c] = offs[c]
        force[pl.ds(c, 1), :] = out[c]


def student(nbr, pos, w_first, w_second):
    beads = nbr.shape[1]
    steps = beads // L
    edges = KB * L
    whole = lambda shape: pl.BlockSpec(shape, lambda i: (0,) * len(shape))
    wide = lambda n: pl.BlockSpec((n, edges), lambda i: (0, i))
    return pl.pallas_call(
        student_kernel,
        grid=(steps,),
        in_specs=[
            pl.BlockSpec((KB, L), lambda i: (0, i)),
            whole(pos.shape),
            whole((8, L)),
            whole((L, 1)),
        ],
        out_specs=[
            pl.BlockSpec((3, L), lambda i: (0, i)),
            pl.BlockSpec((3, KB, L), lambda i: (0, 0, i)),
            wide(8),
            wide(L),
            wide(L),
        ],
        out_shape=[
            jax.ShapeDtypeStruct((3, beads), F32),
            jax.ShapeDtypeStruct((3, KB, beads), F32),
            jax.ShapeDtypeStruct((8, KB * beads), F32),
            jax.ShapeDtypeStruct((L, KB * beads), F32),
            jax.ShapeDtypeStruct((L, KB * beads), F32),
        ],
        compiler_params=pltpu.CompilerParams(vmem_limit_bytes=40 * 2**20),
        cost_estimate=pl.CostEstimate(
            flops=10**9, bytes_accessed=8 * 2**20, transcendentals=10**6
        ),
        name="student",
    )(nbr, pos, w_first, w_second.reshape(L, 1))


CHUNK = 1024


def mapping_kernel(force, bead, dest, start, out):
    step = pl.program_id(0)

    @pl.when(step == 0)
    def _():
        out[...] = jnp.zeros_like(out)

    b = bead[...]
    hot = iota((BPB, CHUNK), 0) == b
    highs = []
    lows = []
    for c in range(3):
        hi, lo = split(force[pl.ds(c, 1), :])
        highs.append(jnp.where(hot, hi, 0.0))
        lows.append(jnp.where(hot, lo, 0.0))
    hi, lo = split(start[...])
    first = (iota((BPB, CHUNK), 0) == 0) & (iota((BPB, CHUNK), 1) % 32 == 0)
    highs.append(jnp.where(first, hi, 0.0))
    lows.append(jnp.where(first, lo, 0.0))
    values = jnp.concatenate(highs + lows, axis=0).astype(BF16)
    place = jnp.where(iota((2 * L, CHUNK), 0) == dest[...], 1.0, 0.0).astype(BF16)
    got = nt(place, values)
    out[...] += got[:, :L] + got[:, L:]


def mapping(force, bead, dest, start):
    atoms = force.shape[1]
    row = lambda n: pl.BlockSpec((n, CHUNK), lambda i: (0, i))
    return pl.pallas_call(
        mapping_kernel,
        grid=(atoms // CHUNK,),
        in_specs=[row(3), row(1), row(1), row(1)],
        out_specs=pl.BlockSpec((2 * L, L), lambda i: (0, 0)),
        out_shape=jax.ShapeDtypeStruct((2 * L, L), F32),
        name="mapping",
    )(force, bead, dest, start)


def bead_kernel(beads_all, recv, weight, pred, offs, basis, hid, slope, force, out):
    step = pl.program_id(0)
    beads = force.shape[1]

    @pl.when(step == 0)
    def _():
        out[...] = jnp.zeros_like(out)
        turned = jnp.concatenate([recv[:L, :].T, recv[L:, :].T], axis=1)
        start = (turned[96:97, :] + 0.5).astype(jnp.int32)
        hot = jnp.where(iota((beads, 2 * L), 0) == start, 1.0, 0.0).astype(BF16)
        hi, lo = split(turned[:96, :])
        got = nt(jnp.concatenate([hi, lo], axis=0).astype(BF16), hot)
        for c in range(3):
            rows = got[c * BPB : (c + 1) * BPB] + got[96 + c * BPB : 96 + (c + 1) * BPB]
            rows = pltpu.roll(rows, 0, 1, stride=1, stride_axis=0)
            force[pl.ds(c, 1), :] = jnp.sum(rows, axis=0, keepdims=True)

    lanes = pl.ds(pl.multiple_of(step * L, L), L)
    w = weight[...]
    loss = jnp.zeros((1, L), F32)
    pull = []
    for c in range(3):
        res = pred[pl.ds(c, 1), :] - force[pl.ds(c, 1), lanes]
        loss += w * (res * res)
        pull.append((2.0 / (3.0 * beads_all)) * w * res)
    ds = sum(offs[c] * pull[c] for c in range(3))
    rows = jnp.concatenate([ds[s : s + 1, :] for s in range(KB)], axis=1)
    rows_hi, rows_lo = split(rows)
    zeros = jnp.zeros((6, rows.shape[1]), F32)
    second_in = jnp.concatenate([rows_hi, rows_lo, zeros], axis=0).astype(BF16)
    first_hi, first_lo = split(basis[...] * rows)
    first_in = jnp.concatenate([first_hi, first_lo], axis=0).astype(BF16)
    slope_hi, slope_lo = (t.astype(BF16) for t in split(slope[...]))
    hid_hi, hid_lo = (t.astype(BF16) for t in split(hid[...]))
    got_hi = nt(first_in, slope_hi)
    got_lo = nt(first_in, slope_lo)
    out[0:8, :] += got_hi[:8] + got_hi[8:] + got_lo[:8]
    two_hi = nt(second_in, hid_hi)
    two_lo = nt(second_in, hid_lo)
    out[8:9, :] += two_hi[0:1] + two_hi[1:2] + two_lo[0:1]
    out[9:10, :] += loss * (1.0 / (3.0 * beads_all))


def bead_stage(recv, weight, pred, offs, basis, hid, slope, beads_all):
    beads = pred.shape[1]
    edges = KB * L
    whole = lambda shape: pl.BlockSpec(shape, lambda i: (0,) * len(shape))
    wide = lambda n: pl.BlockSpec((n, edges), lambda i: (0, i))
    return pl.pallas_call(
        functools.partial(bead_kernel, beads_all),
        grid=(beads // L,),
        in_specs=[
            whole(recv.shape),
            pl.BlockSpec((1, L), lambda i: (0, i)),
            pl.BlockSpec((3, L), lambda i: (0, i)),
            pl.BlockSpec((3, KB, L), lambda i: (0, 0, i)),
            wide(8),
            wide(L),
            wide(L),
        ],
        out_specs=[whole((3, beads)), whole((16, L))],
        out_shape=[
            jax.ShapeDtypeStruct((3, beads), F32),
            jax.ShapeDtypeStruct((16, L), F32),
        ],
        compiler_params=pltpu.CompilerParams(vmem_limit_bytes=40 * 2**20),
        name="beads",
    )(recv, weight, pred, offs, basis, hid, slope)


def halo(cells, width):
    count = lax.axis_size(AXES)
    up = [(i, i + 1) for i in range(count - 1)]
    down = [(i + 1, i) for i in range(count - 1)]
    left = lax.ppermute(cells[:, cells.shape[1] - width :], AXES, up)
    right = lax.ppermute(cells[:, :width], AXES, down)
    return left, right


def local(
    positions,
    features,
    teacher_nbr,
    nbr_count,
    w_rad,
    w_mix,
    w_out,
    block_owner,
    block_start,
    atom_bead,
    bead_pos,
    bead_nbr,
    bead_weight,
    w_first,
    w_second,
):
    atoms = positions.shape[1]
    devices = lax.axis_size(AXES)
    count = devices
    beads = bead_pos.shape[1]
    left, right = halo(features, G)
    small = jnp.concatenate([positions[:, :G], bead_pos[:, :BW]], axis=1)
    small_end = jnp.concatenate([positions[:, atoms - G :], bead_pos[:, beads - BW :]], axis=1)
    up = [(i, i + 1) for i in range(count - 1)]
    down = [(i + 1, i) for i in range(count - 1)]
    small_left = lax.ppermute(small_end, AXES, up)
    small_right = lax.ppermute(small, AXES, down)
    ext_pos = jnp.concatenate([small_left[:, :G], positions, small_right[:, :G]], axis=1)
    bead_ext = jnp.concatenate(
        [small_left[:, G:], bead_pos, small_right[:, G:], jnp.zeros((3, L - 2 * BW), F32)], axis=1
    )
    pred, offs, basis, hid, slope = student(
        bead_nbr.T, bead_ext.reshape(3, (beads + L) // L, L), w_first, w_second
    )
    blocks = block_owner.shape[0]
    block_atoms = atoms // blocks
    order = jnp.arange(blocks, dtype=jnp.int32)
    same = (block_owner[:, None] == block_owner[None, :]) & (order[None, :] < order[:, None])
    dest = 2 * block_owner + jnp.sum(same.astype(jnp.int32), axis=1)
    spread = lambda v: jnp.broadcast_to(v[:, None], (blocks, block_atoms)).reshape(1, atoms)
    acc = teacher(
        teacher_nbr.T, nbr_count, features, left, right, ext_pos, w_rad, w_mix, w_out
    )
    ext_rows = (atoms + 2 * G) // L
    grads = acc[:, :ext_rows].reshape(3, atoms + 2 * G)
    above = lax.ppermute(grads[:, :G], AXES, down)
    below = lax.ppermute(grads[:, atoms + G :], AXES, up)
    force = -grads[:, G : atoms + G]
    force = force - jnp.pad(below, ((0, 0), (0, atoms - G))) - jnp.pad(above, ((0, 0), (atoms - G, 0)))
    outgoing = mapping(
        force, atom_bead.reshape(1, atoms), spread(dest), spread(block_start.astype(F32))
    )
    recv = lax.all_to_all(outgoing, AXES, split_axis=0, concat_axis=0, tiled=True)
    bead_force, sums = bead_stage(
        recv, bead_weight.reshape(1, beads), pred, offs, basis, hid, slope, beads * devices
    )
    sums = lax.psum(sums, AXES)
    return force, bead_force, pred, sums[:8], sums[8], jnp.sum(sums[9])


def solution(mesh):
    wide = P(None, AXES)
    tall = P(AXES, None)
    flat = P(AXES)
    return jax.shard_map(
        local,
        mesh=mesh,
        in_specs=(
            wide, wide, tall, flat, P(), P(), P(), flat, flat, flat, wide, tall, flat, P(), P(),
        ),
        out_specs=(wide, wide, wide, P(), P(), P()),
        check_vma=False,
    )
```

time: 1980 us -> 487 us (0.25)
  local copies, waits for them, and re-layouts: 873 us -> 19.2 us
  other arithmetic: 791 us -> 3.82 us
  Pallas kernels: 0 us -> 342 us
  matrix products: 176 us -> 0 us
    gather x17 -> x0, local copies, waits for them, and re-layouts: 724 us -> none  [the longest x8 348 us: local(): near_pos = ext_pos[:, neighbours]]
    scatter-add x17 -> x0, other arithmetic: 533 us -> none  [the longest x8 513 us: local(): ghost_grad = ghost_grad.at[:, neighbours].add(grad_near)]
    pallas_call x0 -> x4, Pallas kernels: none -> 342 us  [the longest x1 328 us: teacher(): pl.pallas_call(teacher_kernel, grid=(steps,), in_specs=[pl.BlockSpec((K,...]
    dot_general x37 -> x0, matrix products: 176 us -> none  [the longest x16 141 us: block_energy(): jnp.einsum('bkn,bc->ckn', radial_basis, w_rad, precision=HIGHEST_PRECISION)]
    unnamed x24 -> x1, other arithmetic: 171 us -> 0.94 us
    unnamed x235 -> x39, local copies, waits for them, and re-layouts: 109 us -> 13.9 us
    reduce_sum x18 -> x2, other arithmetic: 65.4 us -> 2.04 us  [the longest x1 1.11 us: local(): return (force, bead_force, pred, sums[:8], sums[8], jnp.sum(sums[9]))]
  transfers between devices with their start and end apart: 8 -> 7, of which waited for: 3 -> 3; matrix products, arithmetic and copies ran while one was open for 5% -> 1% of each run, Pallas kernels for 0% -> 1%
where the time goes in v1:
time: 487 us; the launch traced here: 486 us
  Pallas kernels  342 us (70%)
  blocking collectives  65.7 us (13%)
  starting transfers between devices  46.1 us (9%)
  local copies, waits for them, and re-layouts  19.2 us (4%)
  waiting for transfers between devices  8.05 us (2%)
    pallas_call x1, Pallas kernels, teacher(): pl.pallas_call(teacher_kernel, grid=(steps,), in_specs=[pl.BlockSpec((K,...  328 us
    psum x1, blocking collectives, local(): sums = lax.psum(sums, AXES)  65.7 us
    all_to_all x1, starting transfers between devices, local(): lax.all_to_all(outgoing, AXES, split_axis=0, concat_axis=0, tiled=True)  27.3 us
    unnamed x39, local copies, waits for them, and re-layouts  13.9 us
  transfers between devices with their start and end apart: 7, of which 3 were waited for; matrix products, arithmetic and copies ran while one was open for 1% of the time, Pallas kernels for 1%

profile of v1, /device:TPU:0, one launch (start us, length us, event | category | flops | bytes accessed | tf_op | source)
XLA Modules:
  0.0 485.6 jit_solution(11667520946417004967)
XLA Ops:
  2.2 1.3 collective-permute-start.3
  3.5 1.3 fusion.3
  4.8 1.3 collective-permute-start.1
  6.1 5.2 %collective-permute-start = (f32[128,1024]{1,0:T(8,128)S(1)}, f32[128,1024]{1,0:T(8,128)S(1)}, u32[]{:S(2)}, u32[]{:S(2)}) collective-permute-start(f32[128,1024]{1,0:T(8,128)S(1)} %get-tuple-element.21), channel_id=1, source_target_pairs={{0,1},{1,2},{2,3},{3,4},{4,5},{5,6},{6,7},{7,8},{8,9},{9,10},{10,1... | collective-permute-start | bytes 1572872 | tf_op jit(solution)/shard_map/ppermute | solution.py:412
  11.3 3.9 collective-permute-start.2
  15.2 0.9 convert_reduce_fusion
  16.2 2.0 collective-permute-done.2
  18.1 0.9 maximum_bitcast_fusion
  20.0 1.0 copy-done.6
  24.0 328.2 %teacher.1 = f32[3,104,128]{2,1,0:T(8,128)S(1)} custom-call(s32[12,8192]{1,0:T(8,128)S(1)} %bitcast.23, s32[12,8192]{1,0:T(8,128)S(1)} %bitcast.24, s32[64,1,128]{2,1,0:T(1,128)S(1)} %bitcast.25, f32[128,8192]{1,0:T(8,128)} %feat.1, f32[128,1024]{1,0:T(8,128)S(1)} %collective-permute-done.left, f32[128,1024]{1,0:T(8,128)} %copy-done.17, ...), custom_call_target="tpu_custom_call" | custom-call | flops 20000000000 | bytes 8388608 | tf_op jit(solution)/shard_map/teacher/pallas_call | solution.py:175
  352.3 5.9 %collective-permute-start.4 = (f32[3,1024]{1,0:T(4,128)S(1)}, f32[3,1024]{1,0:T(4,128)S(1)}, u32[]{:S(2)}, u32[]{:S(2)}) collective-permute-start(f32[3,1024]{1,0:T(4,128)S(1)} %get-tuple-element.22), channel_id=1, source_target_pairs={{0,1},{1,2},{2,3},{3,4},{4,5},{5,6},{6,7},{7,8},{8,9},{9,10},{10,1... | collective-permute-start | bytes 36872 | tf_op jit(solution)/shard_map/ppermute | solution.py:464
  358.2 1.3 collective-permute-start.5
  361.4 4.8 collective-permute-done.5
  366.9 5.3 %mapping.1 = f32[256,128]{1,0:T(8,128)} custom-call(f32[3,8192]{1,0:T(4,128)} %fusion.2.force, s32[1,8192]{1,0:T(1,128)} %bitcast.32, s32[1,8192]{1,0:T(1,128)} %reshape.53.dest, f32[1,8192]{1,0:T(1,128)} %reshape.54.start), custom_call_target="tpu_custom_call" | custom-call | tf_op jit(solution)/shard_map/mapping/pallas_call | solution.py:328
  372.2 27.3 %all-to-all-start = ((f32[128,2,128]{2,1,0:T(2,128)}), f32[128,2,128]{2,1,0:T(2,128)S(1)}, u32[]{:S(2)}, u32[]{:S(2)}) async-start(f32[128,2,128]{2,1,0:T(2,128)} %bitcast.30), calls=%async_computation | async-start | bytes 262144 | tf_op jit(solution)/shard_map/all_to_all | solution.py:470
  399.6 4.1 student.1
  403.7 1.9 copy-done
  405.7 2.0 copy-done.2
  407.7 1.3 all-to-all-done
  408.9 2.2 copy-done.1
  411.1 2.2 copy-done.3
  414.0 4.2 beads.1
  418.2 65.7 %psum.7 = f32[16,128]{1,0:T(8,128)S(1)} all-reduce(f32[16,128]{1,0:T(8,128)S(1)} %get-tuple-element.19), channel_id=1, replica_groups=mesh['grp'=4,'brick'=32] {'grp','brick'}, use_global_device_ids=true, to_apply=%region_1.2 | all-reduce | flops 2048 | bytes 16384 | tf_op jit(solution)/shard_map/psum | solution.py:474
  483.9 1.1 slice_reduce_fusion
  (62 shorter events, 9.4 us)
Async XLA Ops:
  2.2 14.0 %collective-permute-start.3 = (f32[3,1056]{1,0:T(4,128)S(1)}, f32[3,1056]{1,0:T(4,128)S(1)}, u32[]{:S(2)}, u32[]{:S(2)}) collective-permute-start(f32[3,1056]{1,0:T(4,128)S(1)} %pad_maximum_fusion.2), channel_id=1, source_target_pairs={{1,0},{2,1},{3,2},{4,3},{5,4},{6,5},{7,6},{8,7},{9,8},{10,9},{11,1... | collective-permute-start | bytes 38024 | tf_op jit(solution)/shard_map/ppermute | solution.py:444
  4.8 14.4 %collective-permute-start.1 = (f32[128,1024]{1,0:T(8,128)S(1)}, f32[128,1024]{1,0:T(8,128)S(1)}, u32[]{:S(2)}, u32[]{:S(2)}) collective-permute-start(f32[128,1024]{1,0:T(8,128)S(1)} %get-tuple-element.20), channel_id=1, source_target_pairs={{1,0},{2,1},{3,2},{4,3},{5,4},{6,5},{7,6},{8,7},{9,8},{10,9},{11,1... | collective-permute-start | bytes 1572872 | tf_op jit(solution)/shard_map/ppermute | solution.py:413
  6.1 13.1 %collective-permute-start = (f32[128,1024]{1,0:T(8,128)S(1)}, f32[128,1024]{1,0:T(8,128)S(1)}, u32[]{:S(2)}, u32[]{:S(2)}) collective-permute-start(f32[128,1024]{1,0:T(8,128)S(1)} %get-tuple-element.21), channel_id=1, source_target_pairs={{0,1},{1,2},{2,3},{3,4},{4,5},{5,6},{6,7},{7,8},{8,9},{9,10},{10,1... | collective-permute-start | bytes 1572872 | tf_op jit(solution)/shard_map/ppermute | solution.py:412
  11.3 6.8 %collective-permute-start.2 = (f32[3,1056]{1,0:T(4,128)S(1)}, f32[3,1056]{1,0:T(4,128)S(1)}, u32[]{:S(2)}, u32[]{:S(2)}) collective-permute-start(f32[3,1056]{1,0:T(4,128)S(1)} %pad_maximum_fusion.1), channel_id=1, source_target_pairs={{0,1},{1,2},{2,3},{3,4},{4,5},{5,6},{6,7},{7,8},{8,9},{9,10},{10,1... | collective-permute-start | bytes 38024 | tf_op jit(solution)/shard_map/ppermute | solution.py:443
  19.2 0.8 copy-start.17
  20.0 1.0 copy-start.6
  21.0 0.8 copy-start.7
  21.9 0.8 copy-start.8
  22.6 0.7 copy-start.10
  24.0 335.6 %copy-start.14 = (s32[256]{0:T(256)S(1)}, s32[256]{0:T(256)}, u32[]{:S(2)}) copy-start(s32[256]{0:T(256)} %param.22) | copy-start | bytes 3076
  24.0 335.6 %copy-start.15 = (s32[256]{0:T(256)S(1)}, s32[256]{0:T(256)}, u32[]{:S(2)}) copy-start(s32[256]{0:T(256)} %param.23) | copy-start | bytes 3076
  24.0 335.6 %copy-start.16 = (f32[128]{0:T(128)S(1)}, f32[128]{0:T(128)}, u32[]{:S(2)}) copy-start(f32[128]{0:T(128)} %param.29) | copy-start | bytes 1540
  24.0 375.6 %copy-start.13 = (f32[3,512]{1,0:T(4,128)S(1)}, f32[3,512]{1,0:T(4,128)}, u32[]{:S(2)}) copy-start(f32[3,512]{1,0:T(4,128)} %param.25) | copy-start | bytes 18436
  24.0 375.7 %copy-start.9 = (s32[512,16]{0,1:T(8,128)S(1)}, s32[512,16]{0,1:T(8,128)}, u32[]{:S(2)}) copy-start(s32[512,16]{0,1:T(8,128)} %param.26) | copy-start | bytes 98308
  24.0 375.6 %copy-start.11 = (f32[8,128]{1,0:T(8,128)S(1)}, f32[8,128]{1,0:T(8,128)}, u32[]{:S(2)}) copy-start(f32[8,128]{1,0:T(8,128)} %w_first.1) | copy-start | bytes 12292
  352.2 56.7 %copy-start.5 = (f32[512]{0:T(512)S(1)}, f32[512]{0:T(512)}, u32[]{:S(2)}) copy-start(f32[512]{0:T(512)} %param.27) | copy-start | bytes 6148
  352.3 9.1 %collective-permute-start.4 = (f32[3,1024]{1,0:T(4,128)S(1)}, f32[3,1024]{1,0:T(4,128)S(1)}, u32[]{:S(2)}, u32[]{:S(2)}) collective-permute-start(f32[3,1024]{1,0:T(4,128)S(1)} %get-tuple-element.22), channel_id=1, source_target_pairs={{0,1},{1,2},{2,3},{3,4},{4,5},{5,6},{6,7},{7,8},{8,9},{9,10},{10,1... | collective-permute-start | bytes 36872 | tf_op jit(solution)/shard_map/ppermute | solution.py:464
  358.2 8.0 %collective-permute-start.5 = (f32[3,1024]{1,0:T(4,128)S(1)}, f32[3,1024]{1,0:T(4,128)S(1)}, u32[]{:S(2)}, u32[]{:S(2)}) collective-permute-start(f32[3,1024]{1,0:T(4,128)S(1)} %get-tuple-element.23), channel_id=1, source_target_pairs={{1,0},{2,1},{3,2},{4,3},{5,4},{6,5},{7,6},{8,7},{9,8},{10,9},{11,1... | collective-permute-start | bytes 36872 | tf_op jit(solution)/shard_map/ppermute | solution.py:463
  372.2 36.7 %all-to-all-start = ((f32[128,2,128]{2,1,0:T(2,128)}), f32[128,2,128]{2,1,0:T(2,128)S(1)}, u32[]{:S(2)}, u32[]{:S(2)}) async-start(f32[128,2,128]{2,1,0:T(2,128)} %bitcast.30), calls=%async_computation | async-start | bytes 262144 | tf_op jit(solution)/shard_map/all_to_all | solution.py:470
  403.7 1.9 copy-start
  405.6 2.0 copy-start.2
  408.9 2.2 copy-start.1
  411.1 2.2 copy-start.3
  413.3 0.7 copy-start.4
  (1 other events, 0.7 us)

commit v2 on v1

--- a/solution.py
+++ b/solution.py
@@ -69,129 +69,205 @@
     return jnp.concatenate([hi, hi, lo, jnp.zeros_like(hi)], axis=0)
 
 
-def teacher_kernel(
-    idx_s, idx_v, count_v, feat, left, right, pos, w_rad, w_mix, w_out, acc, table, rows
-):
-    step = pl.program_id(0)
-
-    @pl.when(step == 0)
-    def _():
-        acc[...] = jnp.zeros_like(acc)
-
-        def flip(source, base):
-            def one(j, carry):
-                src = pl.ds(pl.multiple_of(j * L, L), L)
-                dst = pl.ds(pl.multiple_of(base + j * L, L), L)
-                table[dst, :] = source[:, src].T
-                return carry
-
-            lax.fori_loop(0, source.shape[1] // L, one, 0)
-
-        flip(left, 0)
-        flip(feat, G)
-        flip(right, G + feat.shape[1])
-
-    for s in range(K):
-        def fetch(g, carry):
-            base = pl.multiple_of(g * 64, 64)
-            for j in range(64):
-                r = idx_s[s, base + j]
-                rows[pl.ds(s * L + base + j, 1), :] = table[pl.ds(r, 1), :]
-            return carry
-
-        lax.fori_loop(0, L // 64, fetch, 0)
-
-    rel = idx_v[...] - step * L
+PAIR = 2 * L
+
+
+def teacher_block(blk, rows, fetch, idx, count, pos, weights, w_mix, w_out, acc, table):
+    rel = idx - blk * L
     hi = rel >> 7
-    lo = rel & 127
-    sub = iota((L, L), 0)
+    lo16 = (rel & 127).astype(F32).astype(BF16)
+    sub16 = iota((L, L), 0).astype(F32).astype(BF16)
     subw = iota((WIN, L), 0)
-    hot = jnp.concatenate(
-        [jnp.where(sub == lo[s : s + 1, :], 1.0, 0.0) for s in range(K)], axis=1
-    ).astype(BF16)
+    one = jnp.ones((), BF16)
+    zero = jnp.zeros((), BF16)
     masks = [subw == hi[s : s + 1, :] for s in range(K)]
-    source = jnp.concatenate([pos[j, pl.ds(step, WIN), :] for j in range(6)], axis=0)
-    found = nn(source.astype(BF16), hot)
-    own = [pos[c, pl.ds(step + 8, 1), :] + pos[3 + c, pl.ds(step + 8, 1), :] for c in range(3)]
+    source = jnp.concatenate([pos[j, pl.ds(blk, WIN), :] for j in range(6)], axis=0).astype(BF16)
+    own = [pos[c, pl.ds(blk + 8, 1), :] + pos[3 + c, pl.ds(blk + 8, 1), :] for c in range(3)]
     rates = rate_column()
-    live = iota((K, L), 0) < count_v[0]
-    offsets = []
-    bases = []
-    for s in range(K):
-        lanes = slice(s * L, (s + 1) * L)
-        d = []
-        for c in range(3):
-            both = found[c * WIN : (c + 1) * WIN, lanes] + found[(3 + c) * WIN : (4 + c) * WIN, lanes]
-            d.append(jnp.sum(jnp.where(masks[s], both, 0.0), axis=0, keepdims=True) - own[c])
-        q = d[0] * d[0] + d[1] * d[1] + d[2] * d[2]
-        basis = jnp.exp(-rates * q) * jnp.where(live[s : s + 1, :], 1.0, 0.0)
-        offsets.append(d)
-        bases.append(stack_basis(basis))
-    weight = w_rad[...]
-    rate_w = rate_column() * weight
-    weights = jnp.concatenate([stack_weight(weight), stack_weight(-rate_w)], axis=1)
-    radial = tn(jnp.concatenate(bases, axis=1).astype(BF16), weights.astype(BF16))
-    message = jnp.zeros((L, L), F32)
-    for s in range(K):
-        message += radial[s * L : (s + 1) * L, :L] * rows[s * L : (s + 1) * L, :]
+    live = iota((K, L), 0) < count
+    hots = {}
+    found = {}
+    offsets = {}
+    radial = {}
+
+    def find(p):
+        pieces = []
+        for s in (2 * p, 2 * p + 1):
+            pieces.append(jnp.where(sub16 == lo16[s : s + 1, :], one, zero))
+            fetch(16)
+        hots[p] = jnp.concatenate(pieces, axis=1)
+        found[p] = nn(source, hots[p])
+        fetch(64)
+
+    def spread_basis(p):
+        bases = []
+        for j in range(2):
+            s = 2 * p + j
+            lanes = slice(j * L, (j + 1) * L)
+            d = []
+            for c in range(3):
+                both = found[p][c * WIN : (c + 1) * WIN, lanes] + found[p][(3 + c) * WIN : (4 + c) * WIN, lanes]
+                d.append(jnp.sum(jnp.where(masks[s], both, 0.0), axis=0, keepdims=True) - own[c])
+            q = d[0] * d[0] + d[1] * d[1] + d[2] * d[2]
+            basis = jnp.exp(-rates * q) * jnp.where(live[s : s + 1, :], 1.0, 0.0)
+            offsets[s] = d
+            bases.append(stack_basis(basis))
+            fetch(16)
+        radial[p] = tn(jnp.concatenate(bases, axis=1).astype(BF16), weights)
+        fetch(64)
+
+    message = [jnp.zeros((L, L), F32)]
+
+    def add_message(p):
+        fetch(0, (2 * p + 2) * L)
+        for j in range(2):
+            s = 2 * p + j
+            message[0] += radial[p][j * L : (j + 1) * L, :L] * rows[s * L : (s + 1) * L, :]
+            fetch(16)
+
+    pairs = K // 2
+    for p in range(pairs + 2):
+        if p < pairs:
+            find(p)
+        if 0 <= p - 1 < pairs:
+            spread_basis(p - 1)
+        if 0 <= p - 2 < pairs:
+            add_message(p - 2)
     scale = 1.0 / math.sqrt(K)
-    own_rows = table[pl.ds(pl.multiple_of(G + step * L, L), L), :]
-    pre = dot3(nn, message * scale, w_mix[...]) + own_rows
+    own_rows = table[pl.ds(pl.multiple_of(G + blk * L, L), L), :]
+    pre = dot3(nn, message[0] * scale, w_mix[...]) + own_rows
+    fetch(32)
     sig = sigmoid(pre)
     up = w_out[...] * (sig * (1.0 + pre * (1.0 - sig)))
+    fetch(32)
     back = dot3(nt, up * scale, w_mix[...])
-    ones = jnp.ones((2 * L, L), BF16)
-    diag = sub == iota((L, L), 1)
+    fetch(32)
+    diag = iota((L, L), 0) == iota((L, L), 1)
     own_grad = [jnp.zeros((1, L), F32) for _ in range(3)]
-    parts = [[] for _ in range(6)]
-    for s in range(K):
-        prod = back * rows[s * L : (s + 1) * L, :] * radial[s * L : (s + 1) * L, L:]
-        prod_hi, prod_lo = split(prod)
-        total = nn(jnp.concatenate([prod_hi, prod_lo], axis=1).astype(BF16), ones)
-        slope = 2.0 * jnp.sum(jnp.where(diag, total, 0.0), axis=0, keepdims=True)
-        for c in range(3):
-            value = slope * offsets[s][c]
-            own_grad[c] -= value
-            v_hi, v_lo = split(value)
-            parts[c].append(jnp.where(masks[s], v_hi, 0.0))
-            parts[3 + c].append(jnp.where(masks[s], v_lo, 0.0))
-    spread = jnp.concatenate([jnp.concatenate(p, axis=1) for p in parts], axis=0).astype(BF16)
-    out = nt(spread, hot)
+    slopes = {}
+    total = [None]
+
+    def pull(p):
+        for j in range(2):
+            s = 2 * p + j
+            prod = back * rows[s * L : (s + 1) * L, :] * radial[p][j * L : (j + 1) * L, L:]
+            summed = jnp.sum(prod, axis=1, keepdims=True)
+            slopes[s] = 2.0 * jnp.sum(jnp.where(diag, summed, 0.0), axis=0, keepdims=True)
+            fetch(32)
+
+    def push(p):
+        parts = [[] for _ in range(6)]
+        for s in (2 * p, 2 * p + 1):
+            for c in range(3):
+                value = slopes[s] * offsets[s][c]
+                own_grad[c] -= value
+                v_hi, v_lo = split(value)
+                parts[c].append(jnp.where(masks[s], v_hi, 0.0))
+                parts[3 + c].append(jnp.where(masks[s], v_lo, 0.0))
+            fetch(16)
+        spread = jnp.concatenate([jnp.concatenate(x, axis=1) for x in parts], axis=0).astype(BF16)
+        got = nt(spread, hots[p])
+        total[0] = got if total[0] is None else total[0] + got
+        fetch(32)
+
+    for p in range(pairs + 1):
+        if p < pairs:
+            pull(p)
+        if p >= 1:
+            push(p - 1)
+    out = total[0]
     for c in range(3):
         both = out[c * WIN : (c + 1) * WIN] + out[(3 + c) * WIN : (4 + c) * WIN]
         both += jnp.where(subw == 8, own_grad[c], 0.0)
-        acc[c, pl.ds(step, WIN), :] += both
+        acc[c, pl.ds(blk, WIN), :] += both
+    fetch(K * L)
+
+
+def fetcher(table, idx, rows):
+    order = iter(range(K * L))
+
+    done = [0]
+
+    def fetch(n, upto=0):
+        for _ in range(max(n, upto - done[0])):
+            e = next(order, None)
+            if e is None:
+                return
+            done[0] += 1
+            rows[pl.ds(e, 1), :] = table[pl.ds(idx[0, e], 1), :]
+
+    return fetch
+
+
+def teacher_kernel(
+    idx_h, idx_v, count_v, feat, left, right, pos, w_rad, w_mix, w_out,
+    acc, table, rows_a, rows_b, idx_a, idx_b, sem_a, sem_b,
+):
+    blocks = idx_h.shape[0]
+    acc[...] = jnp.zeros_like(acc)
+
+    def flip(source, base):
+        def one(j, carry):
+            src = pl.ds(pl.multiple_of(j * L, L), L)
+            dst = pl.ds(pl.multiple_of(base + j * L, L), L)
+            table[dst, :] = source[:, src].T
+            return carry
+
+        lax.fori_loop(0, source.shape[1] // L, one, 0)
+
+    def bring(blk, idx, sem):
+        return pltpu.make_async_copy(idx_h.at[jnp.minimum(blk, blocks - 1)], idx, sem)
+
+    bring(0, idx_a, sem_a).start()
+    bring(1, idx_b, sem_b).start()
+    flip(left, 0)
+    flip(feat, G)
+    flip(right, G + feat.shape[1])
+    weight = w_rad[...]
+    rate_w = rate_column() * weight
+    weights = jnp.concatenate([stack_weight(weight), stack_weight(-rate_w)], axis=1).astype(BF16)
+
+    def step(i, carry):
+        for t, held, rows, idx, sem in ((0, rows_a, rows_a, idx_a, sem_a), (1, rows_b, rows_b, idx_b, sem_b)):
+            blk = 2 * i + t
+            bring(blk, idx, sem).wait()
+            lanes = pl.ds(pl.multiple_of(blk * L, L), L)
+            teacher_block(
+                blk, held, fetcher(table, idx, rows), idx_v[:, lanes], count_v[:, lanes],
+                pos, weights, w_mix, w_out, acc, table,
+            )
+
+            @pl.when(i < blocks // 2 - 1)
+            def _():
+                bring(blk + 2, idx, sem).start()
+
+        return carry
+
+    lax.fori_loop(0, blocks // 2, step, 0)
 
 
 def teacher(idx, count, feat, left, right, ext_pos, w_rad, w_mix, w_out):
     atoms = feat.shape[1]
-    steps = atoms // L
+    blocks = atoms // L
     ext_rows = (atoms + 2 * G) // L
     tall = ext_rows + 24
     pos = jnp.pad(ext_pos.reshape(3, ext_rows, L), ((0, 0), (0, 24), (0, 0)))
     hi = lax.reduce_precision(pos, 8, 7)
     pos = jnp.concatenate([hi, pos - hi], axis=0)
-    whole = lambda shape: pl.BlockSpec(shape, lambda i: (0,) * len(shape))
+    vmem = pl.BlockSpec(memory_space=pltpu.VMEM)
     return pl.pallas_call(
         teacher_kernel,
-        grid=(steps,),
-        in_specs=[
-            pl.BlockSpec((K, L), lambda i: (0, i), memory_space=pltpu.SMEM),
-            pl.BlockSpec((K, L), lambda i: (0, i)),
-            pl.BlockSpec((1, 1, L), lambda i: (i, 0, 0)),
-            whole(feat.shape),
-            whole(left.shape),
-            whole(right.shape),
-            whole(pos.shape),
-            whole((8, L)),
-            whole((L, L)),
-            whole((1, L)),
-        ],
-        out_specs=whole((3, tall, L)),
+        in_specs=[pl.BlockSpec(memory_space=pl.ANY)] + [vmem] * 9,
+        out_specs=vmem,
         out_shape=jax.ShapeDtypeStruct((3, tall, L), F32),
         scratch_shapes=[
             pltpu.VMEM((atoms + 2 * G, L), F32),
             pltpu.VMEM((K * L, L), F32),
+            pltpu.VMEM((K * L, L), F32),
+            pltpu.SMEM((1, K * L), jnp.int32),
+            pltpu.SMEM((1, K * L), jnp.int32),
+            pltpu.SemaphoreType.DMA,
+            pltpu.SemaphoreType.DMA,
         ],
         compiler_params=pltpu.CompilerParams(vmem_limit_bytes=52 * 2**20),
         cost_estimate=pl.CostEstimate(
@@ -199,9 +275,9 @@
         ),
         name="teacher",
     )(
+        idx.reshape(K, blocks, L).transpose(1, 0, 2).reshape(blocks, 1, K * L),
         idx,
-        idx,
-        count.reshape(steps, 1, L),
+        count.reshape(1, atoms),
         feat,
         left,
         right,
@@ -405,6 +481,135 @@
     )(recv, weight, pred, offs, basis, hid, slope)
 
 
+MESH = pl.DeviceIdType.MESH
+
+
+def exchange_kernel(src, dst, held, landed, send_sem, recv_sem, own_sem):
+    bricks = lax.axis_size("brick")
+    total = lax.axis_size("grp") * bricks
+    me = lax.axis_index("grp") * bricks + lax.axis_index("brick")
+    barrier = pltpu.get_barrier_semaphore()
+
+    def place(d):
+        t = lax.rem(me + d, total)
+        return t, (t // bricks, lax.rem(t, bricks))
+
+    def greet(d, carry):
+        pl.semaphore_signal(barrier, inc=1, device_id=place(d)[1], device_id_type=MESH)
+        return carry
+
+    lax.fori_loop(1, total, greet, 0)
+    held[:, 0, :] = src[:total]
+    held[:, 1, :] = src[total:]
+    own = pltpu.make_async_copy(held.at[me], landed.at[me], own_sem)
+    own.start()
+    pl.semaphore_wait(barrier, total - 1)
+
+    def send(d, carry):
+        t, where = place(d)
+        pltpu.make_async_remote_copy(
+            src_ref=held.at[t],
+            dst_ref=landed.at[me],
+            send_sem=send_sem,
+            recv_sem=recv_sem,
+            device_id=where,
+            device_id_type=MESH,
+        ).start()
+        return carry
+
+    lax.fori_loop(1, total, send, 0)
+    own.wait()
+    most = pl.ds(0, total - 1)
+    pltpu.make_async_copy(held.at[most], held.at[most], send_sem).wait()
+    pltpu.make_async_copy(landed.at[most], landed.at[most], recv_sem).wait()
+    dst[:total] = landed[:, 0, :]
+    dst[total:] = landed[:, 1, :]
+
+
+def exchange(rows):
+    total = rows.shape[0] // 2
+    vmem = pl.BlockSpec(memory_space=pltpu.VMEM)
+    return pl.pallas_call(
+        exchange_kernel,
+        in_specs=[vmem],
+        out_specs=vmem,
+        out_shape=jax.ShapeDtypeStruct(rows.shape, F32),
+        scratch_shapes=[
+            pltpu.VMEM((total, 2, L), F32),
+            pltpu.VMEM((total, 2, L), F32),
+            pltpu.SemaphoreType.DMA,
+            pltpu.SemaphoreType.DMA,
+            pltpu.SemaphoreType.DMA,
+        ],
+        compiler_params=pltpu.CompilerParams(collective_id=1, has_side_effects=True),
+        name="exchange",
+    )(rows)
+
+
+def reduce_kernel(x, out, first, second, third, send_sem, recv_sem):
+    g = lax.axis_index("grp")
+    b = lax.axis_index("brick")
+    groups = first.shape[0]
+    low = second.shape[0]
+    high = third.shape[0]
+    z = lax.rem(b, low)
+    h = b // low
+    stages = (
+        (first, groups, g, lambda d: (lax.rem(g + d, groups), b)),
+        (second, low, z, lambda d: (g, h * low + lax.rem(z + d, low))),
+        (third, high, h, lambda d: (g, lax.rem(h + d, high) * low + z)),
+    )
+    barrier = pltpu.get_barrier_semaphore()
+    partners = 0
+    for _, size, _, where in stages:
+        for d in range(1, size):
+            pl.semaphore_signal(barrier, inc=1, device_id=where(d), device_id_type=MESH)
+            partners += 1
+    pl.semaphore_wait(barrier, partners)
+    value = x[...]
+    used = 0
+    for slots, size, mine, where in stages:
+        slots[pl.ds(mine, 1)] = value[None]
+        copies = []
+        for d in range(1, size):
+            copy = pltpu.make_async_remote_copy(
+                src_ref=slots.at[mine],
+                dst_ref=slots.at[mine],
+                send_sem=send_sem.at[used],
+                recv_sem=recv_sem.at[used],
+                device_id=where(d),
+                device_id_type=MESH,
+            )
+            used += 1
+            copy.start()
+            copies.append(copy)
+        for copy in copies:
+            copy.wait()
+        value = slots[0]
+        for i in range(1, size):
+            value = value + slots[i]
+    out[...] = value
+
+
+def reduce_all(x):
+    groups = lax.axis_size("grp")
+    bricks = lax.axis_size("brick")
+    low = 4
+    high = bricks // low
+    count = groups + low + high - 3
+    vmem = pl.BlockSpec(memory_space=pltpu.VMEM)
+    return pl.pallas_call(
+        reduce_kernel,
+        in_specs=[vmem],
+        out_specs=vmem,
+        out_shape=jax.ShapeDtypeStruct(x.shape, F32),
+        scratch_shapes=[pltpu.VMEM((n,) + x.shape, F32) for n in (groups, low, high)]
+        + [pltpu.SemaphoreType.DMA((count,)), pltpu.SemaphoreType.DMA((count,))],
+        compiler_params=pltpu.CompilerParams(collective_id=2, has_side_effects=True),
+        name="reduce",
+    )(x)
+
+
 def halo(cells, width):
     count = lax.axis_size(AXES)
     up = [(i, i + 1) for i in range(count - 1)]
@@ -453,7 +658,7 @@
     block_atoms = atoms // blocks
     order = jnp.arange(blocks, dtype=jnp.int32)
     same = (block_owner[:, None] == block_owner[None, :]) & (order[None, :] < order[:, None])
-    dest = 2 * block_owner + jnp.sum(same.astype(jnp.int32), axis=1)
+    dest = block_owner + devices * jnp.sum(same.astype(jnp.int32), axis=1)
     spread = lambda v: jnp.broadcast_to(v[:, None], (blocks, block_atoms)).reshape(1, atoms)
     acc = teacher(
         teacher_nbr.T, nbr_count, features, left, right, ext_pos, w_rad, w_mix, w_out
@@ -467,11 +672,11 @@
     outgoing = mapping(
         force, atom_bead.reshape(1, atoms), spread(dest), spread(block_start.astype(F32))
     )
-    recv = lax.all_to_all(outgoing, AXES, split_axis=0, concat_axis=0, tiled=True)
+    recv = exchange(outgoing)
     bead_force, sums = bead_stage(
         recv, bead_weight.reshape(1, beads), pred, offs, basis, hid, slope, beads * devices
     )
-    sums = lax.psum(sums, AXES)
+    sums = reduce_all(sums)
     return force, bead_force, pred, sums[:8], sums[8], jnp.sum(sums[9])
 
 

time: 487 us -> 277 us (0.57)
  Pallas kernels: 342 us -> 231 us
  blocking collectives: 65.7 us -> 0 us
  starting transfers between devices: 46.1 us -> 19.5 us
  waiting for transfers between devices: 8.05 us -> 0.02 us
    pallas_call x1 -> x3, Pallas kernels: 328 us -> 218 us  [the longest x1 160 us: teacher(): pl.pallas_call(teacher_kernel, in_specs=[pl.BlockSpec(memory_space=pl.ANY...]
    psum x1 -> x0, blocking collectives: 65.7 us -> none  [local(): sums = lax.psum(sums, AXES)]
    all_to_all x1 -> x0, starting transfers between devices: 27.3 us -> none  [local(): lax.all_to_all(outgoing, AXES, split_axis=0, concat_axis=0, tiled=True)]
    unnamed x39 -> x38, local copies, waits for them, and re-layouts: 13.9 us -> 11.8 us
  transfers between devices with their start and end apart: 7 -> 6, of which waited for: 3 -> 0; matrix products, arithmetic and copies ran while one was open for 1% -> 3% of each run, Pallas kernels for 1% -> 1%
where the time goes in v2:
time: 277 us; the launch traced here: 276 us
  Pallas kernels  231 us (83%)
  starting transfers between devices  19.5 us (7%)
  local copies, waits for them, and re-layouts  19 us (7%)
  other arithmetic  5.03 us (2%)
    pallas_call x1, Pallas kernels, teacher(): pl.pallas_call(teacher_kernel, in_specs=[pl.BlockSpec(memory_space=pl.ANY...  160 us
    pallas_call x1, Pallas kernels, exchange(): pl.pallas_call(exchange_kernel, in_specs=[vmem], out_specs=vmem, out_shap...  41.6 us
    pallas_call x1, Pallas kernels, reduce_all(): pl.pallas_call(reduce_kernel, in_specs=[vmem], out_specs=vmem, out_shape=...  15.6 us
    unnamed x38, local copies, waits for them, and re-layouts  11.8 us
    ppermute x1, starting transfers between devices, local(): below = lax.ppermute(grads[:, atoms + G:], AXES, up)  6.4 us
  transfers between devices with their start and end apart: 6, of which 0 were waited for; matrix products, arithmetic and copies ran while one was open for 3% of the time, Pallas kernels for 1%

profile of v2, /device:TPU:0, one launch (start us, length us, event | category | flops | bytes accessed | tf_op | source)
XLA Modules:
  0.0 275.9 jit_solution(11770208507675986777)
XLA Ops:
  0.7 0.8 fusion.6
  2.3 1.4 collective-permute-start.3
  3.7 4.5 %collective-permute-start.2 = (f32[3,1056]{1,0:T(4,128)S(1)}, f32[3,1056]{1,0:T(4,128)S(1)}, u32[]{:S(2)}, u32[]{:S(2)}) collective-permute-start(f32[3,1056]{1,0:T(4,128)S(1)} %pad_maximum_fusion.1), channel_id=1, source_target_pairs={{0,1},{1,2},{2,3},{3,4},{4,5},{5,6},{6,7},{7,8},{8,9},{9,10},{10,1... | collective-permute-start | bytes 38024 | tf_op jit(solution)/shard_map/ppermute | solution.py:648
  8.3 1.3 fusion.3
  9.5 1.3 collective-permute-start.1
  10.8 4.6 %collective-permute-start = (f32[128,1024]{1,0:T(8,128)S(1)}, f32[128,1024]{1,0:T(8,128)S(1)}, u32[]{:S(2)}, u32[]{:S(2)}) collective-permute-start(f32[128,1024]{1,0:T(8,128)S(1)} %get-tuple-element.21), channel_id=1, source_target_pairs={{0,1},{1,2},{2,3},{3,4},{4,5},{5,6},{6,7},{7,8},{8,9},{9,10},{10,1... | collective-permute-start | bytes 1572872 | tf_op jit(solution)/shard_map/ppermute | solution.py:617
  15.4 0.9 convert_reduce_fusion
  17.7 0.8 copy.28.w_second
  20.1 1.1 copy.29
  22.4 160.4 %teacher.1 = f32[3,104,128]{2,1,0:T(8,128)S(1)} custom-call(s32[64,1,1536]{2,1,0:T(1,128)S(1)} %reshape.64.idx_h, s32[12,8192]{1,0:T(8,128)S(1)} %bitcast.26, s32[1,8192]{1,0:T(1,128)S(1)} %bitcast.28, f32[128,8192]{1,0:T(8,128)} %feat.1, f32[128,1024]{1,0:T(8,128)S(1)} %collective-permute-done.left, f32[128,1024]{1,0:T(8,128)} %collective-permute-done.1.right, ...), custom_call_target="tpu_custom_call" | custom-call | flops 20000000000 | bytes 8388608 | tf_op jit(solution)/shard_map/teacher/pallas_call | solution.py:258
  182.9 6.4 %collective-permute-start.4 = (f32[3,1024]{1,0:T(4,128)S(1)}, f32[3,1024]{1,0:T(4,128)S(1)}, u32[]{:S(2)}, u32[]{:S(2)}) collective-permute-start(f32[3,1024]{1,0:T(4,128)S(1)} %get-tuple-element.22), channel_id=1, source_target_pairs={{0,1},{1,2},{2,3},{3,4},{4,5},{5,6},{6,7},{7,8},{8,9},{9,10},{10,1... | collective-permute-start | bytes 36872 | tf_op jit(solution)/shard_map/ppermute | solution.py:669
  189.3 1.3 collective-permute-start.5
  190.7 4.1 %student.1 = (f32[3,512]{1,0:T(4,128)}, f32[3,16,512]{2,1,0:T(8,128)S(1)}, f32[8,8192]{1,0:T(8,128)S(1)}, f32[128,8192]{1,0:T(8,128)S(1)}, f32[128,8192]{1,0:T(8,128)S(1)}) custom-call(s32[16,512]{1,0:T(8,128)S(1)} %bitcast.29, f32[3,5,128]{2,1,0:T(8,128)S(1)} %reshape.62.pos, f32[8,128]{1,0:T(8,128)S(1)} %copy-done.13, f32[128,1]{1,0:T(8,128)S(1)} %copy.28.w_second), custom_call_target="tpu_custom_call" | custom-call | flops 1000000000 | bytes 8388608 | tf_op jit(solution)/shard_map/student/pallas_call | solution.py:342
  194.7 1.9 copy-done
  196.7 2.0 copy-done.2
  199.4 5.3 %mapping.1.src = f32[256,128]{1,0:T(8,128)} custom-call(f32[3,8192]{1,0:T(4,128)} %fusion.2.force, s32[1,8192]{1,0:T(1,128)} %bitcast.36, s32[1,8192]{1,0:T(1,128)} %reshape.59.dest, f32[1,8192]{1,0:T(1,128)} %reshape.60.start), custom_call_target="tpu_custom_call" | custom-call | tf_op jit(solution)/shard_map/mapping/pallas_call | solution.py:404
  204.7 41.6 %exchange.1.recv = f32[256,128]{1,0:T(8,128)} custom-call(f32[256,128]{1,0:T(8,128)} %mapping.1.src), custom_call_target="tpu_custom_call" | custom-call | tf_op jit(solution)/shard_map/exchange/pallas_call | solution.py:532
  246.4 2.2 copy-done.1
  248.6 2.2 copy-done.3
  250.8 0.9 copy-done.4
  252.4 4.2 %beads.1 = (f32[3,512]{1,0:T(4,128)}, f32[16,128]{1,0:T(8,128)S(1)}) custom-call(f32[256,128]{1,0:T(8,128)S(1)} %copy-done.4, f32[1,512]{1,0:T(1,128)S(1)} %bitcast.27, f32[3,512]{1,0:T(4,128)S(1)} %copy-done.7, f32[3,16,512]{2,1,0:T(8,128)S(1)} %get-tuple-element.14.offs, f32[8,8192]{1,0:T(8,128)S(1)} %get-tuple-element.15.basis, ...), custom_call_target="tpu_custom_call" | custom-call | tf_op jit(solution)/shard_map/beads/pallas_call | solution.py:462
  257.1 15.6 %reduce.2 = f32[16,128]{1,0:T(8,128)} custom-call(f32[16,128]{1,0:T(8,128)} %copy-done.6), custom_call_target="tpu_custom_call" | custom-call | tf_op jit(solution)/shard_map/reduce/pallas_call | solution.py:601
  272.8 1.9 slice_reduce_fusion
  274.6 1.3 slice.65
  (63 shorter events, 6.8 us)
Async XLA Ops:
  0.6 21.4 %copy-start.16 = (f32[3,512]{1,0:T(4,128)S(1)}, f32[3,512]{1,0:T(4,128)}, u32[]{:S(2)}) copy-start(f32[3,512]{1,0:T(4,128)} %param.25) | copy-start | bytes 18436
  0.6 21.5 %copy-start.15 = (f32[3,8192]{1,0:T(4,128)S(1)}, f32[3,8192]{1,0:T(4,128)}, u32[]{:S(2)}) copy-start(f32[3,8192]{1,0:T(4,128)} %param.15) | copy-start | bytes 294916
  2.2 20.1 %copy-start.5 = (s32[8192,12]{0,1:T(8,128)S(1)}, s32[8192,12]{0,1:T(8,128)}, u32[]{:S(2)}) copy-start(s32[8192,12]{0,1:T(8,128)} %param.17) | copy-start | bytes 1179652
  2.2 20.1 %copy-start.9 = (f32[128,128]{1,0:T(8,128)S(1)}, f32[128,128]{1,0:T(8,128)}, u32[]{:S(2)}) copy-start(f32[128,128]{1,0:T(8,128)} %w_mix.1) | copy-start | bytes 196612
  2.2 20.1 %copy-start.10 = (s32[8192]{0:T(1024)S(1)}, s32[8192]{0:T(1024)}, u32[]{:S(2)}) copy-start(s32[8192]{0:T(1024)} %param.18) | copy-start | bytes 98308
  2.2 20.1 %copy-start.12 = (f32[8,128]{1,0:T(8,128)S(1)}, f32[8,128]{1,0:T(8,128)}, u32[]{:S(2)}) copy-start(f32[8,128]{1,0:T(8,128)} %w_rad.1) | copy-start | bytes 12292
  2.2 20.1 %copy-start.14 = (f32[128]{0:T(128)S(1)}, f32[128]{0:T(128)}, u32[]{:S(2)}) copy-start(f32[128]{0:T(128)} %param.21) | copy-start | bytes 1540
  2.3 19.8 %collective-permute-start.3 = (f32[3,1056]{1,0:T(4,128)S(1)}, f32[3,1056]{1,0:T(4,128)S(1)}, u32[]{:S(2)}, u32[]{:S(2)}) collective-permute-start(f32[3,1056]{1,0:T(4,128)S(1)} %pad_maximum_fusion.2), channel_id=1, source_target_pairs={{1,0},{2,1},{3,2},{4,3},{5,4},{6,5},{7,6},{8,7},{9,8},{10,9},{11,1... | collective-permute-start | bytes 38024 | tf_op jit(solution)/shard_map/ppermute | solution.py:649
  3.7 18.3 %collective-permute-start.2 = (f32[3,1056]{1,0:T(4,128)S(1)}, f32[3,1056]{1,0:T(4,128)S(1)}, u32[]{:S(2)}, u32[]{:S(2)}) collective-permute-start(f32[3,1056]{1,0:T(4,128)S(1)} %pad_maximum_fusion.1), channel_id=1, source_target_pairs={{0,1},{1,2},{2,3},{3,4},{4,5},{5,6},{6,7},{7,8},{8,9},{9,10},{10,1... | collective-permute-start | bytes 38024 | tf_op jit(solution)/shard_map/ppermute | solution.py:648
  9.5 12.8 %collective-permute-start.1 = (f32[128,1024]{1,0:T(8,128)S(1)}, f32[128,1024]{1,0:T(8,128)}, u32[]{:S(2)}, u32[]{:S(2)}) collective-permute-start(f32[128,1024]{1,0:T(8,128)S(1)} %get-tuple-element.20), channel_id=1, source_target_pairs={{1,0},{2,1},{3,2},{4,3},{5,4},{6,5},{7,6},{8,7},{9,8},{10,9},{11,1... | collective-permute-start | bytes 1572872 | tf_op jit(solution)/shard_map/ppermute | solution.py:618
  10.8 11.5 %collective-permute-start = (f32[128,1024]{1,0:T(8,128)S(1)}, f32[128,1024]{1,0:T(8,128)S(1)}, u32[]{:S(2)}, u32[]{:S(2)}) collective-permute-start(f32[128,1024]{1,0:T(8,128)S(1)} %get-tuple-element.21), channel_id=1, source_target_pairs={{0,1},{1,2},{2,3},{3,4},{4,5},{5,6},{6,7},{7,8},{8,9},{9,10},{10,1... | collective-permute-start | bytes 1572872 | tf_op jit(solution)/shard_map/ppermute | solution.py:617
  22.4 168.3 %copy-start.11 = (s32[512,16]{0,1:T(8,128)S(1)}, s32[512,16]{0,1:T(8,128)}, u32[]{:S(2)}) copy-start(s32[512,16]{0,1:T(8,128)} %param.26) | copy-start | bytes 98308
  22.4 168.3 %copy-start.13 = (f32[8,128]{1,0:T(8,128)S(1)}, f32[8,128]{1,0:T(8,128)}, u32[]{:S(2)}) copy-start(f32[8,128]{1,0:T(8,128)} %w_first.1) | copy-start | bytes 12292
  182.8 63.6 %copy-start.8 = (f32[512]{0:T(512)S(1)}, f32[512]{0:T(512)}, u32[]{:S(2)}) copy-start(f32[512]{0:T(512)} %param.27) | copy-start | bytes 6148
  182.9 15.8 %collective-permute-start.4 = (f32[3,1024]{1,0:T(4,128)S(1)}, f32[3,1024]{1,0:T(4,128)S(1)}, u32[]{:S(2)}, u32[]{:S(2)}) collective-permute-start(f32[3,1024]{1,0:T(4,128)S(1)} %get-tuple-element.22), channel_id=1, source_target_pairs={{0,1},{1,2},{2,3},{3,4},{4,5},{5,6},{6,7},{7,8},{8,9},{9,10},{10,1... | collective-permute-start | bytes 36872 | tf_op jit(solution)/shard_map/ppermute | solution.py:669
  189.3 9.4 %collective-permute-start.5 = (f32[3,1024]{1,0:T(4,128)S(1)}, f32[3,1024]{1,0:T(4,128)S(1)}, u32[]{:S(2)}, u32[]{:S(2)}) collective-permute-start(f32[3,1024]{1,0:T(4,128)S(1)} %get-tuple-element.23), channel_id=1, source_target_pairs={{1,0},{2,1},{3,2},{4,3},{5,4},{6,5},{7,6},{8,7},{9,8},{10,9},{11,1... | collective-permute-start | bytes 36872 | tf_op jit(solution)/shard_map/ppermute | solution.py:668
  194.7 1.9 copy-start
  196.7 2.0 copy-start.2
  246.4 2.2 copy-start.1
  248.6 2.2 copy-start.3
  250.8 0.9 copy-start.4
  251.7 0.7 copy-start.7
  256.5 0.6 copy-start.6

commit v3 on v2

v3 whole, which is shorter than its diff:
```python
import functools
import math

import jax
import jax.numpy as jnp
from jax import lax
from jax.experimental import pallas as pl
from jax.experimental.pallas import tpu as pltpu
from jax.sharding import PartitionSpec as P

G = 1024
BPB = 32
BW = 32
K = 12
L = 128
WIN = 24
AXES = ("grp", "brick")
F32 = jnp.float32
BF16 = jnp.bfloat16
RATES = tuple(0.05 * 1.6**b for b in range(8))


def iota(shape, dim):
    return lax.broadcasted_iota(jnp.int32, shape, dim)


def split(x):
    hi = x.astype(BF16).astype(F32)
    return hi, x - hi


def nn(a, b):
    return lax.dot_general(a, b, (((1,), (0,)), ((), ())), preferred_element_type=F32)


def nt(a, b):
    return lax.dot_general(a, b, (((1,), (1,)), ((), ())), preferred_element_type=F32)


def tn(a, b):
    return lax.dot_general(a, b, (((0,), (0,)), ((), ())), preferred_element_type=F32)


def dot3(dot, a, b):
    a_hi, a_lo = (t.astype(BF16) for t in split(a))
    b_hi, b_lo = (t.astype(BF16) for t in split(b))
    return dot(a_hi, b_hi) + dot(a_lo, b_hi) + dot(a_hi, b_lo)


def sigmoid(v):
    return 1.0 / (1.0 + jnp.exp(-v))


def rate_column():
    rows = iota((8, L), 0)
    out = jnp.zeros((8, L), F32)
    for b, rate in enumerate(RATES):
        out = jnp.where(rows == b, rate, out)
    return out


def stack_basis(basis):
    hi, lo = split(basis)
    return jnp.concatenate([hi, lo, hi, jnp.zeros_like(hi)], axis=0)


def stack_weight(weight):
    hi, lo = split(weight)
    return jnp.concatenate([hi, hi, lo, jnp.zeros_like(hi)], axis=0)


PAIR = 2 * L


def forward_part(blk, held, idx_s, idx, count, pos, weights, table):
    rows, slope_w, hots, offs, sent = held
    rel = idx - blk * L
    hi = rel >> 7
    lo16 = (rel & 127).astype(F32).astype(BF16)
    sub16 = iota((L, L), 0).astype(F32).astype(BF16)
    subw = iota((WIN, L), 0)
    one = jnp.ones((), BF16)
    zero = jnp.zeros((), BF16)
    source = jnp.concatenate([pos[j, pl.ds(blk, WIN), :] for j in range(6)], axis=0).astype(BF16)
    own = [pos[c, pl.ds(blk + 8, 1), :] + pos[3 + c, pl.ds(blk + 8, 1), :] for c in range(3)]
    rates = rate_column()
    live = iota((K, L), 0) < count
    found = {}
    radial = {}
    order = iter(range(K * L))
    done = [0]

    def fetch(n, upto=0):
        for _ in range(max(n, upto - done[0])):
            e = next(order, None)
            if e is None:
                return
            done[0] += 1
            rows[pl.ds(e, 1), :] = table[pl.ds(idx_s[0, e], 1), :]

    message = jnp.zeros((L, L), F32)
    pairs = K // 2
    for p in range(pairs + 2):
        if p < pairs:
            pieces = []
            for s in (2 * p, 2 * p + 1):
                pieces.append(jnp.where(sub16 == lo16[s : s + 1, :], one, zero))
                fetch(FETCH)
            hot = jnp.concatenate(pieces, axis=1)
            hots[:, p * PAIR : (p + 1) * PAIR] = hot
            found[p] = nn(source, hot)
            fetch(FETCH)
            yield
        if 0 <= p - 1 < pairs:
            r = p - 1
            bases = []
            for j in range(2):
                s = 2 * r + j
                lanes = slice(j * L, (j + 1) * L)
                mask = subw == hi[s : s + 1, :]
                d = []
                for c in range(3):
                    both = found[r][c * WIN : (c + 1) * WIN, lanes] + found[r][(3 + c) * WIN : (4 + c) * WIN, lanes]
                    d.append(jnp.sum(jnp.where(mask, both, 0.0), axis=0, keepdims=True) - own[c])
                    offs[pl.ds(c * 16 + s, 1), :] = d[c]
                q = d[0] * d[0] + d[1] * d[1] + d[2] * d[2]
                basis = jnp.exp(-rates * q) * jnp.where(live[s : s + 1, :], 1.0, 0.0)
                bases.append(stack_basis(basis))
                fetch(FETCH)
                yield
            both = tn(jnp.concatenate(bases, axis=1).astype(BF16), weights)
            radial[r] = both[:, :L]
            slope_w[r * PAIR : (r + 1) * PAIR, :] = both[:, L:]
            fetch(FETCH)
            yield
        if 0 <= p - 2 < pairs:
            r = p - 2
            fetch(0, (2 * r + 2) * L)
            for j in range(2):
                s = 2 * r + j
                message += radial[r][j * L : (j + 1) * L] * rows[s * L : (s + 1) * L, :]
            yield
    sent[...] = message


def backward_part(blk, held, idx, mix, w_out, acc, table):
    rows, slope_w, hots, offs, sent = held
    hi = (idx - blk * L) >> 7
    subw = iota((WIN, L), 0)
    mix_hh, mix_l, turn_hh, turn_l = mix
    scale = 1.0 / math.sqrt(K)

    def product(x, w_hh, w_l):
        x_hi, x_lo = split(x)
        wide = jnp.concatenate([x_hi, x_lo], axis=1).astype(BF16)
        return nn(wide, w_hh) + nn(wide[:, :L], w_l)

    own_rows = table[pl.ds(pl.multiple_of(G + blk * L, L), L), :]
    mixed = product(sent[...] * scale, mix_hh, mix_l)
    yield
    pre = mixed + own_rows
    sig = sigmoid(pre)
    up = w_out[...] * (sig * (1.0 + pre * (1.0 - sig)))
    yield
    back = product(up * scale, turn_hh, turn_l)
    yield
    diag = iota((L, L), 0) == iota((L, L), 1)
    own_grad = [jnp.zeros((1, L), F32) for _ in range(3)]
    slopes = {}
    out = None
    pairs = K // 2
    for p in range(pairs + 1):
        if p < pairs:
            for j in range(2):
                s = 2 * p + j
                prod = back * rows[s * L : (s + 1) * L, :] * slope_w[s * L : (s + 1) * L, :]
                summed = jnp.sum(prod, axis=1, keepdims=True)
                slopes[s] = 2.0 * jnp.sum(jnp.where(diag, summed, 0.0), axis=0, keepdims=True)
                yield
        if p >= 1:
            r = p - 1
            parts = [[] for _ in range(6)]
            for s in (2 * r, 2 * r + 1):
                mask = subw == hi[s : s + 1, :]
                for c in range(3):
                    value = slopes[s] * offs[pl.ds(c * 16 + s, 1), :]
                    own_grad[c] -= value
                    v_hi, v_lo = split(value)
                    parts[c].append(jnp.where(mask, v_hi, 0.0))
                    parts[3 + c].append(jnp.where(mask, v_lo, 0.0))
            spread = jnp.concatenate([jnp.concatenate(x, axis=1) for x in parts], axis=0).astype(BF16)
            yield
            got = nt(spread, hots[:, r * PAIR : (r + 1) * PAIR])
            out = got if out is None else out + got
            yield
    for c in range(3):
        both = out[c * WIN : (c + 1) * WIN] + out[(3 + c) * WIN : (4 + c) * WIN]
        both += jnp.where(subw == 8, own_grad[c], 0.0)
        acc[c, pl.ds(blk, WIN), :] += both


FETCH = 40


def run_beside(one, two):
    alive = [one, two]
    while alive:
        for part in list(alive):
            if next(part, 1) == 1:
                alive.remove(part)


def teacher_kernel(
    idx_h, idx_v, count_v, feat, left, right, pos, w_rad, w_mix, w_out,
    acc, table, idx_a, idx_b, sem_a, sem_b, *held,
):
    blocks = idx_h.shape[0]
    acc[...] = jnp.zeros_like(acc)
    held_a, held_b = held[:5], held[5:]

    def flip(source, base):
        def one(j, carry):
            src = pl.ds(pl.multiple_of(j * L, L), L)
            dst = pl.ds(pl.multiple_of(base + j * L, L), L)
            table[dst, :] = source[:L, src].T
            return carry

        lax.fori_loop(0, source.shape[1] // L, one, 0)

    def bring(blk, idx, sem):
        return pltpu.make_async_copy(idx_h.at[jnp.minimum(blk, blocks - 1)], idx, sem)

    bring(0, idx_a, sem_a).start()
    bring(1, idx_b, sem_b).start()
    flip(left, 0)
    flip(feat, G)
    flip(right, G + feat.shape[1])
    weight = w_rad[...]
    rate_w = rate_column() * weight
    weights = jnp.concatenate([stack_weight(weight), stack_weight(-rate_w)], axis=1).astype(BF16)
    mix = []
    for w in (w_mix[...], w_mix[...].T):
        w_hi, w_lo = split(w)
        mix += [jnp.concatenate([w_hi, w_hi], axis=0).astype(BF16), w_lo.astype(BF16)]

    def forward(blk, held, idx_s):
        lanes = pl.ds(pl.multiple_of(blk * L, L), L)
        return forward_part(blk, held, idx_s, idx_v[:, lanes], count_v[:, lanes], pos, weights, table)

    def backward(blk, held):
        lanes = pl.ds(pl.multiple_of(blk * L, L), L)
        return backward_part(blk, held, idx_v[:, lanes], mix, w_out, acc, table)

    bring(0, idx_a, sem_a).wait()
    for _ in forward(0, held_a, idx_a):
        pass
    bring(2, idx_a, sem_a).start()

    def step(i, carry):
        for t, old, new, idx, sem in ((0, held_a, held_b, idx_b, sem_b), (1, held_b, held_a, idx_a, sem_a)):
            blk = 2 * i + t
            bring(blk + 1, idx, sem).wait()
            run_beside(backward(blk, old), forward(jnp.minimum(blk + 1, blocks - 1), new, idx))

            @pl.when(i < blocks // 2 - 1)
            def _():
                bring(blk + 3, idx, sem).start()

        return carry

    lax.fori_loop(0, blocks // 2, step, 0)


def teacher(idx, count, feat, left, right, ext_pos, w_rad, w_mix, w_out):
    atoms = feat.shape[1]
    blocks = atoms // L
    ext_rows = (atoms + 2 * G) // L
    tall = ext_rows + 24
    pos = jnp.pad(ext_pos.reshape(3, ext_rows, L), ((0, 0), (0, 24), (0, 0)))
    hi = lax.reduce_precision(pos, 8, 7)
    pos = jnp.concatenate([hi, pos - hi], axis=0)
    vmem = pl.BlockSpec(memory_space=pltpu.VMEM)
    return pl.pallas_call(
        teacher_kernel,
        in_specs=[pl.BlockSpec(memory_space=pl.ANY)] + [vmem] * 9,
        out_specs=vmem,
        out_shape=jax.ShapeDtypeStruct((3, tall, L), F32),
        scratch_shapes=[
            pltpu.VMEM((atoms + 2 * G, L), F32),
            pltpu.SMEM((1, K * L), jnp.int32),
            pltpu.SMEM((1, K * L), jnp.int32),
            pltpu.SemaphoreType.DMA,
            pltpu.SemaphoreType.DMA,
        ]
        + 2
        * [
            pltpu.VMEM((K * L, L), F32),
            pltpu.VMEM((K * L, L), F32),
            pltpu.VMEM((L, K * L), BF16),
            pltpu.VMEM((48, L), F32),
            pltpu.VMEM((L, L), F32),
        ],
        compiler_params=pltpu.CompilerParams(vmem_limit_bytes=52 * 2**20),
        cost_estimate=pl.CostEstimate(
            flops=2 * 10**10, bytes_accessed=8 * 2**20, transcendentals=10**6
        ),
        name="teacher",
    )(
        idx.reshape(K, blocks, L).transpose(1, 0, 2).reshape(blocks, 1, K * L),
        idx,
        count.reshape(1, atoms),
        feat,
        left,
        right,
        pos,
        w_rad,
        w_mix,
        w_out.reshape(1, L),
    )


KB = 16


def student_terms(offs, w_first, w2):
    q = offs[0] * offs[0] + offs[1] * offs[1] + offs[2] * offs[2]
    rates = rate_column()
    basis = [jnp.exp(-rates * q[s : s + 1, :]) for s in range(KB)]
    stacked = jnp.concatenate([stack_basis(b) for b in basis], axis=1).astype(BF16)
    z = tn(stack_weight(w_first).astype(BF16), stacked)
    return basis, z


def student_kernel(nbr, pos, w_first, w_second, force, off_out):
    step = pl.program_id(0)
    rel = nbr[...] - step * L
    hi = rel >> 7
    lo = rel & 127
    lane = iota((1, L), 1)
    near = []
    own = []
    for c in range(3):
        first = pos[c, pl.ds(step, 1), :]
        second = pos[c, pl.ds(step + 1, 1), :]
        take = lambda row: jnp.take_along_axis(
            jnp.broadcast_to(row, (KB, L)), lo, axis=1, mode="promise_in_bounds"
        )
        near.append(jnp.where(hi == 0, take(first), take(second)))
        own.append(
            jnp.where(lane < L - BW, pltpu.roll(first, L - BW, 1), pltpu.roll(second, L - BW, 1))
        )
    offs = [near[c] - own[c] for c in range(3)]
    w2 = w_second[...]
    basis, z = student_terms(offs, w_first[...], w2)
    out = [jnp.zeros((1, L), F32) for _ in range(3)]
    for s in range(KB):
        zs = z[:, s * L : (s + 1) * L]
        strength = jnp.sum(w2 * (zs * sigmoid(zs)), axis=0, keepdims=True)
        for c in range(3):
            out[c] += strength * offs[c][s : s + 1, :]
    for c in range(3):
        off_out[c] = offs[c]
        force[pl.ds(c, 1), :] = out[c]


def student(nbr, pos, w_first, w_second):
    beads = nbr.shape[1]
    whole = lambda shape: pl.BlockSpec(shape, lambda i: (0,) * len(shape))
    return pl.pallas_call(
        student_kernel,
        grid=(beads // L,),
        in_specs=[
            pl.BlockSpec((KB, L), lambda i: (0, i)),
            whole(pos.shape),
            whole((8, L)),
            whole((L, 1)),
        ],
        out_specs=[
            pl.BlockSpec((3, L), lambda i: (0, i)),
            pl.BlockSpec((3, KB, L), lambda i: (0, 0, i)),
        ],
        out_shape=[
            jax.ShapeDtypeStruct((3, beads), F32),
            jax.ShapeDtypeStruct((3, KB, beads), F32),
        ],
        compiler_params=pltpu.CompilerParams(vmem_limit_bytes=40 * 2**20),
        cost_estimate=pl.CostEstimate(
            flops=10**9, bytes_accessed=10**6, transcendentals=10**6
        ),
        name="student",
    )(nbr, pos, w_first, w_second)


CHUNK = 1024


def mapping_kernel(force, bead, dest, start, out):
    step = pl.program_id(0)

    @pl.when(step == 0)
    def _():
        out[...] = jnp.zeros_like(out)

    b = bead[...]
    hot = iota((BPB, CHUNK), 0) == b
    highs = []
    lows = []
    for c in range(3):
        hi, lo = split(force[pl.ds(c, 1), :])
        highs.append(jnp.where(hot, hi, 0.0))
        lows.append(jnp.where(hot, lo, 0.0))
    hi, lo = split(start[...])
    first = (iota((BPB, CHUNK), 0) == 0) & (iota((BPB, CHUNK), 1) % 32 == 0)
    highs.append(jnp.where(first, hi, 0.0))
    lows.append(jnp.where(first, lo, 0.0))
    values = jnp.concatenate(highs + lows, axis=0).astype(BF16)
    place = jnp.where(iota((2 * L, CHUNK), 0) == dest[...], 1.0, 0.0).astype(BF16)
    got = nt(place, values)
    out[...] += got[:, :L] + got[:, L:]


def mapping(force, bead, dest, start):
    atoms = force.shape[1]
    row = lambda n: pl.BlockSpec((n, CHUNK), lambda i: (0, i))
    return pl.pallas_call(
        mapping_kernel,
        grid=(atoms // CHUNK,),
        in_specs=[row(3), row(1), row(1), row(1)],
        out_specs=pl.BlockSpec((2 * L, L), lambda i: (0, 0)),
        out_shape=jax.ShapeDtypeStruct((2 * L, L), F32),
        name="mapping",
    )(force, bead, dest, start)


def bead_kernel(beads_all, recv, weight, pred, offs, w_first, w_second, force, out):
    step = pl.program_id(0)
    beads = force.shape[1]

    @pl.when(step == 0)
    def _():
        out[...] = jnp.zeros_like(out)
        turned = jnp.concatenate([recv[:L, :].T, recv[L:, :].T], axis=1)
        start = (turned[96:97, :] + 0.5).astype(jnp.int32)
        hot = jnp.where(iota((beads, 2 * L), 0) == start, 1.0, 0.0).astype(BF16)
        hi, lo = split(turned[:96, :])
        got = nt(jnp.concatenate([hi, lo], axis=0).astype(BF16), hot)
        for c in range(3):
            rows = got[c * BPB : (c + 1) * BPB] + got[96 + c * BPB : 96 + (c + 1) * BPB]
            rows = pltpu.roll(rows, 0, 1, stride=1, stride_axis=0)
            force[pl.ds(c, 1), :] = jnp.sum(rows, axis=0, keepdims=True)

    lanes = pl.ds(pl.multiple_of(step * L, L), L)
    w = weight[...]
    loss = jnp.zeros((1, L), F32)
    pull = []
    for c in range(3):
        res = pred[pl.ds(c, 1), :] - force[pl.ds(c, 1), lanes]
        loss += w * (res * res)
        pull.append((2.0 / (3.0 * beads_all)) * w * res)
    ds = sum(offs[c] * pull[c] for c in range(3))
    rows = jnp.concatenate([ds[s : s + 1, :] for s in range(KB)], axis=1)
    rows_hi, rows_lo = split(rows)
    zeros = jnp.zeros((6, rows.shape[1]), F32)
    second_in = jnp.concatenate([rows_hi, rows_lo, zeros], axis=0).astype(BF16)
    w2 = w_second[...]
    basis, z = student_terms([offs[c] for c in range(3)], w_first[...], w2)
    sig = sigmoid(z)
    slope = w2 * (sig * (1.0 + z * (1.0 - sig)))
    first_hi, first_lo = split(jnp.concatenate(basis, axis=1) * rows)
    first_in = jnp.concatenate([first_hi, first_lo], axis=0).astype(BF16)
    slope_hi, slope_lo = (t.astype(BF16) for t in split(slope))
    hid_hi, hid_lo = (t.astype(BF16) for t in split(z * sig))
    got_hi = nt(first_in, slope_hi)
    got_lo = nt(first_in, slope_lo)
    out[0:8, :] += got_hi[:8] + got_hi[8:] + got_lo[:8]
    two_hi = nt(second_in, hid_hi)
    two_lo = nt(second_in, hid_lo)
    out[8:9, :] += two_hi[0:1] + two_hi[1:2] + two_lo[0:1]
    out[9:10, :] += loss * (1.0 / (3.0 * beads_all))


def bead_stage(recv, weight, pred, offs, w_first, w_second, beads_all):
    beads = pred.shape[1]
    whole = lambda shape: pl.BlockSpec(shape, lambda i: (0,) * len(shape))
    return pl.pallas_call(
        functools.partial(bead_kernel, beads_all),
        grid=(beads // L,),
        in_specs=[
            whole(recv.shape),
            pl.BlockSpec((1, L), lambda i: (0, i)),
            pl.BlockSpec((3, L), lambda i: (0, i)),
            pl.BlockSpec((3, KB, L), lambda i: (0, 0, i)),
            whole((8, L)),
            whole((L, 1)),
        ],
        out_specs=[whole((3, beads)), whole((16, L))],
        out_shape=[
            jax.ShapeDtypeStruct((3, beads), F32),
            jax.ShapeDtypeStruct((16, L), F32),
        ],
        compiler_params=pltpu.CompilerParams(vmem_limit_bytes=40 * 2**20),
        name="beads",
    )(recv, weight, pred, offs, w_first, w_second)


MESH = pl.DeviceIdType.MESH


LOW = 4


def exchange_kernel(src, dst, first, packed, second, send_sem, recv_sem):
    g = lax.axis_index("grp")
    b = lax.axis_index("brick")
    near = lax.axis_size("grp") * LOW
    far = lax.axis_size("brick") // LOW
    h = b // LOW
    z = lax.rem(b, LOW)
    mine = g * LOW + z
    span = 2 * far

    def near_place(d):
        j = lax.rem(mine + d, near)
        return j, (j // LOW, h * LOW + lax.rem(j, LOW))

    def far_place(d):
        j = lax.rem(h + d, far)
        return j, (g, j * LOW + z)

    barrier = pltpu.get_barrier_semaphore()
    for count, place in ((near, near_place), (far, far_place)):
        for d in range(1, count):
            pl.semaphore_signal(barrier, inc=1, device_id=place(d)[1], device_id_type=MESH)
    pl.semaphore_wait(barrier, near + far - 2)
    at_mine = pl.ds(pl.multiple_of(mine * span, span), span)
    copies = []
    for d in range(1, near):
        j, where = near_place(d)
        copies.append(
            pltpu.make_async_remote_copy(
                src_ref=src.at[pl.ds(pl.multiple_of(j * span, span), span)],
                dst_ref=first.at[at_mine],
                send_sem=send_sem.at[d - 1],
                recv_sem=recv_sem.at[d - 1],
                device_id=where,
                device_id_type=MESH,
            )
        )
        copies[-1].start()
    first[at_mine, :] = src[at_mine, :]
    for copy in copies:
        copy.wait()
    for j in range(far):
        packed[j] = first[pl.ds(j, 2 * near, stride=far), :]
    copies = []
    for d in range(1, far):
        j, where = far_place(d)
        copies.append(
            pltpu.make_async_remote_copy(
                src_ref=packed.at[j],
                dst_ref=second.at[h],
                send_sem=send_sem.at[near + d - 2],
                recv_sem=recv_sem.at[near + d - 2],
                device_id=where,
                device_id_type=MESH,
            )
        )
        copies[-1].start()
    second[pl.ds(h, 1)] = packed[pl.ds(h, 1)]
    for copy in copies:
        copy.wait()
    for j in range(far):
        dst[j * 2 * near : (j + 1) * 2 * near, :] = second[j]


def exchange(rows):
    near = lax.axis_size("grp") * LOW
    far = lax.axis_size("brick") // LOW
    vmem = pl.BlockSpec(memory_space=pltpu.VMEM)
    return pl.pallas_call(
        exchange_kernel,
        in_specs=[vmem],
        out_specs=vmem,
        out_shape=jax.ShapeDtypeStruct(rows.shape, F32),
        scratch_shapes=[
            pltpu.VMEM(rows.shape, F32),
            pltpu.VMEM((far, 2 * near, L), F32),
            pltpu.VMEM((far, 2 * near, L), F32),
            pltpu.SemaphoreType.DMA((near + far - 2,)),
            pltpu.SemaphoreType.DMA((near + far - 2,)),
        ],
        compiler_params=pltpu.CompilerParams(collective_id=1, has_side_effects=True),
        name="exchange",
    )(rows)


def reduce_kernel(x, out, first, second, third, send_sem, recv_sem):
    g = lax.axis_index("grp")
    b = lax.axis_index("brick")
    groups = first.shape[0]
    low = second.shape[0]
    high = third.shape[0]
    z = lax.rem(b, low)
    h = b // low
    stages = (
        (first, groups, g, lambda d: (lax.rem(g + d, groups), b)),
        (second, low, z, lambda d: (g, h * low + lax.rem(z + d, low))),
        (third, high, h, lambda d: (g, lax.rem(h + d, high) * low + z)),
    )
    barrier = pltpu.get_barrier_semaphore()
    partners = 0
    for _, size, _, where in stages:
        for d in range(1, size):
            pl.semaphore_signal(barrier, inc=1, device_id=where(d), device_id_type=MESH)
            partners += 1
    pl.semaphore_wait(barrier, partners)
    value = x[...]
    used = 0
    for slots, size, mine, where in stages:
        slots[pl.ds(mine, 1)] = value[None]
        copies = []
        for d in range(1, size):
            copy = pltpu.make_async_remote_copy(
                src_ref=slots.at[mine],
                dst_ref=slots.at[mine],
                send_sem=send_sem.at[used],
                recv_sem=recv_sem.at[used],
                device_id=where(d),
                device_id_type=MESH,
            )
            used += 1
            copy.start()
            copies.append(copy)
        for copy in copies:
            copy.wait()
        value = slots[0]
        for i in range(1, size):
            value = value + slots[i]
    out[...] = value


def reduce_all(x):
    groups = lax.axis_size("grp")
    bricks = lax.axis_size("brick")
    low = LOW
    high = bricks // low
    count = groups + low + high - 3
    vmem = pl.BlockSpec(memory_space=pltpu.VMEM)
    return pl.pallas_call(
        reduce_kernel,
        in_specs=[vmem],
        out_specs=vmem,
        out_shape=jax.ShapeDtypeStruct(x.shape, F32),
        scratch_shapes=[pltpu.VMEM((n,) + x.shape, F32) for n in (groups, low, high)]
        + [pltpu.SemaphoreType.DMA((count,)), pltpu.SemaphoreType.DMA((count,))],
        compiler_params=pltpu.CompilerParams(collective_id=2, has_side_effects=True),
        name="reduce",
    )(x)


def local(
    positions,
    features,
    teacher_nbr,
    nbr_count,
    w_rad,
    w_mix,
    w_out,
    block_owner,
    block_start,
    atom_bead,
    bead_pos,
    bead_nbr,
    bead_weight,
    w_first,
    w_second,
):
    atoms = positions.shape[1]
    devices = lax.axis_size(AXES)
    count = devices
    beads = bead_pos.shape[1]
    up = [(i, i + 1) for i in range(count - 1)]
    down = [(i + 1, i) for i in range(count - 1)]

    def payload(feat, pos, bead):
        tail = jnp.concatenate([pos, jnp.pad(bead, ((0, 2), (0, G - BW)))], axis=0)
        return jnp.concatenate([feat, tail], axis=0)

    left = lax.ppermute(
        payload(features[:, atoms - G :], positions[:, atoms - G :], bead_pos[:, beads - BW :]), AXES, up
    )
    right = lax.ppermute(payload(features[:, :G], positions[:, :G], bead_pos[:, :BW]), AXES, down)
    ext_pos = jnp.concatenate([left[L : L + 3], positions, right[L : L + 3]], axis=1)
    bead_ext = jnp.concatenate(
        [left[L + 3 : L + 6, :BW], bead_pos, right[L + 3 : L + 6, :BW], jnp.zeros((3, L - 2 * BW), F32)],
        axis=1,
    )
    second = w_second.reshape(L, 1)
    pred, offs = student(bead_nbr.T, bead_ext.reshape(3, (beads + L) // L, L), w_first, second)
    blocks = block_owner.shape[0]
    block_atoms = atoms // blocks
    order = jnp.arange(blocks, dtype=jnp.int32)
    same = (block_owner[:, None] == block_owner[None, :]) & (order[None, :] < order[:, None])
    rank = jnp.sum(same.astype(jnp.int32), axis=1)
    bricks = lax.axis_size("brick")
    far = bricks // LOW
    near_at = (block_owner // bricks) * LOW + block_owner % LOW
    dest = near_at * 2 * far + rank * far + (block_owner % bricks) // LOW
    spread = lambda v: jnp.broadcast_to(v[:, None], (blocks, block_atoms)).reshape(1, atoms)
    acc = teacher(
        teacher_nbr.T, nbr_count, features, left, right, ext_pos, w_rad, w_mix, w_out
    )
    ext_rows = (atoms + 2 * G) // L
    grads = acc[:, :ext_rows].reshape(3, atoms + 2 * G)
    above = lax.ppermute(grads[:, :G], AXES, down)
    below = lax.ppermute(grads[:, atoms + G :], AXES, up)
    force = -grads[:, G : atoms + G]
    force = force - jnp.pad(below, ((0, 0), (0, atoms - G))) - jnp.pad(above, ((0, 0), (atoms - G, 0)))
    outgoing = mapping(
        force, atom_bead.reshape(1, atoms), spread(dest), spread(block_start.astype(F32))
    )
    recv = exchange(outgoing)
    bead_force, sums = bead_stage(
        recv, bead_weight.reshape(1, beads), pred, offs, w_first, second, beads * devices
    )
    sums = reduce_all(sums)
    return force, bead_force, pred, sums[:8], sums[8], jnp.sum(sums[9])


def solution(mesh):
    wide = P(None, AXES)
    tall = P(AXES, None)
    flat = P(AXES)
    return jax.shard_map(
        local,
        mesh=mesh,
        in_specs=(
            wide, wide, tall, flat, P(), P(), P(), flat, flat, flat, wide, tall, flat, P(), P(),
        ),
        out_specs=(wide, wide, wide, P(), P(), P()),
        check_vma=False,
    )
```

time: 277 us -> 220 us (0.79)
  Pallas kernels: 231 us -> 183 us
  local copies, waits for them, and re-layouts: 19 us -> 11.3 us
  waiting for transfers between devices: 0.02 us -> 6.96 us
  starting transfers between devices: 19.5 us -> 13.6 us
    pallas_call x1, Pallas kernels: 160 us -> 124 us  [teacher(): pl.pallas_call(teacher_kernel, in_specs=[pl.BlockSpec(memory_space=pl.ANY...]
    pallas_call x1, Pallas kernels: 41.6 us -> 29.9 us  [exchange(): pl.pallas_call(exchange_kernel, in_specs=[vmem], out_specs=vmem, out_shap...]
    unnamed x38, local copies, waits for them, and re-layouts: 11.8 us -> 2.48 us
    ppermute x4 -> x2, waiting for transfers between devices: 0.01 us -> 6.96 us  [the longest x1 6.96 us: local(): lax.ppermute(payload(features[:, :G], positions[:, :G], bead_pos[:, :BW])...]
    ppermute x4 -> x2, starting transfers between devices: 11.8 us -> 6.66 us  [the longest x1 5.37 us: local(): lax.ppermute(payload(features[:, atoms - G:], positions[:, atoms - G:], b...]
  transfers between devices with their start and end apart: 6 -> 4, of which waited for: 0 -> 1; matrix products, arithmetic and copies ran while one was open for 3% -> 2% of each run, Pallas kernels for 1% -> 1%
where the time goes in v3:
time: 220 us; the launch traced here: 219 us
  Pallas kernels  183 us (83%)
  starting transfers between devices  13.6 us (6%)
  local copies, waits for them, and re-layouts  11.3 us (5%)
  waiting for transfers between devices  6.96 us (3%)
  other arithmetic  3 us (1%)
    pallas_call x1, Pallas kernels, teacher(): pl.pallas_call(teacher_kernel, in_specs=[pl.BlockSpec(memory_space=pl.ANY...  124 us
    pallas_call x1, Pallas kernels, exchange(): pl.pallas_call(exchange_kernel, in_specs=[vmem], out_specs=vmem, out_shap...  29.9 us
    pallas_call x1, Pallas kernels, reduce_all(): pl.pallas_call(reduce_kernel, in_specs=[vmem], out_specs=vmem, out_shape=...  16.1 us
    ppermute x1, waiting for transfers between devices, local(): lax.ppermute(payload(features[:, :G], positions[:, :G], bead_pos[:, :BW])...  6.96 us
    ppermute x1, starting transfers between devices, local(): below = lax.ppermute(grads[:, atoms + G:], AXES, up)  5.6 us
    ppermute x1, starting transfers between devices, local(): lax.ppermute(payload(features[:, atoms - G:], positions[:, atoms - G:], b...  5.37 us
    pallas_call x1, Pallas kernels, mapping(): pl.pallas_call(mapping_kernel, grid=(atoms // CHUNK,), in_specs=[row(3),...  5.35 us
    pallas_call x1, Pallas kernels, bead_stage(): pl.pallas_call(functools.partial(bead_kernel, beads_all), grid=(beads //...  5.2 us
  transfers between devices with their start and end apart: 4, of which 1 were waited for; matrix products, arithmetic and copies ran while one was open for 2% of the time, Pallas kernels for 1%

profile of v3, /device:TPU:0, one launch (start us, length us, event | category | flops | bytes accessed | tf_op | source)
XLA Modules:
  0.0 218.8 jit_solution(6608049958524814657)
XLA Ops:
  0.7 0.8 fusion.8
  1.5 0.7 fusion.7
  2.2 1.3 fusion.5
  3.7 1.3 collective-permute-start.1
  5.0 5.4 %collective-permute-start = (f32[136,1024]{1,0:T(8,128)S(1)}, f32[136,1024]{1,0:T(8,128)}, u32[]{:S(2)}, u32[]{:S(2)}) collective-permute-start(f32[136,1024]{1,0:T(8,128)S(1)} %select_maximum_fusion.1), channel_id=1, source_target_pairs={{0,1},{1,2},{2,3},{3,4},{4,5},{5,6},{6,7},{7,8},{8,9},{9,10},{10,1... | collective-permute-start | bytes 1671176 | tf_op jit(solution)/shard_map/ppermute | solution.py:689
  11.5 0.7 reshape.59.dest
  12.3 0.7 reshape.60.start
  13.3 7.0 %collective-permute-done.1.right = f32[136,1024]{1,0:T(8,128)S(1)} collective-permute-done((f32[136,1024]{1,0:T(8,128)S(1)}, f32[136,1024]{1,0:T(8,128)S(1)}, u32[]{:S(2)}, u32[]{:S(2)}) %collective-permute-start.1) | collective-permute-done | bytes 557088 | tf_op jit(solution)/shard_map/ppermute | solution.py:692
  20.2 0.8 slice.68
  21.2 123.6 %teacher.1 = f32[3,104,128]{2,1,0:T(8,128)S(1)} custom-call(s32[64,1,1536]{2,1,0:T(1,128)S(1)} %reshape.64.idx_h, s32[12,8192]{1,0:T(8,128)S(1)} %bitcast.26, s32[1,8192]{1,0:T(1,128)S(1)} %bitcast.28, f32[128,8192]{1,0:T(8,128)} %feat.1, f32[136,1024]{1,0:T(8,128)} %collective-permute-done.left, f32[136,1024]{1,0:T(8,128)} %copy-done.15, ...), custom_call_target="tpu_custom_call" | custom-call | flops 20000000000 | bytes 8388608 | tf_op jit(solution)/shard_map/teacher/pallas_call | solution.py:283
  145.0 1.3 collective-permute-start.3
  146.3 5.6 %collective-permute-start.2 = (f32[3,1024]{1,0:T(4,128)S(1)}, f32[3,1024]{1,0:T(4,128)S(1)}, u32[]{:S(2)}, u32[]{:S(2)}) collective-permute-start(f32[3,1024]{1,0:T(4,128)S(1)} %get-tuple-element.16), channel_id=1, source_target_pairs={{0,1},{1,2},{2,3},{3,4},{4,5},{5,6},{6,7},{7,8},{8,9},{9,10},{10,1... | collective-permute-start | bytes 36872 | tf_op jit(solution)/shard_map/ppermute | solution.py:716
  151.9 0.7 slice.75
  152.6 0.7 slice.74
  153.4 2.9 %student.1 = (f32[3,512]{1,0:T(4,128)}, f32[3,16,512]{2,1,0:T(8,128)S(1)}) custom-call(s32[16,512]{1,0:T(8,128)S(1)} %bitcast.29, f32[3,5,128]{2,1,0:T(8,128)S(1)} %reshape.62.pos, f32[8,128]{1,0:T(8,128)S(1)} %copy-done.4, f32[128,1]{1,0:T(8,128)S(1)} %copy.30.w_second), custom_call_target="tpu_custom_call" | custom-call | flops 1000000000 | bytes 1000000 | tf_op jit(solution)/shard_map/student/pallas_call | solution.py:369
  156.3 0.7 fusion.2.force
  157.0 5.4 %mapping.1.src = f32[256,128]{1,0:T(8,128)} custom-call(f32[3,8192]{1,0:T(4,128)} %fusion.2.force, s32[1,8192]{1,0:T(1,128)} %bitcast.36, s32[1,8192]{1,0:T(1,128)} %reshape.59.dest, f32[1,8192]{1,0:T(1,128)} %reshape.60.start), custom_call_target="tpu_custom_call" | custom-call | tf_op jit(solution)/shard_map/mapping/pallas_call | solution.py:425
  162.3 29.9 %exchange.1.recv = f32[256,128]{1,0:T(8,128)} custom-call(f32[256,128]{1,0:T(8,128)} %mapping.1.src), custom_call_target="tpu_custom_call" | custom-call | tf_op jit(solution)/shard_map/exchange/pallas_call | solution.py:580
  192.2 0.9 copy-done
  193.1 0.7 copy-done.2
  193.8 5.2 %beads.1 = (f32[3,512]{1,0:T(4,128)}, f32[16,128]{1,0:T(8,128)S(1)}) custom-call(f32[256,128]{1,0:T(8,128)S(1)} %copy-done, f32[1,512]{1,0:T(1,128)S(1)} %bitcast.27, f32[3,512]{1,0:T(4,128)S(1)} %copy-done.2, f32[3,16,512]{2,1,0:T(8,128)S(1)} %get-tuple-element.11.offs, f32[8,128]{1,0:T(8,128)S(1)} %copy-done.4, f32[128,1]{1,0:T(8,128)S(1)} %copy.30.w_second), custom_call_target="tpu_custom_call" | custom-call | tf_op jit(solution)/shard_map/beads/pallas_call | solution.py:485
  199.6 16.1 %reduce.2 = f32[16,128]{1,0:T(8,128)} custom-call(f32[16,128]{1,0:T(8,128)} %copy-done.3), custom_call_target="tpu_custom_call" | custom-call | tf_op jit(solution)/shard_map/reduce/pallas_call | solution.py:649
  215.7 1.3 slice.65
  217.0 1.9 slice_reduce_fusion
  (59 shorter events, 2.4 us)
Async XLA Ops:
  0.6 9.8 %copy-start.1 = (s32[8192,12]{0,1:T(8,128)S(1)}, s32[8192,12]{0,1:T(8,128)}, u32[]{:S(2)}) copy-start(s32[8192,12]{0,1:T(8,128)} %param.17) | copy-start | bytes 1179652
  0.6 10.6 %copy-start.13 = (s32[256]{0:T(256)S(1)}, s32[256]{0:T(256)}, u32[]{:S(2)}) copy-start(s32[256]{0:T(256)} %param.22) | copy-start | bytes 3076
  0.7 11.6 %copy-start.14 = (s32[256]{0:T(256)S(1)}, s32[256]{0:T(256)}, u32[]{:S(2)}) copy-start(s32[256]{0:T(256)} %param.23) | copy-start | bytes 3076
  2.2 10.8 %copy-start.16 = (f32[128]{0:T(128)S(1)}, f32[128]{0:T(128)}, u32[]{:S(2)}) copy-start(f32[128]{0:T(128)} %param.29) | copy-start | bytes 1540
  2.2 18.8 %copy-start.11 = (f32[3,8192]{1,0:T(4,128)S(1)}, f32[3,8192]{1,0:T(4,128)}, u32[]{:S(2)}) copy-start(f32[3,8192]{1,0:T(4,128)} %param.15) | copy-start | bytes 294916
  3.6 17.6 %copy-start.6 = (f32[128,128]{1,0:T(8,128)S(1)}, f32[128,128]{1,0:T(8,128)}, u32[]{:S(2)}) copy-start(f32[128,128]{1,0:T(8,128)} %w_mix.1) | copy-start | bytes 196612
  3.6 17.6 %copy-start.7 = (s32[8192]{0:T(1024)S(1)}, s32[8192]{0:T(1024)}, u32[]{:S(2)}) copy-start(s32[8192]{0:T(1024)} %param.18) | copy-start | bytes 98308
  3.6 17.6 %copy-start.9 = (f32[8,128]{1,0:T(8,128)S(1)}, f32[8,128]{1,0:T(8,128)}, u32[]{:S(2)}) copy-start(f32[8,128]{1,0:T(8,128)} %w_rad.1) | copy-start | bytes 12292
  3.6 17.6 %copy-start.10 = (f32[128]{0:T(128)S(1)}, f32[128]{0:T(128)}, u32[]{:S(2)}) copy-start(f32[128]{0:T(128)} %param.21) | copy-start | bytes 1540
  3.7 16.5 %collective-permute-start.1 = (f32[136,1024]{1,0:T(8,128)S(1)}, f32[136,1024]{1,0:T(8,128)S(1)}, u32[]{:S(2)}, u32[]{:S(2)}) collective-permute-start(f32[136,1024]{1,0:T(8,128)S(1)} %select_maximum_fusion), channel_id=1, source_target_pairs={{1,0},{2,1},{3,2},{4,3},{5,4},{6,5},{7,6},{8,7},{9,8},{10,9},{11,1... | collective-permute-start | bytes 1671176 | tf_op jit(solution)/shard_map/ppermute | solution.py:692
  5.0 15.2 %collective-permute-start = (f32[136,1024]{1,0:T(8,128)S(1)}, f32[136,1024]{1,0:T(8,128)}, u32[]{:S(2)}, u32[]{:S(2)}) collective-permute-start(f32[136,1024]{1,0:T(8,128)S(1)} %select_maximum_fusion.1), channel_id=1, source_target_pairs={{0,1},{1,2},{2,3},{3,4},{4,5},{5,6},{6,7},{7,8},{8,9},{9,10},{10,1... | collective-permute-start | bytes 1671176 | tf_op jit(solution)/shard_map/ppermute | solution.py:689
  20.2 0.9 copy-start.15
  21.2 132.1 %copy-start.12 = (f32[3,512]{1,0:T(4,128)S(1)}, f32[3,512]{1,0:T(4,128)}, u32[]{:S(2)}) copy-start(f32[3,512]{1,0:T(4,128)} %param.25) | copy-start | bytes 18436
  21.2 132.2 %copy-start.4 = (f32[8,128]{1,0:T(8,128)S(1)}, f32[8,128]{1,0:T(8,128)}, u32[]{:S(2)}) copy-start(f32[8,128]{1,0:T(8,128)} %w_first.3) | copy-start | bytes 12292
  21.2 132.1 %copy-start.8 = (s32[512,16]{0,1:T(8,128)S(1)}, s32[512,16]{0,1:T(8,128)}, u32[]{:S(2)}) copy-start(s32[512,16]{0,1:T(8,128)} %param.26) | copy-start | bytes 98308
  144.9 47.3 %copy-start.5 = (f32[512]{0:T(512)S(1)}, f32[512]{0:T(512)}, u32[]{:S(2)}) copy-start(f32[512]{0:T(512)} %param.27) | copy-start | bytes 6148
  145.0 11.3 %collective-permute-start.3 = (f32[3,1024]{1,0:T(4,128)S(1)}, f32[3,1024]{1,0:T(4,128)S(1)}, u32[]{:S(2)}, u32[]{:S(2)}) collective-permute-start(f32[3,1024]{1,0:T(4,128)S(1)} %get-tuple-element.17), channel_id=1, source_target_pairs={{1,0},{2,1},{3,2},{4,3},{5,4},{6,5},{7,6},{8,7},{9,8},{10,9},{11,1... | collective-permute-start | bytes 36872 | tf_op jit(solution)/shard_map/ppermute | solution.py:715
  146.3 10.0 %collective-permute-start.2 = (f32[3,1024]{1,0:T(4,128)S(1)}, f32[3,1024]{1,0:T(4,128)S(1)}, u32[]{:S(2)}, u32[]{:S(2)}) collective-permute-start(f32[3,1024]{1,0:T(4,128)S(1)} %get-tuple-element.16), channel_id=1, source_target_pairs={{0,1},{1,2},{2,3},{3,4},{4,5},{5,6},{6,7},{7,8},{8,9},{9,10},{10,1... | collective-permute-start | bytes 36872 | tf_op jit(solution)/shard_map/ppermute | solution.py:716
  192.2 0.9 copy-start
  193.1 0.7 copy-start.2
  199.0 0.6 copy-start.3

commit v4 on v3

--- a/solution.py
+++ b/solution.py
@@ -143,7 +143,7 @@
     sent[...] = message
 
 
-def backward_part(blk, held, idx, mix, w_out, acc, table):
+def backward_part(blk, own_at, held, idx, mix, w_out, acc, table):
     rows, slope_w, hots, offs, sent = held
     hi = (idx - blk * L) >> 7
     subw = iota((WIN, L), 0)
@@ -155,7 +155,7 @@
         wide = jnp.concatenate([x_hi, x_lo], axis=1).astype(BF16)
         return nn(wide, w_hh) + nn(wide[:, :L], w_l)
 
-    own_rows = table[pl.ds(pl.multiple_of(G + blk * L, L), L), :]
+    own_rows = table[pl.ds(pl.multiple_of(own_at, L), L), :]
     mixed = product(sent[...] * scale, mix_hh, mix_l)
     yield
     pre = mixed + own_rows
@@ -210,31 +210,43 @@
                 alive.remove(part)
 
 
-def teacher_kernel(
-    idx_h, idx_v, count_v, feat, left, right, pos, w_rad, w_mix, w_out,
-    acc, table, idx_a, idx_b, sem_a, sem_b, *held,
-):
+EDGE = G // L
+
+
+def interior_place(blocks, j):
+    return j + EDGE, (j + EDGE) * L
+
+
+def border_place(blocks, j):
+    upper = (j >= EDGE).astype(jnp.int32)
+    return j + upper * (blocks - 2 * EDGE), G + j * L + upper * 2 * G
+
+
+def teacher_kernel(sources, place, with_sums, idx_h, idx_v, count_v, pos, w_rad, w_mix, w_out, *rest):
+    feats, rest = rest[:sources], rest[sources:]
+    if with_sums:
+        sums, rest = rest[0], rest[1:]
+    acc, table, idx_a, idx_b, sem_a, sem_b = rest[:6]
+    held_a, held_b = rest[6:11], rest[11:]
     blocks = idx_h.shape[0]
-    acc[...] = jnp.zeros_like(acc)
-    held_a, held_b = held[:5], held[5:]
-
-    def flip(source, base):
-        def one(j, carry):
-            src = pl.ds(pl.multiple_of(j * L, L), L)
-            dst = pl.ds(pl.multiple_of(base + j * L, L), L)
-            table[dst, :] = source[:L, src].T
-            return carry
-
-        lax.fori_loop(0, source.shape[1] // L, one, 0)
 
     def bring(blk, idx, sem):
         return pltpu.make_async_copy(idx_h.at[jnp.minimum(blk, blocks - 1)], idx, sem)
 
     bring(0, idx_a, sem_a).start()
     bring(1, idx_b, sem_b).start()
-    flip(left, 0)
-    flip(feat, G)
-    flip(right, G + feat.shape[1])
+    acc[...] = sums[...] if with_sums else jnp.zeros_like(acc)
+    base = 0
+    for source in feats:
+        def one(j, carry, source=source, base=base):
+            for u in range(4):
+                src = pl.ds(pl.multiple_of(j * 4 * L + u * L, L), L)
+                dst = pl.ds(pl.multiple_of(base + j * 4 * L + u * L, L), L)
+                table[dst, :] = source[:L, src].T
+            return carry
+
+        lax.fori_loop(0, source.shape[1] // (4 * L), one, 0)
+        base += source.shape[1]
     weight = w_rad[...]
     rate_w = rate_column() * weight
     weights = jnp.concatenate([stack_weight(weight), stack_weight(-rate_w)], axis=1).astype(BF16)
@@ -243,50 +255,61 @@
         w_hi, w_lo = split(w)
         mix += [jnp.concatenate([w_hi, w_hi], axis=0).astype(BF16), w_lo.astype(BF16)]
 
-    def forward(blk, held, idx_s):
+    def forward(j, held, idx_s):
+        blk, _ = place(j)
         lanes = pl.ds(pl.multiple_of(blk * L, L), L)
         return forward_part(blk, held, idx_s, idx_v[:, lanes], count_v[:, lanes], pos, weights, table)
 
-    def backward(blk, held):
+    def backward(j, held):
+        blk, own_at = place(j)
         lanes = pl.ds(pl.multiple_of(blk * L, L), L)
-        return backward_part(blk, held, idx_v[:, lanes], mix, w_out, acc, table)
+        return backward_part(blk, own_at, held, idx_v[:, lanes], mix, w_out, acc, table)
 
     bring(0, idx_a, sem_a).wait()
-    for _ in forward(0, held_a, idx_a):
+    for _ in forward(jnp.int32(0), held_a, idx_a):
         pass
     bring(2, idx_a, sem_a).start()
 
     def step(i, carry):
         for t, old, new, idx, sem in ((0, held_a, held_b, idx_b, sem_b), (1, held_b, held_a, idx_a, sem_a)):
-            blk = 2 * i + t
-            bring(blk + 1, idx, sem).wait()
-            run_beside(backward(blk, old), forward(jnp.minimum(blk + 1, blocks - 1), new, idx))
+            j = 2 * i + t
+            bring(j + 1, idx, sem).wait()
+            run_beside(backward(j, old), forward(jnp.minimum(j + 1, blocks - 1), new, idx))
 
             @pl.when(i < blocks // 2 - 1)
             def _():
-                bring(blk + 3, idx, sem).start()
+                bring(j + 3, idx, sem).start()
 
         return carry
 
     lax.fori_loop(0, blocks // 2, step, 0)
 
 
-def teacher(idx, count, feat, left, right, ext_pos, w_rad, w_mix, w_out):
-    atoms = feat.shape[1]
-    blocks = atoms // L
+def teacher_call(name, place, rows_of, idx, count, ext_pos, weights, feats, sums=None):
+    atoms = idx.shape[1]
     ext_rows = (atoms + 2 * G) // L
     tall = ext_rows + 24
     pos = jnp.pad(ext_pos.reshape(3, ext_rows, L), ((0, 0), (0, 24), (0, 0)))
     hi = lax.reduce_precision(pos, 8, 7)
     pos = jnp.concatenate([hi, pos - hi], axis=0)
     vmem = pl.BlockSpec(memory_space=pltpu.VMEM)
+    whole = lambda x: pl.BlockSpec(x.shape, lambda i: (0,) * x.ndim)
+    w_rad, w_mix, w_out = weights
+    small = (idx, count.reshape(1, atoms), pos, w_rad, w_mix, w_out.reshape(1, L))
+    arrays = [x for x, _ in feats]
+    specs = [s if s is not None else whole(x) for x, s in feats]
+    width = sum(s.block_shape[1] for s in specs)
+    if sums is not None:
+        arrays.append(sums)
+        specs.append(whole(sums))
     return pl.pallas_call(
-        teacher_kernel,
-        in_specs=[pl.BlockSpec(memory_space=pl.ANY)] + [vmem] * 9,
-        out_specs=vmem,
+        functools.partial(teacher_kernel, len(feats), place, sums is not None),
+        grid=(1,),
+        in_specs=[pl.BlockSpec(memory_space=pl.ANY)] + [whole(x) for x in small] + specs,
+        out_specs=pl.BlockSpec((3, tall, L), lambda i: (0, 0, 0)),
         out_shape=jax.ShapeDtypeStruct((3, tall, L), F32),
         scratch_shapes=[
-            pltpu.VMEM((atoms + 2 * G, L), F32),
+            pltpu.VMEM((width, L), F32),
             pltpu.SMEM((1, K * L), jnp.int32),
             pltpu.SMEM((1, K * L), jnp.int32),
             pltpu.SemaphoreType.DMA,
@@ -302,21 +325,18 @@
         ],
         compiler_params=pltpu.CompilerParams(vmem_limit_bytes=52 * 2**20),
         cost_estimate=pl.CostEstimate(
-            flops=2 * 10**10, bytes_accessed=8 * 2**20, transcendentals=10**6
+            flops=5 * 10**10, bytes_accessed=64 * 2**20, transcendentals=10**6
         ),
-        name="teacher",
-    )(
-        idx.reshape(K, blocks, L).transpose(1, 0, 2).reshape(blocks, 1, K * L),
-        idx,
-        count.reshape(1, atoms),
-        feat,
-        left,
-        right,
-        pos,
-        w_rad,
-        w_mix,
-        w_out.reshape(1, L),
-    )
+        name=name,
+    )(rows_of, *small, *arrays)
+
+
+def teacher_parts(idx, atoms):
+    blocks = atoms // L
+    rows = idx.reshape(K, blocks, L).transpose(1, 0, 2).reshape(blocks, 1, K * L)
+    inner = rows[EDGE : blocks - EDGE] - G
+    outer = jnp.concatenate([rows[:EDGE], rows[blocks - EDGE :] - (atoms - 4 * G)], axis=0)
+    return inner, outer
 
 
 KB = 16
@@ -594,35 +614,37 @@
     )(rows)
 
 
-def reduce_kernel(x, out, first, second, third, send_sem, recv_sem):
+def reduce_kernel(x, out, first, second, send_sem, recv_sem):
     g = lax.axis_index("grp")
     b = lax.axis_index("brick")
-    groups = first.shape[0]
-    low = second.shape[0]
-    high = third.shape[0]
-    z = lax.rem(b, low)
-    h = b // low
-    stages = (
-        (first, groups, g, lambda d: (lax.rem(g + d, groups), b)),
-        (second, low, z, lambda d: (g, h * low + lax.rem(z + d, low))),
-        (third, high, h, lambda d: (g, lax.rem(h + d, high) * low + z)),
-    )
+    near = first.shape[0]
+    far = second.shape[0]
+    z = lax.rem(b, LOW)
+    h = b // LOW
+    mine = g * LOW + z
+
+    def near_place(d):
+        j = lax.rem(mine + d, near)
+        return (j // LOW, h * LOW + lax.rem(j, LOW))
+
+    def far_place(d):
+        return (g, lax.rem(h + d, far) * LOW + z)
+
+    stages = ((first, near, mine, near_place), (second, far, h, far_place))
     barrier = pltpu.get_barrier_semaphore()
-    partners = 0
     for _, size, _, where in stages:
         for d in range(1, size):
             pl.semaphore_signal(barrier, inc=1, device_id=where(d), device_id_type=MESH)
-            partners += 1
-    pl.semaphore_wait(barrier, partners)
+    pl.semaphore_wait(barrier, near + far - 2)
     value = x[...]
     used = 0
-    for slots, size, mine, where in stages:
-        slots[pl.ds(mine, 1)] = value[None]
+    for slots, size, at, where in stages:
+        slots[pl.ds(at, 1)] = value[None]
         copies = []
         for d in range(1, size):
             copy = pltpu.make_async_remote_copy(
-                src_ref=slots.at[mine],
-                dst_ref=slots.at[mine],
+                src_ref=slots.at[at],
+                dst_ref=slots.at[at],
                 send_sem=send_sem.at[used],
                 recv_sem=recv_sem.at[used],
                 device_id=where(d),
@@ -640,19 +662,16 @@
 
 
 def reduce_all(x):
-    groups = lax.axis_size("grp")
-    bricks = lax.axis_size("brick")
-    low = LOW
-    high = bricks // low
-    count = groups + low + high - 3
+    near = lax.axis_size("grp") * LOW
+    far = lax.axis_size("brick") // LOW
     vmem = pl.BlockSpec(memory_space=pltpu.VMEM)
     return pl.pallas_call(
         reduce_kernel,
         in_specs=[vmem],
         out_specs=vmem,
         out_shape=jax.ShapeDtypeStruct(x.shape, F32),
-        scratch_shapes=[pltpu.VMEM((n,) + x.shape, F32) for n in (groups, low, high)]
-        + [pltpu.SemaphoreType.DMA((count,)), pltpu.SemaphoreType.DMA((count,))],
+        scratch_shapes=[pltpu.VMEM((n,) + x.shape, F32) for n in (near, far)]
+        + [pltpu.SemaphoreType.DMA((near + far - 2,)), pltpu.SemaphoreType.DMA((near + far - 2,))],
         compiler_params=pltpu.CompilerParams(collective_id=2, has_side_effects=True),
         name="reduce",
     )(x)
@@ -690,6 +709,15 @@
         payload(features[:, atoms - G :], positions[:, atoms - G :], bead_pos[:, beads - BW :]), AXES, up
     )
     right = lax.ppermute(payload(features[:, :G], positions[:, :G], bead_pos[:, :BW]), AXES, down)
+    idx = teacher_nbr.T
+    inner, outer = teacher_parts(idx, atoms)
+    weights = (w_rad, w_mix, w_out)
+    blocks_all = atoms // L
+    acc = teacher_call(
+        "interior", functools.partial(interior_place, blocks_all), inner, idx, nbr_count,
+        jnp.pad(positions, ((0, 0), (G, G))), weights, [(features, None)],
+    )
+    left, right, acc = lax.optimization_barrier((left, right, acc))
     ext_pos = jnp.concatenate([left[L : L + 3], positions, right[L : L + 3]], axis=1)
     bead_ext = jnp.concatenate(
         [left[L + 3 : L + 6, :BW], bead_pos, right[L + 3 : L + 6, :BW], jnp.zeros((3, L - 2 * BW), F32)],
@@ -707,8 +735,11 @@
     near_at = (block_owner // bricks) * LOW + block_owner % LOW
     dest = near_at * 2 * far + rank * far + (block_owner % bricks) // LOW
     spread = lambda v: jnp.broadcast_to(v[:, None], (blocks, block_atoms)).reshape(1, atoms)
-    acc = teacher(
-        teacher_nbr.T, nbr_count, features, left, right, ext_pos, w_rad, w_mix, w_out
+    low_feat = pl.BlockSpec((L, 2 * G), lambda i: (0, 0))
+    high_feat = pl.BlockSpec((L, 2 * G), lambda i: (0, atoms // (2 * G) - 1))
+    acc = teacher_call(
+        "border", functools.partial(border_place, blocks_all), outer, idx, nbr_count, ext_pos, weights,
+        [(left, None), (features, low_feat), (features, high_feat), (right, None)], acc,
     )
     ext_rows = (atoms + 2 * G) // L
     grads = acc[:, :ext_rows].reshape(3, atoms + 2 * G)

time: 220 us -> 203 us (0.923)
  Pallas kernels: 183 us -> 175 us
  waiting for transfers between devices: 6.96 us -> 0.01 us
    ppermute x1, waiting for transfers between devices: 6.96 us -> 0.01 us  [local(): lax.ppermute(payload(features[:, :G], positions[:, :G], bead_pos[:, :BW])...]
    pallas_call x1, Pallas kernels: 29.9 us -> 24.8 us  [exchange(): pl.pallas_call(exchange_kernel, in_specs=[vmem], out_specs=vmem, out_shap...]
    pallas_call x1 -> x2, Pallas kernels: 124 us -> 123 us  [teacher_call(): pl.pallas_call(functools.partial(teacher_kernel, len(feats), place, sums...]
  transfers between devices with their start and end apart: 4 -> 4, of which waited for: 1 -> 0; matrix products, arithmetic and copies ran while one was open for 2% -> 1% of each run, Pallas kernels for 1% -> 46%
where the time goes in v4:
time: 203 us; the launch traced here: 202 us
  Pallas kernels  175 us (86%)
  starting transfers between devices  11.9 us (6%)
  local copies, waits for them, and re-layouts  10.5 us (5%)
  other arithmetic  3.1 us (2%)
    pallas_call x2, Pallas kernels, teacher_call(): pl.pallas_call(functools.partial(teacher_kernel, len(feats), place, sums...  123 us
    pallas_call x1, Pallas kernels, exchange(): pl.pallas_call(exchange_kernel, in_specs=[vmem], out_specs=vmem, out_shap...  24.8 us
    pallas_call x1, Pallas kernels, reduce_all(): pl.pallas_call(reduce_kernel, in_specs=[vmem], out_specs=vmem, out_shape=...  14.7 us
    ppermute x1, starting transfers between devices, local(): below = lax.ppermute(grads[:, atoms + G:], AXES, up)  5.37 us
    pallas_call x1, Pallas kernels, mapping(): pl.pallas_call(mapping_kernel, grid=(atoms // CHUNK,), in_specs=[row(3),...  5.34 us
    pallas_call x1, Pallas kernels, bead_stage(): pl.pallas_call(functools.partial(bead_kernel, beads_all), grid=(beads //...  5.2 us
  transfers between devices with their start and end apart: 4, of which 0 were waited for; matrix products, arithmetic and copies ran while one was open for 1% of the time, Pallas kernels for 46%

profile of v4, /device:TPU:0, one launch (start us, length us, event | category | flops | bytes accessed | tf_op | source)
XLA Modules:
  0.0 202.0 jit_solution(13239324774048257897)
XLA Ops:
  0.7 0.8 fusion.9
  1.5 0.7 fusion.8
  2.2 1.3 fusion.6
  3.6 3.9 %collective-permute-start = (f32[136,1024]{1,0:T(8,128)S(1)}, f32[136,1024]{1,0:T(8,128)S(1)}, u32[]{:S(2)}, u32[]{:S(2)}) collective-permute-start(f32[136,1024]{1,0:T(8,128)S(1)} %select_maximum_fusion.1), channel_id=1, source_target_pairs={{0,1},{1,2},{2,3},{3,4},{4,5},{5,6},{6,7},{7,8},{8,9},{9,10},{10,1... | collective-permute-start | bytes 1671176 | tf_op jit(solution)/shard_map/ppermute | solution.py:708
  7.6 1.3 collective-permute-start.1
  9.9 89.9 %interior.1.rest_4_ = f32[3,104,128]{2,1,0:T(8,128)S(1)} custom-call(s32[48,1,1536]{2,1,0:T(1,128)S(1)} %sub.44.idx_h, s32[12,8192]{1,0:T(8,128)S(1)} %bitcast.34, s32[1,8192]{1,0:T(1,128)S(1)} %bitcast.37, f32[6,104,128]{2,1,0:T(8,128)S(1)} %pad_maximum_fusion.pos, f32[8,128]{1,0:T(8,128)S(1)} %copy-done.9, f32[128,128]{1,0:T(8,128)S(1)} %copy-done.6, ...), custom_call_target="tpu_custom_call" | custom-call | flops 49999998976 | bytes 67108864 | tf_op jit(solution)/shard_map/interior/pallas_call | solution.py:305
  100.0 0.7 reshape.93.dest
  100.9 0.7 reshape.94.start
  101.8 0.8 slice.76
  102.6 0.7 slice.82
  103.5 32.7 %border.1 = f32[3,104,128]{2,1,0:T(8,128)S(1)} custom-call(s32[16,1,1536]{2,1,0:T(1,128)S(1)} %pad_add_fusion.idx_h, s32[12,8192]{1,0:T(8,128)S(1)} %bitcast.35, s32[1,8192]{1,0:T(1,128)S(1)} %bitcast.38, f32[6,104,128]{2,1,0:T(8,128)S(1)} %pad_maximum_fusion.1.pos, f32[8,128]{1,0:T(8,128)S(1)} %copy-done.9, f32[128,128]{1,0:T(8,128)S(1)} %copy-done.6, ...), custom_call_target="tpu_custom_call" | custom-call | flops 49999998976 | bytes 67108864 | tf_op jit(solution)/shard_map/border/pallas_call | solution.py:305
  136.3 1.3 collective-permute-start.3
  137.6 5.4 %collective-permute-start.2 = (f32[3,1024]{1,0:T(4,128)S(1)}, f32[3,1024]{1,0:T(4,128)S(1)}, u32[]{:S(2)}, u32[]{:S(2)}) collective-permute-start(f32[3,1024]{1,0:T(4,128)S(1)} %get-tuple-element.24), channel_id=1, source_target_pairs={{0,1},{1,2},{2,3},{3,4},{4,5},{5,6},{6,7},{7,8},{8,9},{9,10},{10,1... | collective-permute-start | bytes 36872 | tf_op jit(solution)/shard_map/ppermute | solution.py:747
  143.1 2.9 %student.1 = (f32[3,512]{1,0:T(4,128)}, f32[3,16,512]{2,1,0:T(8,128)S(1)}) custom-call(s32[16,512]{1,0:T(8,128)S(1)} %bitcast.39, f32[3,5,128]{2,1,0:T(8,128)S(1)} %reshape.96.pos, f32[8,128]{1,0:T(8,128)S(1)} %copy-done.4, f32[128,1]{1,0:T(8,128)S(1)} %copy.36.w_second), custom_call_target="tpu_custom_call" | custom-call | flops 1000000000 | bytes 1000000 | tf_op jit(solution)/shard_map/student/pallas_call | solution.py:389
  146.0 0.7 fusion.2.force
  146.7 5.3 %mapping.1.src = f32[256,128]{1,0:T(8,128)} custom-call(f32[3,8192]{1,0:T(4,128)} %fusion.2.force, s32[1,8192]{1,0:T(1,128)} %bitcast.47, s32[1,8192]{1,0:T(1,128)} %reshape.93.dest, f32[1,8192]{1,0:T(1,128)} %reshape.94.start), custom_call_target="tpu_custom_call" | custom-call | tf_op jit(solution)/shard_map/mapping/pallas_call | solution.py:445
  152.0 24.8 %exchange.1.recv = f32[256,128]{1,0:T(8,128)} custom-call(f32[256,128]{1,0:T(8,128)} %mapping.1.src), custom_call_target="tpu_custom_call" | custom-call | tf_op jit(solution)/shard_map/exchange/pallas_call | solution.py:600
  176.8 0.9 copy-done
  177.7 0.7 copy-done.2
  178.4 5.2 %beads.1 = (f32[3,512]{1,0:T(4,128)}, f32[16,128]{1,0:T(8,128)S(1)}) custom-call(f32[256,128]{1,0:T(8,128)S(1)} %copy-done, f32[1,512]{1,0:T(1,128)S(1)} %bitcast.36, f32[3,512]{1,0:T(4,128)S(1)} %copy-done.2, f32[3,16,512]{2,1,0:T(8,128)S(1)} %get-tuple-element.17.offs, f32[8,128]{1,0:T(8,128)S(1)} %copy-done.4, f32[128,1]{1,0:T(8,128)S(1)} %copy.36.w_second), custom_call_target="tpu_custom_call" | custom-call | tf_op jit(solution)/shard_map/beads/pallas_call | solution.py:505
  183.6 0.6 copy-done.3
  184.2 14.7 %reduce.2 = f32[16,128]{1,0:T(8,128)} custom-call(f32[16,128]{1,0:T(8,128)} %copy-done.3), custom_call_target="tpu_custom_call" | custom-call | tf_op jit(solution)/shard_map/reduce/pallas_call | solution.py:668
  198.9 1.3 slice.83
  200.2 1.9 slice_reduce_fusion
  (67 shorter events, 1.8 us)
Async XLA Ops:
  0.6 8.5 %copy-start.11 = (f32[3,8192]{1,0:T(4,128)S(1)}, f32[3,8192]{1,0:T(4,128)}, u32[]{:S(2)}) copy-start(f32[3,8192]{1,0:T(4,128)} %param.15) | copy-start | bytes 294916
  0.6 8.3 %copy-start.1 = (s32[8192,12]{0,1:T(8,128)S(1)}, s32[8192,12]{0,1:T(8,128)}, u32[]{:S(2)}) copy-start(s32[8192,12]{0,1:T(8,128)} %param.17) | copy-start | bytes 1179652
  3.5 6.3 %copy-start.6 = (f32[128,128]{1,0:T(8,128)S(1)}, f32[128,128]{1,0:T(8,128)}, u32[]{:S(2)}) copy-start(f32[128,128]{1,0:T(8,128)} %w_mix.3) | copy-start | bytes 196612
  3.5 6.2 %copy-start.7 = (s32[8192]{0:T(1024)S(1)}, s32[8192]{0:T(1024)}, u32[]{:S(2)}) copy-start(s32[8192]{0:T(1024)} %param.18) | copy-start | bytes 98308
  3.5 6.2 %copy-start.9 = (f32[8,128]{1,0:T(8,128)S(1)}, f32[8,128]{1,0:T(8,128)}, u32[]{:S(2)}) copy-start(f32[8,128]{1,0:T(8,128)} %w_rad.3) | copy-start | bytes 12292
  3.6 6.2 %copy-start.10 = (f32[128]{0:T(128)S(1)}, f32[128]{0:T(128)}, u32[]{:S(2)}) copy-start(f32[128]{0:T(128)} %param.21) | copy-start | bytes 1540
  3.6 98.2 %collective-permute-start = (f32[136,1024]{1,0:T(8,128)S(1)}, f32[136,1024]{1,0:T(8,128)S(1)}, u32[]{:S(2)}, u32[]{:S(2)}) collective-permute-start(f32[136,1024]{1,0:T(8,128)S(1)} %select_maximum_fusion.1), channel_id=1, source_target_pairs={{0,1},{1,2},{2,3},{3,4},{4,5},{5,6},{6,7},{7,8},{8,9},{9,10},{10,1... | collective-permute-start | bytes 1671176 | tf_op jit(solution)/shard_map/ppermute | solution.py:708
  7.6 94.2 %collective-permute-start.1 = (f32[136,1024]{1,0:T(8,128)S(1)}, f32[136,1024]{1,0:T(8,128)}, u32[]{:S(2)}, u32[]{:S(2)}) collective-permute-start(f32[136,1024]{1,0:T(8,128)S(1)} %select_maximum_fusion), channel_id=1, source_target_pairs={{1,0},{2,1},{3,2},{4,3},{5,4},{6,5},{7,6},{8,7},{9,8},{10,9},{11,1... | collective-permute-start | bytes 1671176 | tf_op jit(solution)/shard_map/ppermute | solution.py:711
  9.8 89.9 %copy-start.13 = (s32[256]{0:T(256)S(1)}, s32[256]{0:T(256)}, u32[]{:S(2)}) copy-start(s32[256]{0:T(256)} %param.22) | copy-start | bytes 3076
  9.8 90.9 %copy-start.14 = (s32[256]{0:T(256)S(1)}, s32[256]{0:T(256)}, u32[]{:S(2)}) copy-start(s32[256]{0:T(256)} %param.23) | copy-start | bytes 3076
  9.8 91.8 %copy-start.15 = (f32[128]{0:T(128)S(1)}, f32[128]{0:T(128)}, u32[]{:S(2)}) copy-start(f32[128]{0:T(128)} %param.29) | copy-start | bytes 1540
  103.4 39.6 %copy-start.12 = (f32[3,512]{1,0:T(4,128)S(1)}, f32[3,512]{1,0:T(4,128)}, u32[]{:S(2)}) copy-start(f32[3,512]{1,0:T(4,128)} %param.25) | copy-start | bytes 18436
  103.4 39.6 %copy-start.4 = (f32[8,128]{1,0:T(8,128)S(1)}, f32[8,128]{1,0:T(8,128)}, u32[]{:S(2)}) copy-start(f32[8,128]{1,0:T(8,128)} %w_first.3) | copy-start | bytes 12292
  103.4 39.6 %copy-start.8 = (s32[512,16]{0,1:T(8,128)S(1)}, s32[512,16]{0,1:T(8,128)}, u32[]{:S(2)}) copy-start(s32[512,16]{0,1:T(8,128)} %param.26) | copy-start | bytes 98308
  136.2 40.6 %copy-start.5 = (f32[512]{0:T(512)S(1)}, f32[512]{0:T(512)}, u32[]{:S(2)}) copy-start(f32[512]{0:T(512)} %param.27) | copy-start | bytes 6148
  136.3 9.7 %collective-permute-start.3 = (f32[3,1024]{1,0:T(4,128)S(1)}, f32[3,1024]{1,0:T(4,128)S(1)}, u32[]{:S(2)}, u32[]{:S(2)}) collective-permute-start(f32[3,1024]{1,0:T(4,128)S(1)} %get-tuple-element.25), channel_id=1, source_target_pairs={{1,0},{2,1},{3,2},{4,3},{5,4},{6,5},{7,6},{8,7},{9,8},{10,9},{11,1... | collective-permute-start | bytes 36872 | tf_op jit(solution)/shard_map/ppermute | solution.py:746
  137.6 8.4 %collective-permute-start.2 = (f32[3,1024]{1,0:T(4,128)S(1)}, f32[3,1024]{1,0:T(4,128)S(1)}, u32[]{:S(2)}, u32[]{:S(2)}) collective-permute-start(f32[3,1024]{1,0:T(4,128)S(1)} %get-tuple-element.24), channel_id=1, source_target_pairs={{0,1},{1,2},{2,3},{3,4},{4,5},{5,6},{6,7},{7,8},{8,9},{9,10},{10,1... | collective-permute-start | bytes 36872 | tf_op jit(solution)/shard_map/ppermute | solution.py:747
  176.8 0.9 copy-start
  177.7 0.7 copy-start.2
  183.6 0.6 copy-start.3

commit v5 on v4

--- a/solution.py
+++ b/solution.py
@@ -69,7 +69,8 @@
     return jnp.concatenate([hi, hi, lo, jnp.zeros_like(hi)], axis=0)
 
 
-PAIR = 2 * L
+GF = 4
+GB = 4
 
 
 def forward_part(blk, held, idx_s, idx, count, pos, weights, table):
@@ -99,23 +100,24 @@
             rows[pl.ds(e, 1), :] = table[pl.ds(idx_s[0, e], 1), :]
 
     message = jnp.zeros((L, L), F32)
-    pairs = K // 2
+    pairs = K // GF
+    width = GF * L
     for p in range(pairs + 2):
         if p < pairs:
             pieces = []
-            for s in (2 * p, 2 * p + 1):
+            for s in range(GF * p, GF * p + GF):
                 pieces.append(jnp.where(sub16 == lo16[s : s + 1, :], one, zero))
                 fetch(FETCH)
             hot = jnp.concatenate(pieces, axis=1)
-            hots[:, p * PAIR : (p + 1) * PAIR] = hot
+            hots[:, p * width : (p + 1) * width] = hot
             found[p] = nn(source, hot)
             fetch(FETCH)
             yield
         if 0 <= p - 1 < pairs:
             r = p - 1
             bases = []
-            for j in range(2):
-                s = 2 * r + j
+            for j in range(GF):
+                s = GF * r + j
                 lanes = slice(j * L, (j + 1) * L)
                 mask = subw == hi[s : s + 1, :]
                 d = []
@@ -130,14 +132,14 @@
                 yield
             both = tn(jnp.concatenate(bases, axis=1).astype(BF16), weights)
             radial[r] = both[:, :L]
-            slope_w[r * PAIR : (r + 1) * PAIR, :] = both[:, L:]
+            slope_w[r * width : (r + 1) * width, :] = both[:, L:]
             fetch(FETCH)
             yield
         if 0 <= p - 2 < pairs:
             r = p - 2
-            fetch(0, (2 * r + 2) * L)
-            for j in range(2):
-                s = 2 * r + j
+            fetch(0, (r + 1) * width)
+            for j in range(GF):
+                s = GF * r + j
                 message += radial[r][j * L : (j + 1) * L] * rows[s * L : (s + 1) * L, :]
             yield
     sent[...] = message
@@ -168,11 +170,12 @@
     own_grad = [jnp.zeros((1, L), F32) for _ in range(3)]
     slopes = {}
     out = None
-    pairs = K // 2
+    pairs = K // GB
+    width = GB * L
     for p in range(pairs + 1):
         if p < pairs:
-            for j in range(2):
-                s = 2 * p + j
+            for j in range(GB):
+                s = GB * p + j
                 prod = back * rows[s * L : (s + 1) * L, :] * slope_w[s * L : (s + 1) * L, :]
                 summed = jnp.sum(prod, axis=1, keepdims=True)
                 slopes[s] = 2.0 * jnp.sum(jnp.where(diag, summed, 0.0), axis=0, keepdims=True)
@@ -180,7 +183,7 @@
         if p >= 1:
             r = p - 1
             parts = [[] for _ in range(6)]
-            for s in (2 * r, 2 * r + 1):
+            for s in range(GB * r, GB * r + GB):
                 mask = subw == hi[s : s + 1, :]
                 for c in range(3):
                     value = slopes[s] * offs[pl.ds(c * 16 + s, 1), :]
@@ -190,7 +193,7 @@
                     parts[3 + c].append(jnp.where(mask, v_lo, 0.0))
             spread = jnp.concatenate([jnp.concatenate(x, axis=1) for x in parts], axis=0).astype(BF16)
             yield
-            got = nt(spread, hots[:, r * PAIR : (r + 1) * PAIR])
+            got = nt(spread, hots[:, r * width : (r + 1) * width])
             out = got if out is None else out + got
             yield
     for c in range(3):
@@ -414,12 +417,13 @@
 CHUNK = 1024
 
 
-def mapping_kernel(force, bead, dest, start, out):
+def mapping_kernel(force, bead, dest, start, *rest):
     step = pl.program_id(0)
+    out = rest[-1]
 
     @pl.when(step == 0)
     def _():
-        out[...] = jnp.zeros_like(out)
+        out[...] = rest[0][...] if len(rest) > 1 else jnp.zeros_like(out)
 
     b = bead[...]
     hot = iota((BPB, CHUNK), 0) == b
@@ -439,17 +443,20 @@
     out[...] += got[:, :L] + got[:, L:]
 
 
-def mapping(force, bead, dest, start):
-    atoms = force.shape[1]
-    row = lambda n: pl.BlockSpec((n, CHUNK), lambda i: (0, i))
+def mapping(force, bead, dest, start, name, count, at, sums=()):
+    row = lambda n: pl.BlockSpec((n, CHUNK), lambda i: (0, at(i)))
+    flat = pl.BlockSpec((2 * L, L), lambda i: (0, 0))
     return pl.pallas_call(
         mapping_kernel,
-        grid=(atoms // CHUNK,),
-        in_specs=[row(3), row(1), row(1), row(1)],
-        out_specs=pl.BlockSpec((2 * L, L), lambda i: (0, 0)),
+        grid=(count,),
+        in_specs=[row(3), row(1), row(1), row(1)] + [flat] * len(sums),
+        out_specs=flat,
         out_shape=jax.ShapeDtypeStruct((2 * L, L), F32),
-        name="mapping",
-    )(force, bead, dest, start)
+        cost_estimate=pl.CostEstimate(
+            flops=10**9, bytes_accessed=10**6, transcendentals=0
+        ),
+        name=name,
+    )(force, bead, dest, start, *sums)
 
 
 def bead_kernel(beads_all, recv, weight, pred, offs, w_first, w_second, force, out):
@@ -745,11 +752,13 @@
     grads = acc[:, :ext_rows].reshape(3, atoms + 2 * G)
     above = lax.ppermute(grads[:, :G], AXES, down)
     below = lax.ppermute(grads[:, atoms + G :], AXES, up)
-    force = -grads[:, G : atoms + G]
-    force = force - jnp.pad(below, ((0, 0), (0, atoms - G))) - jnp.pad(above, ((0, 0), (atoms - G, 0)))
-    outgoing = mapping(
-        force, atom_bead.reshape(1, atoms), spread(dest), spread(block_start.astype(F32))
-    )
+    raw = -grads[:, G : atoms + G]
+    details = (atom_bead.reshape(1, atoms), spread(dest), spread(block_start.astype(F32)))
+    last = atoms // CHUNK - 1
+    partial = mapping(raw, *details, "mapping_inner", last - 1, lambda i: i + 1)
+    above, below, partial = lax.optimization_barrier((above, below, partial))
+    force = raw - jnp.pad(below, ((0, 0), (0, atoms - G))) - jnp.pad(above, ((0, 0), (atoms - G, 0)))
+    outgoing = mapping(force, *details, "mapping_border", 2, lambda i: i * last, (partial,))
     recv = exchange(outgoing)
     bead_force, sums = bead_stage(
         recv, bead_weight.reshape(1, beads), pred, offs, w_first, second, beads * devices

time: 203 us -> 196 us (0.966)
  Pallas kernels: 175 us -> 169 us
    pallas_call x2, Pallas kernels: 123 us -> 116 us  [teacher_call(): pl.pallas_call(functools.partial(teacher_kernel, len(feats), place, sums...]
    pallas_call x1 -> x2, Pallas kernels: 5.34 us -> 6.61 us  [mapping(): pl.pallas_call(mapping_kernel, grid=(count,), in_specs=[row(3), row(1), r...]
  transfers between devices with their start and end apart: 4 -> 4, of which waited for: 0 -> 0; matrix products, arithmetic and copies ran while one was open for 1% -> 2% of each run, Pallas kernels for 46% -> 47%
where the time goes in v5:
time: 196 us; the launch traced here: 195 us
  Pallas kernels  169 us (86%)
  starting transfers between devices  11.9 us (6%)
  local copies, waits for them, and re-layouts  9.79 us (5%)
  other arithmetic  3.79 us (2%)
    pallas_call x2, Pallas kernels, teacher_call(): pl.pallas_call(functools.partial(teacher_kernel, len(feats), place, sums...  116 us
    pallas_call x1, Pallas kernels, exchange(): pl.pallas_call(exchange_kernel, in_specs=[vmem], out_specs=vmem, out_shap...  23.7 us
    pallas_call x1, Pallas kernels, reduce_all(): pl.pallas_call(reduce_kernel, in_specs=[vmem], out_specs=vmem, out_shape=...  14.1 us
    pallas_call x2, Pallas kernels, mapping(): pl.pallas_call(mapping_kernel, grid=(count,), in_specs=[row(3), row(1), r...  6.61 us
    ppermute x1, starting transfers between devices, local(): below = lax.ppermute(grads[:, atoms + G:], AXES, up)  5.34 us
    pallas_call x1, Pallas kernels, bead_stage(): pl.pallas_call(functools.partial(bead_kernel, beads_all), grid=(beads //...  5.19 us
    ppermute x1, starting transfers between devices, local(): lax.ppermute(payload(features[:, atoms - G:], positions[:, atoms - G:], b...  3.94 us
  transfers between devices with their start and end apart: 4, of which 0 were waited for; matrix products, arithmetic and copies ran while one was open for 2% of the time, Pallas kernels for 47%

profile of v5, /device:TPU:0, one launch (start us, length us, event | category | flops | bytes accessed | tf_op | source)
XLA Modules:
  0.0 195.4 jit_solution(4408391347880032319)
XLA Ops:
  0.7 0.8 fusion.7
  1.5 0.7 fusion.6
  2.2 1.3 fusion.4
  3.6 3.9 %collective-permute-start = (f32[136,1024]{1,0:T(8,128)S(1)}, f32[136,1024]{1,0:T(8,128)S(1)}, u32[]{:S(2)}, u32[]{:S(2)}) collective-permute-start(f32[136,1024]{1,0:T(8,128)S(1)} %select_maximum_fusion.1), channel_id=1, source_target_pairs={{0,1},{1,2},{2,3},{3,4},{4,5},{5,6},{6,7},{7,8},{8,9},{9,10},{10,1... | collective-permute-start | bytes 1671176 | tf_op jit(solution)/shard_map/ppermute | solution.py:715
  7.6 1.3 collective-permute-start.1
  9.9 85.1 %interior.1.rest_4_ = f32[3,104,128]{2,1,0:T(8,128)S(1)} custom-call(s32[48,1,1536]{2,1,0:T(1,128)S(1)} %sub.44.idx_h, s32[12,8192]{1,0:T(8,128)S(1)} %bitcast.34, s32[1,8192]{1,0:T(1,128)S(1)} %bitcast.37, f32[6,104,128]{2,1,0:T(8,128)S(1)} %pad_maximum_fusion.pos, f32[8,128]{1,0:T(8,128)S(1)} %copy-done.9, f32[128,128]{1,0:T(8,128)S(1)} %copy-done.6, ...), custom_call_target="tpu_custom_call" | custom-call | flops 49999998976 | bytes 67108864 | tf_op jit(solution)/shard_map/interior/pallas_call | solution.py:308
  95.2 0.7 reshape.93.dest
  96.1 0.7 reshape.94.start
  97.1 0.8 slice.76
  98.0 31.3 %border.1 = f32[3,104,128]{2,1,0:T(8,128)S(1)} custom-call(s32[16,1,1536]{2,1,0:T(1,128)S(1)} %pad_add_fusion.idx_h, s32[12,8192]{1,0:T(8,128)S(1)} %bitcast.35, s32[1,8192]{1,0:T(1,128)S(1)} %bitcast.38, f32[6,104,128]{2,1,0:T(8,128)S(1)} %pad_maximum_fusion.1.pos, f32[8,128]{1,0:T(8,128)S(1)} %copy-done.9, f32[128,128]{1,0:T(8,128)S(1)} %copy-done.6, ...), custom_call_target="tpu_custom_call" | custom-call | flops 49999998976 | bytes 67108864 | tf_op jit(solution)/shard_map/border/pallas_call | solution.py:308
  129.4 0.7 slice_negate_fusion.force
  130.0 0.7 slice.82
  130.7 1.3 collective-permute-start.2
  132.0 5.3 %collective-permute-start.3 = (f32[3,1024]{1,0:T(4,128)S(1)}, f32[3,1024]{1,0:T(4,128)S(1)}, u32[]{:S(2)}, u32[]{:S(2)}) collective-permute-start(f32[3,1024]{1,0:T(4,128)S(1)} %get-tuple-element.30), channel_id=1, source_target_pairs={{0,1},{1,2},{2,3},{3,4},{4,5},{5,6},{6,7},{7,8},{8,9},{9,10},{10,1... | collective-permute-start | bytes 36872 | tf_op jit(solution)/shard_map/ppermute | solution.py:754
  137.5 4.3 %mapping_inner.1.rest_0_ = f32[256,128]{1,0:T(8,128)} custom-call(f32[3,8192]{1,0:T(4,128)} %slice_negate_fusion.force, s32[1,8192]{1,0:T(1,128)} %bitcast.49, s32[1,8192]{1,0:T(1,128)} %reshape.93.dest, f32[1,8192]{1,0:T(1,128)} %reshape.94.start), custom_call_target="tpu_custom_call" | custom-call | flops 1000000000 | bytes 1000000 | tf_op jit(solution)/shard_map/mapping_inner/pallas_call | solution.py:449
  141.8 2.9 %student.1 = (f32[3,512]{1,0:T(4,128)}, f32[3,16,512]{2,1,0:T(8,128)S(1)}) custom-call(s32[16,512]{1,0:T(8,128)S(1)} %bitcast.39, f32[3,5,128]{2,1,0:T(8,128)S(1)} %reshape.96.pos, f32[8,128]{1,0:T(8,128)S(1)} %copy-done.4, f32[128,1]{1,0:T(8,128)S(1)} %copy.36.w_second), custom_call_target="tpu_custom_call" | custom-call | flops 1000000000 | bytes 1000000 | tf_op jit(solution)/shard_map/student/pallas_call | solution.py:392
  144.7 0.7 pad_subtract_fusion.2.force
  145.4 2.3 %mapping_border.1.src = f32[256,128]{1,0:T(8,128)} custom-call(f32[3,8192]{1,0:T(4,128)} %pad_subtract_fusion.2.force, s32[1,8192]{1,0:T(1,128)} %bitcast.50, s32[1,8192]{1,0:T(1,128)} %reshape.93.dest, f32[1,8192]{1,0:T(1,128)} %reshape.94.start, f32[256,128]{1,0:T(8,128)} %mapping_inner.1.rest_0_), custom_call_target="tpu_custom_call" | custom-call | flops 1000000000 | bytes 1000000 | tf_op jit(solution)/shard_map/mapping_border/pallas_call | solution.py:449
  147.7 23.7 %exchange.1.recv = f32[256,128]{1,0:T(8,128)} custom-call(f32[256,128]{1,0:T(8,128)} %mapping_border.1.src), custom_call_target="tpu_custom_call" | custom-call | tf_op jit(solution)/shard_map/exchange/pallas_call | solution.py:607
  171.5 0.9 copy-done
  172.4 5.2 %beads.1 = (f32[3,512]{1,0:T(4,128)}, f32[16,128]{1,0:T(8,128)S(1)}) custom-call(f32[256,128]{1,0:T(8,128)S(1)} %copy-done, f32[1,512]{1,0:T(1,128)S(1)} %bitcast.36, f32[3,512]{1,0:T(4,128)S(1)} %copy-done.2, f32[3,16,512]{2,1,0:T(8,128)S(1)} %get-tuple-element.23.offs, f32[8,128]{1,0:T(8,128)S(1)} %copy-done.4, f32[128,1]{1,0:T(8,128)S(1)} %copy.36.w_second), custom_call_target="tpu_custom_call" | custom-call | tf_op jit(solution)/shard_map/beads/pallas_call | solution.py:512
  178.2 14.1 %reduce.2 = f32[16,128]{1,0:T(8,128)} custom-call(f32[16,128]{1,0:T(8,128)} %copy-done.3), custom_call_target="tpu_custom_call" | custom-call | tf_op jit(solution)/shard_map/reduce/pallas_call | solution.py:675
  192.3 1.3 slice.83
  193.6 1.9 slice_reduce_fusion
  (69 shorter events, 2.4 us)
Async XLA Ops:
  0.6 8.5 %copy-start.11 = (f32[3,8192]{1,0:T(4,128)S(1)}, f32[3,8192]{1,0:T(4,128)}, u32[]{:S(2)}) copy-start(f32[3,8192]{1,0:T(4,128)} %param.15) | copy-start | bytes 294916
  0.6 8.3 %copy-start.1 = (s32[8192,12]{0,1:T(8,128)S(1)}, s32[8192,12]{0,1:T(8,128)}, u32[]{:S(2)}) copy-start(s32[8192,12]{0,1:T(8,128)} %param.17) | copy-start | bytes 1179652
  3.5 6.3 %copy-start.6 = (f32[128,128]{1,0:T(8,128)S(1)}, f32[128,128]{1,0:T(8,128)}, u32[]{:S(2)}) copy-start(f32[128,128]{1,0:T(8,128)} %w_mix.3) | copy-start | bytes 196612
  3.5 6.2 %copy-start.7 = (s32[8192]{0:T(1024)S(1)}, s32[8192]{0:T(1024)}, u32[]{:S(2)}) copy-start(s32[8192]{0:T(1024)} %param.18) | copy-start | bytes 98308
  3.5 6.2 %copy-start.9 = (f32[8,128]{1,0:T(8,128)S(1)}, f32[8,128]{1,0:T(8,128)}, u32[]{:S(2)}) copy-start(f32[8,128]{1,0:T(8,128)} %w_rad.3) | copy-start | bytes 12292
  3.6 6.2 %copy-start.10 = (f32[128]{0:T(128)S(1)}, f32[128]{0:T(128)}, u32[]{:S(2)}) copy-start(f32[128]{0:T(128)} %param.21) | copy-start | bytes 1540
  3.6 93.4 %collective-permute-start = (f32[136,1024]{1,0:T(8,128)S(1)}, f32[136,1024]{1,0:T(8,128)S(1)}, u32[]{:S(2)}, u32[]{:S(2)}) collective-permute-start(f32[136,1024]{1,0:T(8,128)S(1)} %select_maximum_fusion.1), channel_id=1, source_target_pairs={{0,1},{1,2},{2,3},{3,4},{4,5},{5,6},{6,7},{7,8},{8,9},{9,10},{10,1... | collective-permute-start | bytes 1671176 | tf_op jit(solution)/shard_map/ppermute | solution.py:715
  7.6 89.4 %collective-permute-start.1 = (f32[136,1024]{1,0:T(8,128)S(1)}, f32[136,1024]{1,0:T(8,128)}, u32[]{:S(2)}, u32[]{:S(2)}) collective-permute-start(f32[136,1024]{1,0:T(8,128)S(1)} %select_maximum_fusion), channel_id=1, source_target_pairs={{1,0},{2,1},{3,2},{4,3},{5,4},{6,5},{7,6},{8,7},{9,8},{10,9},{11,1... | collective-permute-start | bytes 1671176 | tf_op jit(solution)/shard_map/ppermute | solution.py:718
  9.8 85.1 %copy-start.13 = (s32[256]{0:T(256)S(1)}, s32[256]{0:T(256)}, u32[]{:S(2)}) copy-start(s32[256]{0:T(256)} %param.22) | copy-start | bytes 3076
  9.8 86.2 %copy-start.14 = (s32[256]{0:T(256)S(1)}, s32[256]{0:T(256)}, u32[]{:S(2)}) copy-start(s32[256]{0:T(256)} %param.23) | copy-start | bytes 3076
  9.8 87.0 %copy-start.15 = (f32[128]{0:T(128)S(1)}, f32[128]{0:T(128)}, u32[]{:S(2)}) copy-start(f32[128]{0:T(128)} %param.29) | copy-start | bytes 1540
  97.9 39.4 %copy-start.12 = (f32[3,512]{1,0:T(4,128)S(1)}, f32[3,512]{1,0:T(4,128)}, u32[]{:S(2)}) copy-start(f32[3,512]{1,0:T(4,128)} %param.25) | copy-start | bytes 18436
  129.2 12.5 %copy-start.4 = (f32[8,128]{1,0:T(8,128)S(1)}, f32[8,128]{1,0:T(8,128)}, u32[]{:S(2)}) copy-start(f32[8,128]{1,0:T(8,128)} %w_first.3) | copy-start | bytes 12292
  129.2 12.5 %copy-start.8 = (s32[512,16]{0,1:T(8,128)S(1)}, s32[512,16]{0,1:T(8,128)}, u32[]{:S(2)}) copy-start(s32[512,16]{0,1:T(8,128)} %param.26) | copy-start | bytes 98308
  130.7 14.0 %collective-permute-start.2 = (f32[3,1024]{1,0:T(4,128)S(1)}, f32[3,1024]{1,0:T(4,128)S(1)}, u32[]{:S(2)}, u32[]{:S(2)}) collective-permute-start(f32[3,1024]{1,0:T(4,128)S(1)} %get-tuple-element.31), channel_id=1, source_target_pairs={{1,0},{2,1},{3,2},{4,3},{5,4},{6,5},{7,6},{8,7},{9,8},{10,9},{11,1... | collective-permute-start | bytes 36872 | tf_op jit(solution)/shard_map/ppermute | solution.py:753
  132.0 12.7 %collective-permute-start.3 = (f32[3,1024]{1,0:T(4,128)S(1)}, f32[3,1024]{1,0:T(4,128)S(1)}, u32[]{:S(2)}, u32[]{:S(2)}) collective-permute-start(f32[3,1024]{1,0:T(4,128)S(1)} %get-tuple-element.30), channel_id=1, source_target_pairs={{0,1},{1,2},{2,3},{3,4},{4,5},{5,6},{6,7},{7,8},{8,9},{9,10},{10,1... | collective-permute-start | bytes 36872 | tf_op jit(solution)/shard_map/ppermute | solution.py:754
  141.8 29.7 %copy-start.5 = (f32[512]{0:T(512)S(1)}, f32[512]{0:T(512)}, u32[]{:S(2)}) copy-start(f32[512]{0:T(512)} %param.27) | copy-start | bytes 6148
  144.7 26.8 %copy-start.2 = (f32[3,512]{1,0:T(4,128)S(1)}, f32[3,512]{1,0:T(4,128)}, u32[]{:S(2)}) copy-start(f32[3,512]{1,0:T(4,128)} %get-tuple-element.12.pred) | copy-start | bytes 18436
  171.4 0.9 copy-start
  177.5 0.6 copy-start.3

commit v6 on v5

--- a/solution.py
+++ b/solution.py
@@ -621,7 +621,7 @@
     )(rows)
 
 
-def reduce_kernel(x, out, first, second, send_sem, recv_sem):
+def reduce_kernel(x, grad_one, grad_two, loss, first, second, send_sem, recv_sem):
     g = lax.axis_index("grp")
     b = lax.axis_index("brick")
     near = first.shape[0]
@@ -665,7 +665,9 @@
         value = slots[0]
         for i in range(1, size):
             value = value + slots[i]
-    out[...] = value
+    grad_one[...] = value[:8]
+    grad_two[...] = value[8:9]
+    loss[...] = jnp.sum(value[9:10], axis=1, keepdims=True)
 
 
 def reduce_all(x):
@@ -675,8 +677,8 @@
     return pl.pallas_call(
         reduce_kernel,
         in_specs=[vmem],
-        out_specs=vmem,
-        out_shape=jax.ShapeDtypeStruct(x.shape, F32),
+        out_specs=[vmem] * 3,
+        out_shape=[jax.ShapeDtypeStruct(s, F32) for s in ((8, L), (1, L), (1, 1))],
         scratch_shapes=[pltpu.VMEM((n,) + x.shape, F32) for n in (near, far)]
         + [pltpu.SemaphoreType.DMA((near + far - 2,)), pltpu.SemaphoreType.DMA((near + far - 2,))],
         compiler_params=pltpu.CompilerParams(collective_id=2, has_side_effects=True),
@@ -763,8 +765,8 @@
     bead_force, sums = bead_stage(
         recv, bead_weight.reshape(1, beads), pred, offs, w_first, second, beads * devices
     )
-    sums = reduce_all(sums)
-    return force, bead_force, pred, sums[:8], sums[8], jnp.sum(sums[9])
+    grad_one, grad_two, loss = reduce_all(sums)
+    return force, bead_force, pred, grad_one, grad_two.reshape(L), loss.reshape(())
 
 
 def solution(mesh):

time: 196 us -> 197 us (level)
    unnamed x38 -> x40, local copies, waits for them, and re-layouts: 1.82 us -> 4.22 us
  transfers between devices with their start and end apart: 4 -> 4, of which waited for: 0 -> 0; matrix products, arithmetic and copies ran while one was open for 2% -> 1% of each run, Pallas kernels for 47% -> 47%
where the time goes in v6:
time: 197 us; the launch traced here: 196 us
  Pallas kernels  169 us (86%)
  starting transfers between devices  11.8 us (6%)
  local copies, waits for them, and re-layouts  10.9 us (6%)
  between operations  2.84 us (1%)
    pallas_call x2, Pallas kernels, teacher_call(): pl.pallas_call(functools.partial(teacher_kernel, len(feats), place, sums...  116 us
    pallas_call x1, Pallas kernels, exchange(): pl.pallas_call(exchange_kernel, in_specs=[vmem], out_specs=vmem, out_shap...  23.8 us
    pallas_call x1, Pallas kernels, reduce_all(): pl.pallas_call(reduce_kernel, in_specs=[vmem], out_specs=[vmem] * 3, out_...  14.1 us
    pallas_call x2, Pallas kernels, mapping(): pl.pallas_call(mapping_kernel, grid=(count,), in_specs=[row(3), row(1), r...  6.61 us
    ppermute x1, starting transfers between devices, local(): below = lax.ppermute(grads[:, atoms + G:], AXES, up)  5.3 us
    pallas_call x1, Pallas kernels, bead_stage(): pl.pallas_call(functools.partial(bead_kernel, beads_all), grid=(beads //...  5.19 us
    unnamed x40, local copies, waits for them, and re-layouts  4.22 us
  transfers between devices with their start and end apart: 4, of which 0 were waited for; matrix products, arithmetic and copies ran while one was open for 1% of the time, Pallas kernels for 47%

profile of v6, /device:TPU:0, one launch (start us, length us, event | category | flops | bytes accessed | tf_op | source)
XLA Modules:
  0.0 196.4 jit_solution(11700224503801069018)
XLA Ops:
  0.7 0.8 fusion.7
  1.5 0.7 fusion.6
  2.2 1.3 fusion.4
  3.6 3.9 %collective-permute-start = (f32[136,1024]{1,0:T(8,128)S(1)}, f32[136,1024]{1,0:T(8,128)S(1)}, u32[]{:S(2)}, u32[]{:S(2)}) collective-permute-start(f32[136,1024]{1,0:T(8,128)S(1)} %select_maximum_fusion.1), channel_id=1, source_target_pairs={{0,1},{1,2},{2,3},{3,4},{4,5},{5,6},{6,7},{7,8},{8,9},{9,10},{10,1... | collective-permute-start | bytes 1671176 | tf_op jit(solution)/shard_map/ppermute | solution.py:717
  7.6 1.3 collective-permute-start.1
  9.9 85.1 %interior.1.rest_4_ = f32[3,104,128]{2,1,0:T(8,128)S(1)} custom-call(s32[48,1,1536]{2,1,0:T(1,128)S(1)} %sub.44.idx_h, s32[12,8192]{1,0:T(8,128)S(1)} %bitcast.34, s32[1,8192]{1,0:T(1,128)S(1)} %bitcast.37, f32[6,104,128]{2,1,0:T(8,128)S(1)} %pad_maximum_fusion.pos, f32[8,128]{1,0:T(8,128)S(1)} %copy-done.9, f32[128,128]{1,0:T(8,128)S(1)} %copy-done.6, ...), custom_call_target="tpu_custom_call" | custom-call | flops 49999998976 | bytes 67108864 | tf_op jit(solution)/shard_map/interior/pallas_call | solution.py:308
  95.3 0.7 reshape.99.dest
  96.1 0.7 reshape.100.start
  97.0 0.8 slice.67
  97.9 31.3 %border.1 = f32[3,104,128]{2,1,0:T(8,128)S(1)} custom-call(s32[16,1,1536]{2,1,0:T(1,128)S(1)} %pad_add_fusion.idx_h, s32[12,8192]{1,0:T(8,128)S(1)} %bitcast.35, s32[1,8192]{1,0:T(1,128)S(1)} %bitcast.38, f32[6,104,128]{2,1,0:T(8,128)S(1)} %pad_maximum_fusion.1.pos, f32[8,128]{1,0:T(8,128)S(1)} %copy-done.9, f32[128,128]{1,0:T(8,128)S(1)} %copy-done.6, ...), custom_call_target="tpu_custom_call" | custom-call | flops 49999998976 | bytes 67108864 | tf_op jit(solution)/shard_map/border/pallas_call | solution.py:308
  129.3 0.7 slice_negate_fusion.force
  130.0 0.7 slice.73
  130.7 1.3 collective-permute-start.2
  132.0 5.3 %collective-permute-start.3 = (f32[3,1024]{1,0:T(4,128)S(1)}, f32[3,1024]{1,0:T(4,128)S(1)}, u32[]{:S(2)}, u32[]{:S(2)}) collective-permute-start(f32[3,1024]{1,0:T(4,128)S(1)} %get-tuple-element.36), channel_id=1, source_target_pairs={{0,1},{1,2},{2,3},{3,4},{4,5},{5,6},{6,7},{7,8},{8,9},{9,10},{10,1... | collective-permute-start | bytes 36872 | tf_op jit(solution)/shard_map/ppermute | solution.py:756
  137.4 4.3 %mapping_inner.1.rest_0_ = f32[256,128]{1,0:T(8,128)} custom-call(f32[3,8192]{1,0:T(4,128)} %slice_negate_fusion.force, s32[1,8192]{1,0:T(1,128)} %bitcast.49, s32[1,8192]{1,0:T(1,128)} %reshape.99.dest, f32[1,8192]{1,0:T(1,128)} %reshape.100.start), custom_call_target="tpu_custom_call" | custom-call | flops 1000000000 | bytes 1000000 | tf_op jit(solution)/shard_map/mapping_inner/pallas_call | solution.py:449
  141.7 2.9 %student.1 = (f32[3,512]{1,0:T(4,128)}, f32[3,16,512]{2,1,0:T(8,128)S(1)}) custom-call(s32[16,512]{1,0:T(8,128)S(1)} %bitcast.39, f32[3,5,128]{2,1,0:T(8,128)S(1)} %reshape.102.pos, f32[8,128]{1,0:T(8,128)S(1)} %copy-done.4, f32[128,1]{1,0:T(8,128)S(1)} %copy.36.w_second), custom_call_target="tpu_custom_call" | custom-call | flops 1000000000 | bytes 1000000 | tf_op jit(solution)/shard_map/student/pallas_call | solution.py:392
  144.6 0.7 pad_subtract_fusion.2.force
  145.3 2.3 %mapping_border.1.src = f32[256,128]{1,0:T(8,128)} custom-call(f32[3,8192]{1,0:T(4,128)} %pad_subtract_fusion.2.force, s32[1,8192]{1,0:T(1,128)} %bitcast.50, s32[1,8192]{1,0:T(1,128)} %reshape.99.dest, f32[1,8192]{1,0:T(1,128)} %reshape.100.start, f32[256,128]{1,0:T(8,128)} %mapping_inner.1.rest_0_), custom_call_target="tpu_custom_call" | custom-call | flops 1000000000 | bytes 1000000 | tf_op jit(solution)/shard_map/mapping_border/pallas_call | solution.py:449
  147.6 23.8 %exchange.1.recv = f32[256,128]{1,0:T(8,128)} custom-call(f32[256,128]{1,0:T(8,128)} %mapping_border.1.src), custom_call_target="tpu_custom_call" | custom-call | tf_op jit(solution)/shard_map/exchange/pallas_call | solution.py:607
  171.4 0.9 copy-done
  172.3 5.2 %beads.1 = (f32[3,512]{1,0:T(4,128)}, f32[16,128]{1,0:T(8,128)S(1)}) custom-call(f32[256,128]{1,0:T(8,128)S(1)} %copy-done, f32[1,512]{1,0:T(1,128)S(1)} %bitcast.36, f32[3,512]{1,0:T(4,128)S(1)} %copy-done.2, f32[3,16,512]{2,1,0:T(8,128)S(1)} %get-tuple-element.26.offs, f32[8,128]{1,0:T(8,128)S(1)} %copy-done.4, f32[128,1]{1,0:T(8,128)S(1)} %copy.36.w_second), custom_call_target="tpu_custom_call" | custom-call | tf_op jit(solution)/shard_map/beads/pallas_call | solution.py:512
  178.1 14.1 %reduce.1 = (f32[8,128]{1,0:T(8,128)}, f32[1,128]{1,0:T(1,128)}, f32[1,1]{1,0:T(1,128)}) custom-call(f32[16,128]{1,0:T(8,128)} %copy-done.3), custom_call_target="tpu_custom_call" | custom-call | tf_op jit(solution)/shard_map/reduce/pallas_call | solution.py:677
  192.2 1.3 copy.51
  193.5 1.1 copy.52
  (69 shorter events, 2.4 us)
Async XLA Ops:
  0.6 8.5 %copy-start.11 = (f32[3,8192]{1,0:T(4,128)S(1)}, f32[3,8192]{1,0:T(4,128)}, u32[]{:S(2)}) copy-start(f32[3,8192]{1,0:T(4,128)} %param.15) | copy-start | bytes 294916
  0.6 8.3 %copy-start.1 = (s32[8192,12]{0,1:T(8,128)S(1)}, s32[8192,12]{0,1:T(8,128)}, u32[]{:S(2)}) copy-start(s32[8192,12]{0,1:T(8,128)} %param.17) | copy-start | bytes 1179652
  3.5 6.3 %copy-start.6 = (f32[128,128]{1,0:T(8,128)S(1)}, f32[128,128]{1,0:T(8,128)}, u32[]{:S(2)}) copy-start(f32[128,128]{1,0:T(8,128)} %w_mix.3) | copy-start | bytes 196612
  3.5 6.2 %copy-start.7 = (s32[8192]{0:T(1024)S(1)}, s32[8192]{0:T(1024)}, u32[]{:S(2)}) copy-start(s32[8192]{0:T(1024)} %param.18) | copy-start | bytes 98308
  3.5 6.2 %copy-start.9 = (f32[8,128]{1,0:T(8,128)S(1)}, f32[8,128]{1,0:T(8,128)}, u32[]{:S(2)}) copy-start(f32[8,128]{1,0:T(8,128)} %w_rad.3) | copy-start | bytes 12292
  3.6 6.2 %copy-start.10 = (f32[128]{0:T(128)S(1)}, f32[128]{0:T(128)}, u32[]{:S(2)}) copy-start(f32[128]{0:T(128)} %param.21) | copy-start | bytes 1540
  3.6 93.4 %collective-permute-start = (f32[136,1024]{1,0:T(8,128)S(1)}, f32[136,1024]{1,0:T(8,128)S(1)}, u32[]{:S(2)}, u32[]{:S(2)}) collective-permute-start(f32[136,1024]{1,0:T(8,128)S(1)} %select_maximum_fusion.1), channel_id=1, source_target_pairs={{0,1},{1,2},{2,3},{3,4},{4,5},{5,6},{6,7},{7,8},{8,9},{9,10},{10,1... | collective-permute-start | bytes 1671176 | tf_op jit(solution)/shard_map/ppermute | solution.py:717
  7.6 89.4 %collective-permute-start.1 = (f32[136,1024]{1,0:T(8,128)S(1)}, f32[136,1024]{1,0:T(8,128)}, u32[]{:S(2)}, u32[]{:S(2)}) collective-permute-start(f32[136,1024]{1,0:T(8,128)S(1)} %select_maximum_fusion), channel_id=1, source_target_pairs={{1,0},{2,1},{3,2},{4,3},{5,4},{6,5},{7,6},{8,7},{9,8},{10,9},{11,1... | collective-permute-start | bytes 1671176 | tf_op jit(solution)/shard_map/ppermute | solution.py:720
  9.8 85.1 %copy-start.13 = (s32[256]{0:T(256)S(1)}, s32[256]{0:T(256)}, u32[]{:S(2)}) copy-start(s32[256]{0:T(256)} %param.22) | copy-start | bytes 3076
  9.8 86.2 %copy-start.14 = (s32[256]{0:T(256)S(1)}, s32[256]{0:T(256)}, u32[]{:S(2)}) copy-start(s32[256]{0:T(256)} %param.23) | copy-start | bytes 3076
  9.8 87.0 %copy-start.15 = (f32[128]{0:T(128)S(1)}, f32[128]{0:T(128)}, u32[]{:S(2)}) copy-start(f32[128]{0:T(128)} %param.29) | copy-start | bytes 1540
  97.9 39.4 %copy-start.12 = (f32[3,512]{1,0:T(4,128)S(1)}, f32[3,512]{1,0:T(4,128)}, u32[]{:S(2)}) copy-start(f32[3,512]{1,0:T(4,128)} %param.25) | copy-start | bytes 18436
  129.2 12.5 %copy-start.4 = (f32[8,128]{1,0:T(8,128)S(1)}, f32[8,128]{1,0:T(8,128)}, u32[]{:S(2)}) copy-start(f32[8,128]{1,0:T(8,128)} %w_first.3) | copy-start | bytes 12292
  129.2 12.5 %copy-start.8 = (s32[512,16]{0,1:T(8,128)S(1)}, s32[512,16]{0,1:T(8,128)}, u32[]{:S(2)}) copy-start(s32[512,16]{0,1:T(8,128)} %param.26) | copy-start | bytes 98308
  130.7 13.9 %collective-permute-start.2 = (f32[3,1024]{1,0:T(4,128)S(1)}, f32[3,1024]{1,0:T(4,128)S(1)}, u32[]{:S(2)}, u32[]{:S(2)}) collective-permute-start(f32[3,1024]{1,0:T(4,128)S(1)} %get-tuple-element.37), channel_id=1, source_target_pairs={{1,0},{2,1},{3,2},{4,3},{5,4},{6,5},{7,6},{8,7},{9,8},{10,9},{11,1... | collective-permute-start | bytes 36872 | tf_op jit(solution)/shard_map/ppermute | solution.py:755
  132.0 12.6 %collective-permute-start.3 = (f32[3,1024]{1,0:T(4,128)S(1)}, f32[3,1024]{1,0:T(4,128)S(1)}, u32[]{:S(2)}, u32[]{:S(2)}) collective-permute-start(f32[3,1024]{1,0:T(4,128)S(1)} %get-tuple-element.36), channel_id=1, source_target_pairs={{0,1},{1,2},{2,3},{3,4},{4,5},{5,6},{6,7},{7,8},{8,9},{9,10},{10,1... | collective-permute-start | bytes 36872 | tf_op jit(solution)/shard_map/ppermute | solution.py:756
  141.7 29.7 %copy-start.5 = (f32[512]{0:T(512)S(1)}, f32[512]{0:T(512)}, u32[]{:S(2)}) copy-start(f32[512]{0:T(512)} %param.27) | copy-start | bytes 6148
  144.6 26.8 %copy-start.2 = (f32[3,512]{1,0:T(4,128)S(1)}, f32[3,512]{1,0:T(4,128)}, u32[]{:S(2)}) copy-start(f32[3,512]{1,0:T(4,128)} %get-tuple-element.54.pred) | copy-start | bytes 18436
  171.4 0.9 copy-start
  177.5 0.6 copy-start.3
